TPU v7x, 256 devices: a whole 4x4x8 slice. The times are simulated.
256 devices in a mesh: blk: 16 (over y_hi, x, core), dp: 16 (over z, y_lo).
Axes of the slice: x: 4, y: 4 (y_hi: 2, y_lo: 2; y = y_hi * 2 + y_lo), z: 8, core: 2. Of those that a mesh axis runs over, the one named last changes fastest.
Arguments:
- images: bfloat16 [65536, 1152], P(('blk', 'dp')), may hold values from -24 to 24
- texts: bfloat16 [65536, 1152], P(('blk', 'dp')), may hold values from -6 to 6
- head: bfloat16 [1152, 1152], replicated, may hold values from -0.1875 to 0.1875
- scale: float32 [1], replicated, may hold values from 4 to 12
- bias: float32 [1], replicated, may hold values from -3 to -1
Outputs:
- grad_image: float32 [65536, 1152], P(('blk', 'dp'))
- grad_text: float32 [65536, 1152], P(('blk', 'dp'))
- head_grad: float32 [1152, 1152], P('dp')
All inputs are finite; a program needn't handle non-finite values.
Results may differ from a plain program's by a relative error of at most 0.012.
Values may be sent and summed in bfloat16 or wider, within the bound.
No kernel may reach another device: no remote copies, remote signals or barrier semaphores. Data moves between devices by JAX's collectives and lax.ppermute only.
A program may use at most 64 MiB of HBM per device.

v0:
```python
import jax
import jax.numpy as jnp
from jax import lax
from jax.sharding import PartitionSpec as P

STEPS = 4


def passed_along(value, axis, steps):
    count = lax.axis_size(axis)
    pairs = [(source, (source + steps) % count) for source in range(count)]
    return lax.ppermute(value, axis, pairs)


def on_device(images, texts, head, scale, bias):
    scl = scale[0]
    bia = bias[0]
    proj = jnp.dot(images, head, preferred_element_type=jnp.float32)
    pnorm = jnp.sqrt(jnp.sum(proj * proj, -1, keepdims=True) + 1e-06)
    unit_img = proj / pnorm
    tfloat = texts.astype(jnp.float32)
    tnorm = jnp.sqrt(jnp.sum(tfloat * tfloat, -1, keepdims=True) + 1e-06)
    unit_txt = tfloat / tnorm
    img_b = unit_img.astype(jnp.bfloat16)
    txt_b = unit_txt.astype(jnp.bfloat16)
    count = images.shape[0]
    eye = lax.broadcasted_iota(jnp.int32, (count, count), 0) == lax.broadcasted_iota(
        jnp.int32, (count, count), 1
    )
    label_home = jnp.where(eye, 1.0, -1.0).astype(jnp.float32)
    label_away = -jnp.ones((count, count), jnp.float32)
    block = txt_b
    dimg = jnp.zeros(unit_img.shape, jnp.float32)
    carried = jnp.zeros(unit_txt.shape, jnp.float32)
    for step in range(STEPS + 1):
        label = label_home if step == 0 else label_away
        logit = scl * jnp.dot(img_b, block.T, preferred_element_type=jnp.float32) + bia
        grad_b = (-label * jax.nn.sigmoid(-label * logit)).astype(jnp.bfloat16)
        dimg = dimg + scl * jnp.dot(grad_b, block, preferred_element_type=jnp.float32)
        txt_term = scl * jnp.einsum("ij,ik->jk", grad_b, img_b, preferred_element_type=jnp.float32)
        carried = carried + txt_term
        if step < STEPS:
            carried = passed_along(carried, "blk", 1)
        if step < STEPS:
            block = passed_along(block, "blk", 1)
    dtxt = passed_along(carried.astype(jnp.bfloat16), "blk", -STEPS).astype(carried.dtype)
    grad_text = (dtxt - unit_txt * jnp.sum(unit_txt * dtxt, -1, keepdims=True)) / tnorm
    dproj_b = ((dimg - unit_img * jnp.sum(unit_img * dimg, -1, keepdims=True)) / pnorm).astype(
        jnp.bfloat16
    )
    grad_image = jnp.einsum("ie,de->id", dproj_b, head, preferred_element_type=jnp.float32)
    total_pairs = count * lax.axis_size("blk") * lax.axis_size("dp")
    norm_factor = 1.0 / jnp.sqrt(jnp.float32(total_pairs))
    width = images.shape[1]
    own_rows = width // lax.axis_size("dp")
    whole = lax.psum(
        jnp.einsum("id,ie->de", images, dproj_b, preferred_element_type=jnp.float32), ("blk", "dp")
    )
    mine = lax.dynamic_slice_in_dim(whole, lax.axis_index("dp") * own_rows, own_rows, 0)
    head_grad = mine * norm_factor
    return (grad_image, grad_text, head_grad)


def solution(mesh):
    placed = (P(("blk", "dp"), None), P(("blk", "dp"), None), P(), P(), P())
    return jax.shard_map(
        on_device,
        mesh=mesh,
        in_specs=placed,
        out_specs=(P(("blk", "dp"), None), P(("blk", "dp"), None), P("dp", None)),
        check_vma=False,
    )
```

profile of v0, /device:TPU:1, one launch (start us, length us, event | category | flops | bytes accessed | tf_op | source)
XLA Modules:
  0.0 367.8 jit_solution(2161456829096449778)
XLA Ops:
  7.2 1.4 fusion.2
  8.7 1.3 fusion.37
  10.0 2.7 collective-permute-start
  16.1 3.4 collective-permute-done
  19.5 2.5 collective-permute-start.1
  23.0 15.4 %collective-permute-done.1 = bf16[256,1152]{1,0:T(8,128)(2,1)S(1)} collective-permute-done((bf16[256,1152]{1,0:T(8,128)(2,1)S(1)}, bf16[256,1152]{1,0:T(8,128)(2,1)S(1)}, u32[]{:S(2)}, u32[]{:S(2)}) %collective-permute-start.1) | collective-permute-done | bytes 589856 | tf_op jit(solution)/shard_map/ppermute | solution.py:12
  38.4 2.5 collective-permute-start.2
  42.1 5.6 %collective-permute-done.2 = bf16[256,1152]{1,0:T(8,128)(2,1)S(1)} collective-permute-done((bf16[256,1152]{1,0:T(8,128)(2,1)S(1)}, bf16[256,1152]{1,0:T(8,128)(2,1)S(1)}, u32[]{:S(2)}, u32[]{:S(2)}) %collective-permute-start.2) | collective-permute-done | bytes 589856 | tf_op jit(solution)/shard_map/ppermute | solution.py:12
  47.7 2.5 collective-permute-start.3
  51.3 9.0 %collective-permute-done.5 = f32[256,1152]{1,0:T(8,128)S(1)} collective-permute-done((f32[256,1152]{1,0:T(8,128)S(1)}, f32[256,1152]{1,0:T(8,128)S(1)}, u32[]{:S(2)}, u32[]{:S(2)}) %collective-permute-start.5) | collective-permute-done | bytes 1179680 | tf_op jit(solution)/shard_map/ppermute | solution.py:12
  61.5 2.5 collective-permute-start.6
  64.0 2.7 collective-permute-done.3
  68.7 3.3 convolution_bitcast_fusion
  72.4 7.0 %collective-permute-done.6 = f32[256,1152]{1,0:T(8,128)} collective-permute-done((f32[256,1152]{1,0:T(8,128)}, f32[256,1152]{1,0:T(8,128)}, u32[]{:S(2)}, u32[]{:S(2)}) %collective-permute-start.6) | collective-permute-done | bytes 1179680 | tf_op jit(solution)/shard_map/ppermute | solution.py:12
  79.4 1.4 add.101
  80.8 2.6 collective-permute-start.7
  83.8 14.6 %collective-permute-done.7 = f32[256,1152]{1,0:T(8,128)S(1)} collective-permute-done((f32[256,1152]{1,0:T(8,128)S(1)}, f32[256,1152]{1,0:T(8,128)S(1)}, u32[]{:S(2)}, u32[]{:S(2)}) %collective-permute-start.7) | collective-permute-done | bytes 1179680 | tf_op jit(solution)/shard_map/ppermute | solution.py:12
  99.3 5.1 %collective-permute-start.8 = (bf16[256,1152]{1,0:T(8,128)(2,1)}, bf16[256,1152]{1,0:T(8,128)(2,1)}, u32[]{:S(2)}, u32[]{:S(2)}) collective-permute-start(bf16[256,1152]{1,0:T(8,128)(2,1)} %add_convert_fusion), channel_id=1, source_target_pairs={{0,192},{16,208},{32,224},{48,240},{64,0},{80,16},{96,32},{112,48}... | collective-permute-start | bytes 1769480 | tf_op jit(solution)/shard_map/ppermute | solution.py:12
  104.4 2.1 fusion.40
  106.5 246.4 %all-reduce.2.cloned.1.call-done = f32[1152,1152]{0,1:T(8,128)} async-done(((f32[1152,1152]{0,1:T(8,128)}), f32[1152,1152]{0,1:T(8,128)}) %all-reduce.2.cloned.1.call-update) | async-done | bytes 5308432 | tf_op jit(solution)/shard_map/psum | solution.py:56
  352.8 2.4 dynamic-slice_multiply_fusion
  355.2 2.0 copy.8
  357.2 1.4 fusion.3
  358.6 2.4 fusion.4
  (40 shorter events, 10.3 us)
Async XLA Ops:
  7.2 5.5 %copy-start = (bf16[1152,1152]{1,0:T(8,128)(2,1)S(1)}, bf16[1152,1152]{1,0:T(8,128)(2,1)}, u32[]{:S(2)}) copy-start(bf16[1152,1152]{1,0:T(8,128)(2,1)} %param.7) | copy-start | bytes 7962628
  7.2 5.5 %copy-start.4 = (bf16[256,1152]{1,0:T(8,128)(2,1)S(1)}, bf16[256,1152]{1,0:T(8,128)(2,1)}, u32[]{:S(2)}) copy-start(bf16[256,1152]{1,0:T(8,128)(2,1)} %param.5) | copy-start | bytes 1769476
  7.2 345.6 %all-reduce.2.cloned.1.call-start = ((), (), s32[]{:S(2)}) async-start(), calls=%async_computation | async-start | bytes 10616832 | tf_op jit(solution)/shard_map/psum | solution.py:56
  10.0 9.5 %collective-permute-start = (bf16[256,1152]{1,0:T(8,128)(2,1)S(1)}, bf16[256,1152]{1,0:T(8,128)(2,1)S(1)}, u32[]{:S(2)}, u32[]{:S(2)}) collective-permute-start(bf16[256,1152]{1,0:T(8,128)(2,1)S(1)} %fusion.37), channel_id=1, source_target_pairs={{0,16},{16,32},{32,48},{48,64},{64,80},{80,96},{96,112},{112,128},... | collective-permute-start | bytes 1769480 | tf_op jit(solution)/shard_map/ppermute | solution.py:12
  16.0 24.9 %collective-permute-start.4 = (f32[256,1152]{1,0:T(8,128)S(1)}, f32[256,1152]{1,0:T(8,128)S(1)}, u32[]{:S(2)}, u32[]{:S(2)}) collective-permute-start(f32[256,1152]{1,0:T(8,128)S(1)} %convolution_multiply_fusion.4), channel_id=1, source_target_pairs={{0,16},{16,32},{32,48},{48,64},{64,80},{80,96},{96,112},{112,128},... | collective-permute-start | bytes 3538952 | tf_op jit(solution)/shard_map/ppermute | solution.py:12
  19.5 19.0 %collective-permute-start.1 = (bf16[256,1152]{1,0:T(8,128)(2,1)S(1)}, bf16[256,1152]{1,0:T(8,128)(2,1)S(1)}, u32[]{:S(2)}, u32[]{:S(2)}) collective-permute-start(bf16[256,1152]{1,0:T(8,128)(2,1)S(1)} %collective-permute-done), channel_id=1, source_target_pairs={{0,16},{16,32},{32,48},{48,64},{64,80},{80,96},{96,112},{112,128},... | collective-permute-start | bytes 1769480 | tf_op jit(solution)/shard_map/ppermute | solution.py:12
  38.4 9.3 %collective-permute-start.2 = (bf16[256,1152]{1,0:T(8,128)(2,1)S(1)}, bf16[256,1152]{1,0:T(8,128)(2,1)S(1)}, u32[]{:S(2)}, u32[]{:S(2)}) collective-permute-start(bf16[256,1152]{1,0:T(8,128)(2,1)S(1)} %collective-permute-done.1), channel_id=1, source_target_pairs={{0,16},{16,32},{32,48},{48,64},{64,80},{80,96},{96,112},{112,128},... | collective-permute-start | bytes 1769480 | tf_op jit(solution)/shard_map/ppermute | solution.py:12
  41.3 19.1 %collective-permute-start.5 = (f32[256,1152]{1,0:T(8,128)S(1)}, f32[256,1152]{1,0:T(8,128)S(1)}, u32[]{:S(2)}, u32[]{:S(2)}) collective-permute-start(f32[256,1152]{1,0:T(8,128)S(1)} %fusion.1), channel_id=1, source_target_pairs={{0,16},{16,32},{32,48},{48,64},{64,80},{80,96},{96,112},{112,128},... | collective-permute-start | bytes 3538952 | tf_op jit(solution)/shard_map/ppermute | solution.py:12
  47.7 19.0 %collective-permute-start.3 = (bf16[256,1152]{1,0:T(8,128)(2,1)S(1)}, bf16[256,1152]{1,0:T(8,128)(2,1)S(1)}, u32[]{:S(2)}, u32[]{:S(2)}) collective-permute-start(bf16[256,1152]{1,0:T(8,128)(2,1)S(1)} %collective-permute-done.2), channel_id=1, source_target_pairs={{0,16},{16,32},{32,48},{48,64},{64,80},{80,96},{96,112},{112,128},... | collective-permute-start | bytes 1769480 | tf_op jit(solution)/shard_map/ppermute | solution.py:12
  61.5 17.9 %collective-permute-start.6 = (f32[256,1152]{1,0:T(8,128)}, f32[256,1152]{1,0:T(8,128)}, u32[]{:S(2)}, u32[]{:S(2)}) collective-permute-start(f32[256,1152]{1,0:T(8,128)} %add.100), channel_id=1, source_target_pairs={{0,16},{16,32},{32,48},{48,64},{64,80},{80,96},{96,112},{112,128},... | collective-permute-start | bytes 3538952 | tf_op jit(solution)/shard_map/ppermute | solution.py:12
  67.6 1.1 copy-start.5
  67.9 0.8 copy-start.2
  80.8 17.5 %collective-permute-start.7 = (f32[256,1152]{1,0:T(8,128)S(1)}, f32[256,1152]{1,0:T(8,128)S(1)}, u32[]{:S(2)}, u32[]{:S(2)}) collective-permute-start(f32[256,1152]{1,0:T(8,128)S(1)} %add.101), channel_id=1, source_target_pairs={{0,16},{16,32},{32,48},{48,64},{64,80},{80,96},{96,112},{112,128},... | collective-permute-start | bytes 3538952 | tf_op jit(solution)/shard_map/ppermute | solution.py:12
  83.8 20.6 %copy-start.3 = (bf16[256,1152]{1,0:T(8,128)(2,1)S(1)}, bf16[256,1152]{1,0:T(8,128)(2,1)}, u32[]{:S(2)}) copy-start(bf16[256,1152]{1,0:T(8,128)(2,1)} %copy-done.2) | copy-start | bytes 1769476
  99.3 257.9 %collective-permute-start.8 = (bf16[256,1152]{1,0:T(8,128)(2,1)}, bf16[256,1152]{1,0:T(8,128)(2,1)}, u32[]{:S(2)}, u32[]{:S(2)}) collective-permute-start(bf16[256,1152]{1,0:T(8,128)(2,1)} %add_convert_fusion), channel_id=1, source_target_pairs={{0,192},{16,208},{32,224},{48,240},{64,0},{80,16},{96,32},{112,48}... | collective-permute-start | bytes 1769480 | tf_op jit(solution)/shard_map/ppermute | solution.py:12
  106.5 250.7 %copy-start.1 = (bf16[256,1152]{1,0:T(8,128)(2,1)S(1)}, bf16[256,1152]{1,0:T(8,128)(2,1)}, u32[]{:S(2)}) copy-start(bf16[256,1152]{1,0:T(8,128)(2,1)} %param.6) | copy-start | bytes 1769476
Sparse Core Ops, SparseCore 0:
  72.2 280.6 all-reduce.1
where the time goes:
time: 369 us; the launch traced here: 368 us
  waiting for transfers between devices  304 us (82%)
  starting transfers between devices  20.5 us (6%)
  between operations  15.5 us (4%)
  other arithmetic  12.7 us (3%)
  matrix products  12.2 us (3%)
    psum x1, waiting for transfers between devices, on_device(): lax.psum(jnp.einsum('id,ie->de', images, dproj_b, preferred_element_type=...  246 us
    ppermute x9, waiting for transfers between devices, passed_along(): return lax.ppermute(value, axis, pairs)  57.7 us
    ppermute x9, starting transfers between devices, passed_along(): return lax.ppermute(value, axis, pairs)  20.4 us
  transfers between devices with their start and end apart: 10, of which 8 were waited for; matrix products, arithmetic and copies ran while one was open for 6% of the time, Pallas kernels for 0%

commit v1 on v0

v1 whole, which is shorter than its diff:
```python
import jax
import jax.numpy as jnp
from jax import lax
from jax.sharding import Mesh, PartitionSpec as P

AXES = ("yh", "x", "core", "z", "yl")
SIZES = (2, 4, 2, 8, 2)
BF = jnp.bfloat16
F32 = jnp.float32


def chip_pairs(steps):
    _, xs, cores, zs, yls = SIZES
    inner = zs * yls
    count = 16 * inner
    shift = steps * cores * inner
    return [(source, (source + shift) % count) for source in range(count)]


def core_pairs():
    inner = SIZES[3] * SIZES[4]
    return [(source, source ^ inner) for source in range(16 * inner)]


def moved(value, pairs):
    return lax.ppermute(value, AXES, pairs)


def mm(a, b, dims):
    return lax.dot_general(a, b, ((dims[:1], dims[1:]), ((), ())), preferred_element_type=F32)


def on_device(images, texts, head, scale, bias):
    scl = scale[0]
    bia = bias[0]
    core = lax.axis_index("core")
    first = core == 0
    ahead, back, swap = chip_pairs(1), chip_pairs(-1), core_pairs()

    tfloat = texts.astype(F32)
    tnorm = jnp.sqrt(jnp.sum(tfloat * tfloat, -1, keepdims=True) + 1e-06)
    unit_txt = tfloat / tnorm
    txt_b = unit_txt.astype(BF)
    t1 = moved(txt_b, ahead)
    proj = jnp.dot(images, head, preferred_element_type=F32)
    pnorm = jnp.sqrt(jnp.sum(proj * proj, -1, keepdims=True) + 1e-06)
    unit_img = proj / pnorm
    img_b = unit_img.astype(BF)
    i1 = moved(img_b, back)
    images2 = moved(images, swap)
    r1 = moved(jnp.where(first, txt_b, img_b), swap)

    def pair_grad(rows, cols):
        logit = scl * mm(rows, cols, (1, 1)) + bia
        return jax.nn.sigmoid(logit).astype(BF)

    def applied(rows, cols):
        return mm(pair_grad(rows, cols), cols, (1, 0))

    count = images.shape[0]
    eye = lax.broadcasted_iota(jnp.int32, (count, count), 0) == lax.broadcasted_iota(
        jnp.int32, (count, count), 1
    )
    logit = scl * mm(img_b, txt_b, (1, 1)) + bia
    g0 = jnp.where(eye, -jax.nn.sigmoid(-logit), jax.nn.sigmoid(logit)).astype(BF)
    dimg = mm(g0, txt_b, (1, 0))
    dtxt = mm(g0, img_b, (0, 0))

    a1 = applied(jnp.where(first, txt_b, img_b), r1)
    dimg = dimg + jnp.where(first, 0.0, a1)
    dtxt = dtxt + jnp.where(first, a1, 0.0)

    t2 = moved(t1, ahead)
    i2 = moved(i1, back)
    t1s = moved(t1, swap)
    i1s = moved(i1, swap)
    dimg = dimg + applied(img_b, t1) + applied(img_b, t1s)
    dtxt = dtxt + applied(txt_b, i1) + applied(txt_b, i1s)

    r3 = moved(jnp.where(first, i2, t2), swap)
    dimg = dimg + applied(img_b, t2)
    dtxt = dtxt + applied(txt_b, i2)
    a3 = applied(jnp.where(first, img_b, txt_b), r3)
    dimg = scl * (dimg + jnp.where(first, a3, 0.0))
    dtxt = scl * (dtxt + jnp.where(first, 0.0, a3))

    dproj_b = ((dimg - unit_img * jnp.sum(unit_img * dimg, -1, keepdims=True)) / pnorm).astype(BF)

    width = images.shape[1]
    half = width // 2
    low, high = dproj_b[:, :half], dproj_b[:, half:]
    mine = jnp.where(first, low, high)
    other = moved(jnp.where(first, high, low), swap)
    part = mm(
        jnp.concatenate([mine, other], 0), jnp.concatenate([images, images2], 0), (0, 0)
    ).astype(BF)
    chips = SIZES[0] * SIZES[1]
    piece = half // chips
    part = lax.all_to_all(part.reshape(chips, piece, width), ("yh", "x"), 0, 0)
    part = jnp.sum(part.astype(F32), 0).astype(BF)
    dps = SIZES[3] * SIZES[4]
    own = width // dps
    part = part.reshape(piece, dps, own).transpose(1, 0, 2)
    part = lax.all_to_all(part, ("z", "yl"), 0, 0)
    part = jnp.sum(part.astype(F32), 0).astype(BF)
    blks = chips * SIZES[2]
    whole = lax.all_to_all(jnp.broadcast_to(part[None], (blks, piece, own)), ("yh", "x", "core"), 0, 0)
    order = whole.reshape(chips, SIZES[2], piece, own).transpose(3, 1, 0, 2).reshape(own, width)
    total_pairs = count * 256
    head_grad = order.astype(F32) * (1.0 / jnp.sqrt(jnp.float32(total_pairs)))

    grad_image = mm(dproj_b, head, (1, 1))
    grad_text = (dtxt - unit_txt * jnp.sum(unit_txt * dtxt, -1, keepdims=True)) / tnorm
    return (grad_image, grad_text, head_grad)


def solution(mesh):
    fine = Mesh(mesh.devices.reshape(SIZES), AXES)
    rows = P(AXES, None)
    return jax.shard_map(
        on_device,
        mesh=fine,
        in_specs=(rows, rows, P(), P(), P()),
        out_specs=(rows, rows, P(("z", "yl"), None)),
        check_vma=False,
    )
```

time: 369 us -> 142 us (0.38)
  waiting for transfers between devices: 304 us -> 30.3 us
  matrix products: 12.2 us -> 41.7 us
  starting transfers between devices: 20.5 us -> 46.4 us
  between operations: 15.5 us -> 2.08 us
  local copies, waits for them, and re-layouts: 2.85 us -> 8.86 us
    psum x1 -> x0, waiting for transfers between devices: 246 us -> none  [on_device(): lax.psum(jnp.einsum('id,ie->de', images, dproj_b, preferred_element_type=...]
    ppermute x9 -> x10, waiting for transfers between devices: 57.7 us -> 8.83 us  [moved(): return lax.ppermute(value, AXES, pairs)]
    dot_general x18 -> x14, matrix products: 12.2 us -> 41.7 us  [the longest x13 39.5 us: mm(): lax.dot_general(a, b, ((dims[:1], dims[1:]), ((), ())), preferred_element...]
    all_to_all x0 -> x3, starting transfers between devices: none -> 23.4 us  [the longest x1 9.08 us: on_device(): part = lax.all_to_all(part, ('z', 'yl'), 0, 0)]
    all_to_all x0 -> x3, waiting for transfers between devices: none -> 21.5 us  [the longest x1 8.38 us: on_device(): part = lax.all_to_all(part, ('z', 'yl'), 0, 0)]
    ppermute x9 -> x10, starting transfers between devices: 20.4 us -> 22.9 us  [moved(): return lax.ppermute(value, AXES, pairs)]
  transfers between devices with their start and end apart: 10 -> 13, of which waited for: 8 -> 6; matrix products, arithmetic and copies ran while one was open for 6% -> 30% of each run, Pallas kernels for 0% -> 0%
where the time goes in v1:
time: 142 us
  starting transfers between devices  46.4 us (33%)
  matrix products  41.7 us (29%)
  waiting for transfers between devices  30.3 us (21%)
  other arithmetic  12.2 us (9%)
  local copies, waits for them, and re-layouts  8.86 us (6%)
  between operations  2.08 us (1%)
    dot_general x13, matrix products, mm(): lax.dot_general(a, b, ((dims[:1], dims[1:]), ((), ())), preferred_element...  39.5 us
    ppermute x10, starting transfers between devices, moved(): return lax.ppermute(value, AXES, pairs)  22.9 us
    all_to_all x1, starting transfers between devices, on_device(): part = lax.all_to_all(part, ('z', 'yl'), 0, 0)  9.08 us
    ppermute x10, waiting for transfers between devices, moved(): return lax.ppermute(value, AXES, pairs)  8.83 us
    all_to_all x1, waiting for transfers between devices, on_device(): part = lax.all_to_all(part, ('z', 'yl'), 0, 0)  8.38 us
    all_to_all x1, starting transfers between devices, on_device(): part = lax.all_to_all(part.reshape(chips, piece, width), ('yh', 'x'), 0, 0)  8.3 us
    all_to_all x1, waiting for transfers between devices, on_device(): lax.all_to_all(jnp.broadcast_to(part[None], (blks, piece, own)), ('yh', '...  6.85 us
    all_to_all x1, waiting for transfers between devices, on_device(): part = lax.all_to_all(part.reshape(chips, piece, width), ('yh', 'x'), 0, 0)  6.29 us
  transfers between devices with their start and end apart: 13, of which 6 were waited for; matrix products, arithmetic and copies ran while one was open for 30% of the time, Pallas kernels for 0%

profile of v1, /device:TPU:1, one launch (start us, length us, event | category | flops | bytes accessed | tf_op | source)
XLA Modules:
  0.0 141.5 jit_solution(3111369222761425296)
XLA Ops:
  7.8 3.9 %collective-permute-start.4 = (bf16[256,1152]{1,0:T(8,128)(2,1)S(1)}, bf16[256,1152]{1,0:T(8,128)(2,1)}, u32[]{:S(2)}, u32[]{:S(2)}) collective-permute-start(bf16[256,1152]{1,0:T(8,128)(2,1)S(1)} %get-tuple-element.4), channel_id=1, source_target_pairs={{0,224},{1,225},{2,226},{3,227},{4,228},{5,229},{6,230},{7,231},{8... | collective-permute-start | bytes 1769480 | tf_op jit(solution)/shard_map/ppermute | solution.py:26
  11.7 2.9 %collective-permute-start = (bf16[256,1152]{1,0:T(8,128)(2,1)S(1)}, bf16[256,1152]{1,0:T(8,128)(2,1)S(1)}, u32[]{:S(2)}, u32[]{:S(2)}) collective-permute-start(bf16[256,1152]{1,0:T(8,128)(2,1)S(1)} %get-tuple-element.3), channel_id=1, source_target_pairs={{0,16},{1,17},{2,18},{3,19},{4,20},{5,21},{6,22},{7,23},{8,24},{9,... | collective-permute-start | bytes 1769480 | tf_op jit(solution)/shard_map/ppermute | solution.py:26
  16.0 6.8 %collective-permute-done.1 = bf16[256,1152]{1,0:T(8,128)(2,1)} collective-permute-done((bf16[256,1152]{1,0:T(8,128)(2,1)S(1)}, bf16[256,1152]{1,0:T(8,128)(2,1)}, u32[]{:S(2)}, u32[]{:S(2)}) %collective-permute-start.1) | collective-permute-done | bytes 589856 | tf_op jit(solution)/shard_map/ppermute | solution.py:26
  22.8 5.1 %collective-permute-start.5 = (bf16[256,1152]{1,0:T(8,128)(2,1)}, bf16[256,1152]{1,0:T(8,128)(2,1)}, u32[]{:S(2)}, u32[]{:S(2)}) collective-permute-start(bf16[256,1152]{1,0:T(8,128)(2,1)} %collective-permute-done.4), channel_id=1, source_target_pairs={{0,224},{1,225},{2,226},{3,227},{4,228},{5,229},{6,230},{7,231},{8... | collective-permute-start | bytes 1769480 | tf_op jit(solution)/shard_map/ppermute | solution.py:26
  29.7 3.9 %collective-permute-start.2 = (bf16[256,1152]{1,0:T(8,128)(2,1)}, bf16[256,1152]{1,0:T(8,128)(2,1)}, u32[]{:S(2)}, u32[]{:S(2)}) collective-permute-start(bf16[256,1152]{1,0:T(8,128)(2,1)} %collective-permute-done.1), channel_id=1, source_target_pairs={{0,16},{1,17},{2,18},{3,19},{4,20},{5,21},{6,22},{7,23},{8,24},{9,... | collective-permute-start | bytes 1769480 | tf_op jit(solution)/shard_map/ppermute | solution.py:26
  34.4 3.4 %fusion.62 = f32[256,1152]{1,0:T(8,128)} fusion(bf16[256,1152]{1,0:T(8,128)(2,1)} %copy-done.8, bf16[256,1152]{1,0:T(8,128)(2,1)} %copy-done.7, f32[]{:T(128)} %bitcast.59, f32[]{:T(128)} %bitcast.50), kind=kOutput, calls=%fused_computation.83 | convolution fusion | flops 302383104 | bytes 2359304 | tf_op jit(solution)/shard_map/dot_general | solution.py:30
  40.3 4.2 %collective-permute-start.6 = (bf16[256,1152]{1,0:T(8,128)(2,1)}, bf16[256,1152]{1,0:T(8,128)(2,1)}, u32[]{:S(2)}, u32[]{:S(2)}) collective-permute-start(bf16[256,1152]{1,0:T(8,128)(2,1)} %broadcast_select_fusion), channel_id=1, source_target_pairs={{0,16},{1,17},{2,18},{3,19},{4,20},{5,21},{6,22},{7,23},{8,24},{9,... | collective-permute-start | bytes 1769480 | tf_op jit(solution)/shard_map/ppermute | solution.py:26
  44.5 4.1 %convolution_add_fusion.3 = f32[256,1152]{1,0:T(8,128)} fusion(bf16[256,1152]{1,0:T(8,128)(2,1)} %collective-permute-done.1, f32[256,1152]{1,0:T(8,128)} %fusion.107, f32[256,1152]{1,0:T(8,128)} %fusion.62, bf16[256,1152]{1,0:T(8,128)(2,1)} %copy-done.1, pred[]{:T(512)S(6)} %eq.7, f32[]{:T(128)} %bitcast.58, f32[]{:T(128)} %bitcast.49), kind=kOutput, calls=%fused_computation.4 | convolution fusion | flops 303267840 | bytes 4718601 | tf_op jit(solution)/shard_map/dot_general | solution.py:30
  48.6 3.4 %fusion.61 = f32[256,1152]{1,0:T(8,128)} fusion(bf16[256,1152]{1,0:T(8,128)(2,1)} %collective-permute-done.3, bf16[256,1152]{1,0:T(8,128)(2,1)} %copy-done.1, f32[]{:T(128)} %bitcast.56, f32[]{:T(128)} %bitcast.48), kind=kOutput, calls=%fused_computation.82 | convolution fusion | flops 302383104 | bytes 2359304 | tf_op jit(solution)/shard_map/dot_general | solution.py:30
  52.1 3.2 %fusion.60 = f32[256,1152]{1,0:T(8,128)} fusion(bf16[256,1152]{1,0:T(8,128)(2,1)} %collective-permute-done.6, bf16[256,1152]{1,0:T(8,128)(2,1)} %copy-done.1, bf16[256,1152]{1,0:T(8,128)(2,1)S(1)} %get-tuple-element.5, pred[]{:T(512)S(6)} %eq.7, f32[]{:T(128)} %bitcast.55, f32[]{:T(128)} %bitcast.47), kind=kOutput, calls=%fused_computation.81 | convolution fusion | flops 302678016 | bytes 2949129 | tf_op jit(solution)/shard_map/dot_general | solution.py:30
  55.3 4.5 %multiply_reduce_fusion.1 = (f32[256]{0:T(256)S(1)}, f32[256,1152]{1,0:T(8,128)}) fusion(f32[256,1152]{1,0:T(8,128)} %copy-done.4, f32[256]{0:T(256)S(1)} %get-tuple-element.15, f32[256,1152]{1,0:T(8,128)} %fusion.60, pred[]{:T(512)S(6)} %eq.7, f32[256,1152]{1,0:T(8,128)} %fusion.61, f32[256,1152]{1,0:T(8,128)} %convolution_add_fusion.3, ...), kind=kOutput, calls=%fused_computation.20 | convolution fusion | flops 304742144 | bytes 7079945 | tf_op jit(solution)/shard_map/dot_general | solution.py:30
  64.6 3.3 %convolution_convert_fusion = bf16[576,1152]{1,0:T(8,128)(2,1)} fusion(bf16[256,1152]{1,0:T(8,128)(2,1)} %collective-permute-done.9, bf16[256,1152]{1,0:T(8,128)(2,1)} %param.5, bf16[256,576]{1,0:T(8,128)(2,1)S(1)} %collective-permute-done.8, bf16[256,576]{1,0:T(8,128)(2,1)S(1)} %get-tuple-element.6), kind=kOutput, calls=%fused_computation | convolution fusion | flops 683679744 | bytes 3096576 | tf_op jit(solution)/shard_map/dot_general | solution.py:30
  67.8 8.3 %all-to-all-start = ((bf16[8,72,1152]{2,1,0:T(8,128)(2,1)}), bf16[8,72,1152]{2,1,0:T(8,128)(2,1)}, u32[]{:S(2)}, u32[]{:S(2)}) async-start(bf16[8,72,1152]{2,1,0:T(8,128)(2,1)} %bitcast.61), calls=%async_computation | async-start | bytes 2654208 | tf_op jit(solution)/shard_map/all_to_all | solution.py:99
  76.2 2.4 %fusion.109 = f32[256,1152]{1,0:T(8,128)} fusion(bf16[256,256]{1,0:T(8,128)(2,1)S(1)} %select_convert_fusion, bf16[256,1152]{1,0:T(8,128)(2,1)} %copy-done.1), kind=kOutput, calls=%fused_computation.136 | convolution fusion | flops 150994944 | bytes 1900544 | tf_op jit(solution)/shard_map/dot_general | solution.py:30
  79.0 3.6 %convolution_add_fusion.1 = f32[256,1152]{1,0:T(8,128)} fusion(bf16[256,1152]{1,0:T(8,128)(2,1)} %collective-permute-done.4, f32[256,1152]{1,0:T(8,128)} %fusion.109, f32[256,1152]{1,0:T(8,128)} %fusion.62, bf16[256,1152]{1,0:T(8,128)(2,1)S(1)} %get-tuple-element.5, pred[]{:T(512)S(6)} %eq.7, f32[]{:T(128)} %bitcast.54, f32[]{:T(128)} %bitcast.46), kind=kOutput, calls=%fused_computation.2 | convolution fusion | flops 303267840 | bytes 4718601 | tf_op jit(solution)/shard_map/dot_general | solution.py:30
  82.6 3.2 %fusion.59 = f32[256,1152]{1,0:T(8,128)} fusion(bf16[256,1152]{1,0:T(8,128)(2,1)} %collective-permute-done.5, bf16[256,1152]{1,0:T(8,128)(2,1)S(1)} %get-tuple-element.5, f32[]{:T(128)} %bitcast.52, f32[]{:T(128)} %bitcast.45), kind=kOutput, calls=%fused_computation.80 | convolution fusion | flops 302383104 | bytes 2359304 | tf_op jit(solution)/shard_map/dot_general | solution.py:30
  85.8 4.5 %multiply_reduce_fusion = (f32[256]{0:T(256)S(1)}, f32[256,1152]{1,0:T(8,128)}) fusion(f32[256]{0:T(256)S(1)} %get-tuple-element.14, bf16[256,1152]{1,0:T(8,128)(2,1)} %param.6, f32[256,1152]{1,0:T(8,128)} %fusion.60, pred[]{:T(512)S(6)} %eq.7, f32[256,1152]{1,0:T(8,128)} %fusion.59, f32[256,1152]{1,0:T(8,128)} %convolution_add_fusion.1, ...), kind=kOutput, calls=%fused_computation.18 | convolution fusion | flops 305037056 | bytes 6490121 | tf_op jit(solution)/shard_map/dot_general | solution.py:30
  90.3 6.3 %all-to-all-done = bf16[8,72,1152]{2,1,0:T(8,128)(2,1)} async-done(((bf16[8,72,1152]{2,1,0:T(8,128)(2,1)}), bf16[8,72,1152]{2,1,0:T(8,128)(2,1)}, u32[]{:S(2)}, u32[]{:S(2)}) %all-to-all-start) | async-done | bytes 1327136 | tf_op jit(solution)/shard_map/all_to_all | solution.py:99
  96.6 2.2 %reduce_sum.64 = bf16[72,1152]{1,0:T(8,128)(2,1)} reduce(bf16[8,72,1152]{2,1,0:T(8,128)(2,1)} %all-to-all-done, bf16[]{:T(256)} %constant.17.clone.1), dimensions={0}, to_apply=%region_4.5 | reduce | flops 580608 | bytes 1492994 | tf_op jit(solution)/shard_map/reduce_sum | solution.py:100
  101.1 9.1 %all-to-all-start.1 = ((bf16[16,72,72]{2,1,0:T(8,128)(2,1)}), bf16[16,72,72]{2,1,0:T(8,128)(2,1)S(1)}, u32[]{:S(2)}, u32[]{:S(2)}) async-start(bf16[16,72,72]{2,1,0:T(8,128)(2,1)} %copy.10), calls=%async_computation.1 | async-start | bytes 589824 | tf_op jit(solution)/shard_map/all_to_all | solution.py:104
  110.2 2.6 %subtract_divide_fusion = f32[256,1152]{1,0:T(8,128)} fusion(f32[256,1152]{1,0:T(8,128)} %get-tuple-element.13, f32[256]{0:T(256)S(1)} %get-tuple-element.12, f32[256]{0:T(256)S(1)} %get-tuple-element.14, bf16[256,1152]{1,0:T(8,128)(2,1)S(1)} %copy-done.3), kind=kLoop, calls=%fused_computation.17 | loop fusion | flops 1474560 | bytes 2951168 | tf_op jit(solution)/shard_map/div | solution.py:113
  112.8 8.4 %all-to-all-done.1 = bf16[16,72,72]{2,1,0:T(8,128)(2,1)S(1)} async-done(((bf16[16,72,72]{2,1,0:T(8,128)(2,1)}), bf16[16,72,72]{2,1,0:T(8,128)(2,1)S(1)}, u32[]{:S(2)}, u32[]{:S(2)}) %all-to-all-start.1) | async-done | bytes 165920 | tf_op jit(solution)/shard_map/all_to_all | solution.py:104
  123.3 6.1 %all-to-all-start.2 = ((bf16[16,72,72]{2,1,0:T(8,128)(2,1)}), bf16[16,72,72]{2,1,0:T(8,128)(2,1)S(1)}, u32[]{:S(2)}, u32[]{:S(2)}) async-start(bf16[16,72,72]{2,1,0:T(8,128)(2,1)} %broadcast_in_dim.11), calls=%async_computation.2 | async-start | bytes 589824 | tf_op jit(solution)/shard_map/all_to_all | solution.py:107
  131.4 6.8 %all-to-all-done.2 = bf16[16,72,72]{2,1,0:T(8,128)(2,1)S(1)} async-done(((bf16[16,72,72]{2,1,0:T(8,128)(2,1)}), bf16[16,72,72]{2,1,0:T(8,128)(2,1)S(1)}, u32[]{:S(2)}, u32[]{:S(2)}) %all-to-all-start.2) | async-done | bytes 165920 | tf_op jit(solution)/shard_map/all_to_all | solution.py:107
  (49 shorter events, 27.2 us)
Async XLA Ops:
  0.6 1.9 %copy-start = (bf16[1152,1152]{1,0:T(8,128)(2,1)S(1)}, bf16[1152,1152]{1,0:T(8,128)(2,1)}, u32[]{:S(2)}) copy-start(bf16[1152,1152]{1,0:T(8,128)(2,1)} %param.7) | copy-start | bytes 7962628
  2.6 2.2 %copy-start.2 = (bf16[256,1152]{1,0:T(8,128)(2,1)S(1)}, bf16[256,1152]{1,0:T(8,128)(2,1)}, u32[]{:S(2)}) copy-start(bf16[256,1152]{1,0:T(8,128)(2,1)} %param.6) | copy-start | bytes 1769476
  4.8 1.0 copy-start.4
  5.8 22.5 %copy-start.1 = (bf16[256,1152]{1,0:T(8,128)(2,1)}, bf16[256,1152]{1,0:T(8,128)(2,1)S(1)}, u32[]{:S(2)}) copy-start(bf16[256,1152]{1,0:T(8,128)(2,1)S(1)} %get-tuple-element.4) | copy-start | bytes 1769476
  5.8 22.5 %copy-start.7 = (bf16[256,1152]{1,0:T(8,128)(2,1)}, bf16[256,1152]{1,0:T(8,128)(2,1)S(1)}, u32[]{:S(2)}) copy-start(bf16[256,1152]{1,0:T(8,128)(2,1)S(1)} %get-tuple-element.3) | copy-start | bytes 1769476
  5.8 17.0 %collective-permute-start.1 = (bf16[256,1152]{1,0:T(8,128)(2,1)S(1)}, bf16[256,1152]{1,0:T(8,128)(2,1)}, u32[]{:S(2)}, u32[]{:S(2)}) collective-permute-start(bf16[256,1152]{1,0:T(8,128)(2,1)S(1)} %get-tuple-element.5), channel_id=1, source_target_pairs={{0,32},{1,33},{2,34},{3,35},{4,36},{5,37},{6,38},{7,39},{8,40},{9,... | collective-permute-start | bytes 1769480 | tf_op jit(solution)/shard_map/ppermute | solution.py:26
  7.8 15.0 %collective-permute-start.4 = (bf16[256,1152]{1,0:T(8,128)(2,1)S(1)}, bf16[256,1152]{1,0:T(8,128)(2,1)}, u32[]{:S(2)}, u32[]{:S(2)}) collective-permute-start(bf16[256,1152]{1,0:T(8,128)(2,1)S(1)} %get-tuple-element.4), channel_id=1, source_target_pairs={{0,224},{1,225},{2,226},{3,227},{4,228},{5,229},{6,230},{7,231},{8... | collective-permute-start | bytes 1769480 | tf_op jit(solution)/shard_map/ppermute | solution.py:26
  11.7 21.8 %collective-permute-start = (bf16[256,1152]{1,0:T(8,128)(2,1)S(1)}, bf16[256,1152]{1,0:T(8,128)(2,1)S(1)}, u32[]{:S(2)}, u32[]{:S(2)}) collective-permute-start(bf16[256,1152]{1,0:T(8,128)(2,1)S(1)} %get-tuple-element.3), channel_id=1, source_target_pairs={{0,16},{1,17},{2,18},{3,19},{4,20},{5,21},{6,22},{7,23},{8,24},{9,... | collective-permute-start | bytes 1769480 | tf_op jit(solution)/shard_map/ppermute | solution.py:26
  14.7 48.4 %collective-permute-start.9 = (bf16[256,1152]{1,0:T(8,128)(2,1)}, bf16[256,1152]{1,0:T(8,128)(2,1)}, u32[]{:S(2)}, u32[]{:S(2)}) collective-permute-start(bf16[256,1152]{1,0:T(8,128)(2,1)} %param.5), channel_id=1, source_target_pairs={{0,16},{1,17},{2,18},{3,19},{4,20},{5,21},{6,22},{7,23},{8,24},{9,... | collective-permute-start | bytes 1769480 | tf_op jit(solution)/shard_map/ppermute | solution.py:26
  22.8 15.4 %collective-permute-start.3 = (bf16[256,1152]{1,0:T(8,128)(2,1)}, bf16[256,1152]{1,0:T(8,128)(2,1)}, u32[]{:S(2)}, u32[]{:S(2)}) collective-permute-start(bf16[256,1152]{1,0:T(8,128)(2,1)} %collective-permute-done.1), channel_id=1, source_target_pairs={{0,32},{1,33},{2,34},{3,35},{4,36},{5,37},{6,38},{7,39},{8,40},{9,... | collective-permute-start | bytes 1769480 | tf_op jit(solution)/shard_map/ppermute | solution.py:26
  22.8 15.4 %collective-permute-start.5 = (bf16[256,1152]{1,0:T(8,128)(2,1)}, bf16[256,1152]{1,0:T(8,128)(2,1)}, u32[]{:S(2)}, u32[]{:S(2)}) collective-permute-start(bf16[256,1152]{1,0:T(8,128)(2,1)} %collective-permute-done.4), channel_id=1, source_target_pairs={{0,224},{1,225},{2,226},{3,227},{4,228},{5,229},{6,230},{7,231},{8... | collective-permute-start | bytes 1769480 | tf_op jit(solution)/shard_map/ppermute | solution.py:26
  29.7 25.6 %collective-permute-start.2 = (bf16[256,1152]{1,0:T(8,128)(2,1)}, bf16[256,1152]{1,0:T(8,128)(2,1)}, u32[]{:S(2)}, u32[]{:S(2)}) collective-permute-start(bf16[256,1152]{1,0:T(8,128)(2,1)} %collective-permute-done.1), channel_id=1, source_target_pairs={{0,16},{1,17},{2,18},{3,19},{4,20},{5,21},{6,22},{7,23},{8,24},{9,... | collective-permute-start | bytes 1769480 | tf_op jit(solution)/shard_map/ppermute | solution.py:26
  33.6 0.8 copy-start.8
  40.3 11.8 %collective-permute-start.6 = (bf16[256,1152]{1,0:T(8,128)(2,1)}, bf16[256,1152]{1,0:T(8,128)(2,1)}, u32[]{:S(2)}, u32[]{:S(2)}) collective-permute-start(bf16[256,1152]{1,0:T(8,128)(2,1)} %broadcast_select_fusion), channel_id=1, source_target_pairs={{0,16},{1,17},{2,18},{3,19},{4,20},{5,21},{6,22},{7,23},{8,24},{9,... | collective-permute-start | bytes 1769480 | tf_op jit(solution)/shard_map/ppermute | solution.py:26
  61.7 0.8 copy-start.5
  62.7 1.9 %collective-permute-start.8 = (bf16[256,576]{1,0:T(8,128)(2,1)S(1)}, bf16[256,576]{1,0:T(8,128)(2,1)S(1)}, u32[]{:S(2)}, u32[]{:S(2)}) collective-permute-start(bf16[256,576]{1,0:T(8,128)(2,1)S(1)} %get-tuple-element.7), channel_id=1, source_target_pairs={{0,16},{1,17},{2,18},{3,19},{4,20},{5,21},{6,22},{7,23},{8,24},{9,... | collective-permute-start | bytes 884744 | tf_op jit(solution)/shard_map/ppermute | solution.py:26
  67.8 28.8 %all-to-all-start = ((bf16[8,72,1152]{2,1,0:T(8,128)(2,1)}), bf16[8,72,1152]{2,1,0:T(8,128)(2,1)}, u32[]{:S(2)}, u32[]{:S(2)}) async-start(bf16[8,72,1152]{2,1,0:T(8,128)(2,1)} %bitcast.61), calls=%async_computation | async-start | bytes 2654208 | tf_op jit(solution)/shard_map/all_to_all | solution.py:99
  78.6 7.2 %collective-permute-start.7 = (bf16[256,1152]{1,0:T(8,128)(2,1)}, bf16[256,1152]{1,0:T(8,128)(2,1)}, u32[]{:S(2)}, u32[]{:S(2)}) collective-permute-start(bf16[256,1152]{1,0:T(8,128)(2,1)} %collective-permute-done.4), channel_id=1, source_target_pairs={{0,16},{1,17},{2,18},{3,19},{4,20},{5,21},{6,22},{7,23},{8,24},{9,... | collective-permute-start | bytes 1769480 | tf_op jit(solution)/shard_map/ppermute | solution.py:26
  98.8 11.4 %copy-start.3 = (bf16[256,1152]{1,0:T(8,128)(2,1)S(1)}, bf16[256,1152]{1,0:T(8,128)(2,1)}, u32[]{:S(2)}) copy-start(bf16[256,1152]{1,0:T(8,128)(2,1)} %param.6) | copy-start | bytes 1769476
  101.1 20.0 %all-to-all-start.1 = ((bf16[16,72,72]{2,1,0:T(8,128)(2,1)}), bf16[16,72,72]{2,1,0:T(8,128)(2,1)S(1)}, u32[]{:S(2)}, u32[]{:S(2)}) async-start(bf16[16,72,72]{2,1,0:T(8,128)(2,1)} %copy.10), calls=%async_computation.1 | async-start | bytes 589824 | tf_op jit(solution)/shard_map/all_to_all | solution.py:104
  112.8 16.6 %copy-start.6 = (bf16[256,1152]{1,0:T(8,128)(2,1)S(1)}, bf16[256,1152]{1,0:T(8,128)(2,1)}, u32[]{:S(2)}) copy-start(bf16[256,1152]{1,0:T(8,128)(2,1)} %copy-done.5) | copy-start | bytes 1769476
  123.3 15.0 %all-to-all-start.2 = ((bf16[16,72,72]{2,1,0:T(8,128)(2,1)}), bf16[16,72,72]{2,1,0:T(8,128)(2,1)S(1)}, u32[]{:S(2)}, u32[]{:S(2)}) async-start(bf16[16,72,72]{2,1,0:T(8,128)(2,1)} %broadcast_in_dim.11), calls=%async_computation.2 | async-start | bytes 589824 | tf_op jit(solution)/shard_map/all_to_all | solution.py:107

commit v2 on v1

v2 whole, which is shorter than its diff:
```python
import functools

import jax
import jax.numpy as jnp
from jax import lax
from jax.experimental import pallas as pl
from jax.experimental.pallas import tpu as pltpu
from jax.sharding import Mesh, PartitionSpec as P

AXES = ("yh", "x", "core", "z", "yl")
SIZES = (2, 4, 2, 8, 2)
INNER = SIZES[3] * SIZES[4]
COUNT = 16 * INNER
CHIPS = SIZES[0] * SIZES[1]
BLKS = CHIPS * SIZES[2]
BF = jnp.bfloat16
F32 = jnp.float32


def chip_pairs(steps):
    shift = steps * SIZES[2] * INNER
    return [(source, (source + shift) % COUNT) for source in range(COUNT)]


def core_pairs(only=None):
    return [
        (source, source ^ INNER)
        for source in range(COUNT)
        if only is None or (source // INNER) % 2 == only
    ]


def moved(value, pairs):
    return lax.ppermute(value, AXES, pairs)


def mm(a, b, dims):
    return lax.dot_general(a, b, ((dims[:1], dims[1:]), ((), ())), preferred_element_type=F32)


def call(body, outs, *args, scalars=(), pairs=0.0):
    in_specs = [pl.BlockSpec(memory_space=pltpu.SMEM)] * len(scalars)
    in_specs += [pl.BlockSpec(memory_space=pltpu.VMEM)] * len(args)
    return pl.pallas_call(
        body,
        out_shape=[jax.ShapeDtypeStruct(shape, dtype) for shape, dtype in outs],
        in_specs=in_specs,
        out_specs=[pl.BlockSpec(memory_space=pltpu.VMEM)] * len(outs),
        cost_estimate=pl.CostEstimate(
            flops=int(pairs * 3.02e8),
            bytes_accessed=sum(int(a.size) * a.dtype.itemsize for a in args),
            transcendentals=0,
        ),
        compiler_params=pltpu.CompilerParams(vmem_limit_bytes=32 * 2**20),
    )(*scalars, *args)


def sigmoid(x):
    return 1.0 / (1.0 + jnp.exp(-x))


def applied(par, rows, cols):
    logit = par[0] * mm(rows, cols, (1, 1)) + par[1]
    return mm(sigmoid(logit).astype(BF), cols, (1, 0))


def text_unit(texts):
    tfloat = texts.astype(F32)
    tnorm = jnp.sqrt(jnp.sum(tfloat * tfloat, -1, keepdims=True) + 1e-06)
    return tfloat / tnorm, tnorm


def text_body(texts, out):
    out[...] = text_unit(texts[...])[0].astype(BF)


def image_body(core, images, head, txt_b, unit, norm, img_b, mixed):
    proj = jnp.dot(images[...], head[...], preferred_element_type=F32)
    pnorm = jnp.sqrt(jnp.sum(proj * proj, -1, keepdims=True) + 1e-06)
    value = proj / pnorm
    unit[...] = value
    norm[...] = pnorm
    low = value.astype(BF)
    img_b[...] = low

    @pl.when(core[0] == 0)
    def _():
        mixed[...] = txt_b[...]

    @pl.when(core[0] != 0)
    def _():
        mixed[...] = low


def home_body(par, core, img_b, txt_b, r1, dimg, dtxt):
    logit = par[0] * mm(img_b[...], txt_b[...], (1, 1)) + par[1]
    eye = lax.broadcasted_iota(jnp.int32, logit.shape, 0) == lax.broadcasted_iota(
        jnp.int32, logit.shape, 1
    )
    away = sigmoid(logit)
    grad = jnp.where(eye, -sigmoid(-logit), away).astype(BF)
    dimg[...] = mm(grad, txt_b[...], (1, 0))
    dtxt[...] = mm(grad, img_b[...], (0, 0))

    @pl.when(core[0] == 0)
    def _():
        dtxt[...] += applied(par, txt_b[...], r1[...])

    @pl.when(core[0] != 0)
    def _():
        dimg[...] += applied(par, img_b[...], r1[...])


def two_body(par, own, near, nears, old, new):
    new[...] = old[...] + applied(par, own[...], near[...]) + applied(par, own[...], nears[...])


def one_body(par, own, near, old, new):
    new[...] = old[...] + applied(par, own[...], near[...])


def image_end_body(par, core, img_b, r3, old, unit, norm, whole, keep, send, total):
    total[...] = old[...]

    @pl.when(core[0] == 0)
    def _():
        total[...] += applied(par, img_b[...], r3[...])

    dimg = par[0] * total[...]
    value = unit[...]
    dproj = ((dimg - value * jnp.sum(value * dimg, -1, keepdims=True)) / norm[...]).astype(BF)
    whole[...] = dproj
    half = dproj.shape[1] // 2

    @pl.when(core[0] == 0)
    def _():
        keep[...] = dproj[:, :half]
        send[...] = dproj[:, half:]

    @pl.when(core[0] != 0)
    def _():
        keep[...] = dproj[:, half:]
        send[...] = dproj[:, :half]


def head_body(keep, other, images, images2, out):
    total = mm(keep[...], images[...], (0, 0)) + mm(other[...], images2[...], (0, 0))
    out[...] = total.astype(BF).reshape(out.shape)


def text_end_body(par, core, txt_b, i2, r3, old, texts, out):
    out[...] = old[...] + applied(par, txt_b[...], i2[...])

    @pl.when(core[0] != 0)
    def _():
        out[...] += applied(par, txt_b[...], r3[...])

    dtxt = par[0] * out[...]
    value, tnorm = text_unit(texts[...])
    out[...] = (dtxt - value * jnp.sum(value * dtxt, -1, keepdims=True)) / tnorm


def grad_image_body(dproj, head, out):
    out[...] = mm(dproj[...], head[...], (1, 1))


def added(ref):
    total = ref[0].astype(F32)
    for k in range(1, ref.shape[0]):
        total = total + ref[k].astype(F32)
    return total


def split_body(parts, out):
    total = added(parts)
    own = out.shape[2]
    for k in range(out.shape[0]):
        out[k] = total[:, k * own : (k + 1) * own].astype(BF)


def spread_body(parts, out):
    total = added(parts).astype(BF)
    for k in range(out.shape[0]):
        out[k] = total


def join_body(factor, parts, out):
    cores = SIZES[2]
    pieces = [
        parts[chip * cores + core].astype(F32) for core in range(cores) for chip in range(CHIPS)
    ]
    out[...] = jnp.concatenate(pieces, 0).T * factor


def on_device(images, texts, head, scale, bias):
    par = jnp.concatenate([scale, bias])
    core = lax.axis_index("core").astype(jnp.int32).reshape(1)
    ahead, back, swap = chip_pairs(1), chip_pairs(-1), core_pairs()
    count, width = images.shape
    half = width // 2
    big = (count, width)

    (txt_b,) = call(text_body, [(big, BF)], texts, pairs=1)
    t1 = moved(txt_b, ahead)
    unit_img, pnorm, img_b, mixed = call(
        image_body,
        [(big, F32), ((count, 1), F32), (big, BF), (big, BF)],
        images, head, txt_b, scalars=(core,), pairs=4,
    )
    i1 = moved(img_b, back)
    images2 = moved(images, swap)
    r1 = moved(mixed, swap)
    dimg, dtxt = call(home_body, [(big, F32)] * 2, img_b, txt_b, r1, scalars=(par, core), pairs=3)

    t2 = moved(t1, ahead)
    i2 = moved(i1, back)
    t1s = moved(t1, swap)
    i1s = moved(i1, swap)
    (dimg,) = call(two_body, [(big, F32)], img_b, t1, t1s, dimg, scalars=(par,), pairs=2)
    (dtxt,) = call(two_body, [(big, F32)], txt_b, i1, i1s, dtxt, scalars=(par,), pairs=2)

    r3t = moved(t2, core_pairs(1))
    r3i = moved(i2, core_pairs(0))
    (dimg,) = call(one_body, [(big, F32)], img_b, t2, dimg, scalars=(par,), pairs=1)
    dproj, keep, send = call(
        image_end_body,
        [(big, BF), ((count, half), BF), ((count, half), BF), (big, F32)],
        img_b, r3t, dimg, unit_img, pnorm, scalars=(par, core), pairs=2,
    )[:3]
    other = moved(send, swap)
    piece = half // CHIPS
    (part,) = call(head_body, [((CHIPS, piece, width), BF)], keep, other, images, images2, pairs=2)
    part = lax.all_to_all(part, ("yh", "x"), 0, 0)
    own = width // INNER
    (grad_text,) = call(
        text_end_body, [(big, F32)], txt_b, i2, r3i, dtxt, texts, scalars=(par, core), pairs=3
    )
    (grad_image,) = call(grad_image_body, [(big, F32)], dproj, head, pairs=2)
    (part,) = call(split_body, [((INNER, piece, own), BF)], part)
    part = lax.all_to_all(part, ("z", "yl"), 0, 0)
    (part,) = call(spread_body, [((BLKS, piece, own), BF)], part)
    part = lax.all_to_all(part, ("yh", "x", "core"), 0, 0)
    factor = 1.0 / float(count * COUNT) ** 0.5
    (head_grad,) = call(functools.partial(join_body, factor), [((own, width), F32)], part)
    return (grad_image, grad_text, head_grad)


def solution(mesh):
    fine = Mesh(mesh.devices.reshape(SIZES), AXES)
    rows = P(AXES, None)
    return jax.shard_map(
        on_device,
        mesh=fine,
        in_specs=(rows, rows, P(), P(), P()),
        out_specs=(rows, rows, P(("z", "yl"), None)),
        check_vma=False,
    )
```

time: 142 us -> 138 us (0.972)
  matrix products: 41.7 us -> 0 us
  waiting for transfers between devices: 30.3 us -> 54.9 us
  Pallas kernels: 0 us -> 22.2 us
  blocking collectives: 0 us -> 18.9 us
  other arithmetic: 12.2 us -> 0.08 us
  starting transfers between devices: 46.4 us -> 34.8 us
  local copies, waits for them, and re-layouts: 8.86 us -> 4.91 us
    ppermute x10 -> x11, waiting for transfers between devices: 8.83 us -> 54.9 us  [moved(): return lax.ppermute(value, AXES, pairs)]
    dot_general x14 -> x0, matrix products: 41.7 us -> none  [the longest x13 39.5 us: mm(): lax.dot_general(a, b, ((dims[:1], dims[1:]), ((), ())), preferred_element...]
    pallas_call x0 -> x13, Pallas kernels: none -> 22.2 us  [call(): pl.pallas_call(body, out_shape=[jax.ShapeDtypeStruct(shape, dtype) for sh...]
    all_to_all x3 -> x2, waiting for transfers between devices: 21.5 us -> 0.01 us  [the longest x1 0.01 us: on_device(): part = lax.all_to_all(part, ('yh', 'x'), 0, 0)]
    all_to_all x0 -> x1, blocking collectives: none -> 18.9 us  [on_device(): part = lax.all_to_all(part, ('z', 'yl'), 0, 0)]
    all_to_all x3 -> x2, starting transfers between devices: 23.4 us -> 15.3 us  [the longest x1 9.37 us: on_device(): part = lax.all_to_all(part, ('yh', 'x', 'core'), 0, 0)]
    reduce_sum x3 -> x0, other arithmetic: 4.3 us -> none  [the longest x2 2.89 us: on_device(): part = jnp.sum(part.astype(F32), 0).astype(BF)]
    ppermute x10 -> x11, starting transfers between devices: 22.9 us -> 19.5 us  [moved(): return lax.ppermute(value, AXES, pairs)]
  transfers between devices with their start and end apart: 13 -> 13, of which waited for: 6 -> 5; matrix products, arithmetic and copies ran while one was open for 30% -> 0% of each run, Pallas kernels for 0% -> 15%
where the time goes in v2:
time: 138 us
  waiting for transfers between devices  54.9 us (40%)
  starting transfers between devices  34.8 us (25%)
  Pallas kernels  22.2 us (16%)
  blocking collectives  18.9 us (14%)
  local copies, waits for them, and re-layouts  4.91 us (4%)
  between operations  2.1 us (2%)
    ppermute x11, waiting for transfers between devices, moved(): return lax.ppermute(value, AXES, pairs)  54.9 us
    pallas_call x13, Pallas kernels, call(): pl.pallas_call(body, out_shape=[jax.ShapeDtypeStruct(shape, dtype) for sh...  22.2 us
    ppermute x11, starting transfers between devices, moved(): return lax.ppermute(value, AXES, pairs)  19.5 us
    all_to_all x1, blocking collectives, on_device(): part = lax.all_to_all(part, ('z', 'yl'), 0, 0)  18.9 us
    all_to_all x1, starting transfers between devices, on_device(): part = lax.all_to_all(part, ('yh', 'x', 'core'), 0, 0)  9.37 us
    all_to_all x1, starting transfers between devices, on_device(): part = lax.all_to_all(part, ('yh', 'x'), 0, 0)  5.91 us
    unnamed x16, local copies, waits for them, and re-layouts  4.91 us
  transfers between devices with their start and end apart: 13, of which 5 were waited for; matrix products, arithmetic and copies ran while one was open for 0% of the time, Pallas kernels for 15%

profile of v2, /device:TPU:1, one launch (start us, length us, event | category | flops | bytes accessed | tf_op | source)
XLA Modules:
  0.0 137.8 jit_solution(17266586307783590540)
XLA Ops:
  1.9 2.1 %collective-permute-start = (bf16[256,1152]{1,0:T(8,128)(2,1)S(1)}, bf16[256,1152]{1,0:T(8,128)(2,1)S(1)}, u32[]{:S(2)}, u32[]{:S(2)}) collective-permute-start(bf16[256,1152]{1,0:T(8,128)(2,1)S(1)} %shard_map.76.txt_b.own), channel_id=1, source_target_pairs={{0,32},{1,33},{2,34},{3,35},{4,36},{5,37},{6,38},{7,39},{8,40},{9,... | collective-permute-start | bytes 1769480 | tf_op jit(solution)/shard_map/ppermute | solution.py:34
  4.0 14.9 %collective-permute-done.near = bf16[256,1152]{1,0:T(8,128)(2,1)S(1)} collective-permute-done((bf16[256,1152]{1,0:T(8,128)(2,1)S(1)}, bf16[256,1152]{1,0:T(8,128)(2,1)S(1)}, u32[]{:S(2)}, u32[]{:S(2)}) %collective-permute-start) | collective-permute-done | bytes 589856 | tf_op jit(solution)/shard_map/ppermute | solution.py:34
  18.9 1.7 %copy-done.1 = bf16[1152,1152]{1,0:T(8,128)(2,1)S(1)} copy-done((bf16[1152,1152]{1,0:T(8,128)(2,1)S(1)}, bf16[1152,1152]{1,0:T(8,128)(2,1)}, u32[]{:S(2)}) %copy-start.1) | copy-done | bytes 2654232
  20.7 1.3 shard_map.77
  22.0 3.4 %collective-permute-start.4 = (bf16[256,1152]{1,0:T(8,128)(2,1)S(1)}, bf16[256,1152]{1,0:T(8,128)(2,1)S(1)}, u32[]{:S(2)}, u32[]{:S(2)}) collective-permute-start(bf16[256,1152]{1,0:T(8,128)(2,1)S(1)} %get-tuple-element.13), channel_id=1, source_target_pairs={{0,16},{1,17},{2,18},{3,19},{4,20},{5,21},{6,22},{7,23},{8,24},{9,... | collective-permute-start | bytes 1769480 | tf_op jit(solution)/shard_map/ppermute | solution.py:34
  25.4 8.6 %collective-permute-done.1.near = bf16[256,1152]{1,0:T(8,128)(2,1)S(1)} collective-permute-done((bf16[256,1152]{1,0:T(8,128)(2,1)S(1)}, bf16[256,1152]{1,0:T(8,128)(2,1)S(1)}, u32[]{:S(2)}, u32[]{:S(2)}) %collective-permute-start.1) | collective-permute-done | bytes 589856 | tf_op jit(solution)/shard_map/ppermute | solution.py:34
  34.1 6.1 %collective-permute-start.2 = (bf16[256,1152]{1,0:T(8,128)(2,1)S(1)}, bf16[256,1152]{1,0:T(8,128)(2,1)S(1)}, u32[]{:S(2)}, u32[]{:S(2)}) collective-permute-start(bf16[256,1152]{1,0:T(8,128)(2,1)S(1)} %collective-permute-done.1.near), channel_id=1, source_target_pairs={{16,0},{17,1},{18,2},{19,3},{20,4},{21,5},{22,6},{23,7},{24,8},{25... | collective-permute-start | bytes 1769480 | tf_op jit(solution)/shard_map/ppermute | solution.py:34
  41.7 2.6 %shard_map.78 = (f32[256,1152]{1,0:T(8,128)S(1)}, f32[256,1152]{1,0:T(8,128)S(1)}) custom-call(f32[2]{0:T(128)S(1)} %pad_maximum_fusion.par, s32[1]{0:T(128)} %bitcast.core, bf16[256,1152]{1,0:T(8,128)(2,1)S(1)} %get-tuple-element.12.img_b.own, bf16[256,1152]{1,0:T(8,128)(2,1)S(1)} %shard_map.76.txt_b.own, bf16[256,1152]{1,0:T(8,128)(2,1)S(1)} %collective-permute-done.4.r1), custom_call_target="tpu_custom_call" | custom-call | flops 906000000 | bytes 1769472 | tf_op jit(solution)/shard_map/pallas_call | solution.py:44
  45.3 2.0 %shard_map.79.old = f32[256,1152]{1,0:T(8,128)S(1)} custom-call(f32[2]{0:T(128)S(1)} %pad_maximum_fusion.par, bf16[256,1152]{1,0:T(8,128)(2,1)S(1)} %get-tuple-element.12.img_b.own, bf16[256,1152]{1,0:T(8,128)(2,1)S(1)} %collective-permute-done.near, bf16[256,1152]{1,0:T(8,128)(2,1)S(1)} %collective-permute-done.3.nears, f32[256,1152]{1,0:T(8,128)S(1)} %get-tuple-element.14.old), custom_call_target="tpu_custom_call" | custom-call | flops 604000000 | bytes 2949120 | tf_op jit(solution)/shard_map/pallas_call | solution.py:44
  47.3 1.5 %shard_map.80.old = f32[256,1152]{1,0:T(8,128)S(1)} custom-call(f32[2]{0:T(128)S(1)} %pad_maximum_fusion.par, bf16[256,1152]{1,0:T(8,128)(2,1)S(1)} %get-tuple-element.12.img_b.own, bf16[256,1152]{1,0:T(8,128)(2,1)S(1)} %collective-permute-done.1.near, f32[256,1152]{1,0:T(8,128)S(1)} %shard_map.79.old), custom_call_target="tpu_custom_call" | custom-call | flops 302000000 | bytes 2359296 | tf_op jit(solution)/shard_map/pallas_call | solution.py:44
  48.8 2.2 %shard_map.81 = (bf16[256,1152]{1,0:T(8,128)(2,1)S(1)}, bf16[256,576]{1,0:T(8,128)(2,1)S(1)}, bf16[256,576]{1,0:T(8,128)(2,1)S(1)}, f32[256,1152]{1,0:T(8,128)}) custom-call(f32[2]{0:T(128)S(1)} %pad_maximum_fusion.par, s32[1]{0:T(128)} %bitcast.core, bf16[256,1152]{1,0:T(8,128)(2,1)S(1)} %get-tuple-element.12.img_b.own, ...), custom_call_target="tpu_custom_call" | custom-call | flops 604000000 | bytes 3539968 | tf_op jit(solution)/shard_map/pallas_call | solution.py:44
  51.1 1.4 %collective-permute-start.9 = (bf16[256,576]{1,0:T(8,128)(2,1)S(1)}, bf16[256,576]{1,0:T(8,128)(2,1)S(1)}, u32[]{:S(2)}, u32[]{:S(2)}) collective-permute-start(bf16[256,576]{1,0:T(8,128)(2,1)S(1)} %get-tuple-element.20), channel_id=1, source_target_pairs={{0,16},{1,17},{2,18},{3,19},{4,20},{5,21},{6,22},{7,23},{8,24},{9,... | collective-permute-start | bytes 884744 | tf_op jit(solution)/shard_map/ppermute | solution.py:34
  52.5 1.2 collective-permute-done.9.other
  55.8 5.9 %all-to-all-start = ((bf16[8,72,1152]{2,1,0:T(8,128)(2,1)}), bf16[8,72,1152]{2,1,0:T(8,128)(2,1)S(1)}, u32[]{:S(2)}, u32[]{:S(2)}) async-start(bf16[8,72,1152]{2,1,0:T(8,128)(2,1)} %copy-done), calls=%async_computation | async-start | bytes 2654208 | tf_op jit(solution)/shard_map/all_to_all | solution.py:233
  61.7 5.9 %collective-permute-done.5.near = bf16[256,1152]{1,0:T(8,128)(2,1)} collective-permute-done((bf16[256,1152]{1,0:T(8,128)(2,1)S(1)}, bf16[256,1152]{1,0:T(8,128)(2,1)}, u32[]{:S(2)}, u32[]{:S(2)}) %collective-permute-start.5) | collective-permute-done | bytes 589856 | tf_op jit(solution)/shard_map/ppermute | solution.py:34
  67.5 3.8 %collective-permute-start.6 = (bf16[256,1152]{1,0:T(8,128)(2,1)}, bf16[256,1152]{1,0:T(8,128)(2,1)}, u32[]{:S(2)}, u32[]{:S(2)}) collective-permute-start(bf16[256,1152]{1,0:T(8,128)(2,1)} %collective-permute-done.5.near), channel_id=1, source_target_pairs={{0,224},{1,225},{2,226},{3,227},{4,228},{5,229},{6,230},{7,231},{8... | collective-permute-start | bytes 1769480 | tf_op jit(solution)/shard_map/ppermute | solution.py:34
  71.3 1.1 collective-permute-start.8
  72.5 24.3 %collective-permute-done.6.i2 = bf16[256,1152]{1,0:T(8,128)(2,1)} collective-permute-done((bf16[256,1152]{1,0:T(8,128)(2,1)}, bf16[256,1152]{1,0:T(8,128)(2,1)}, u32[]{:S(2)}, u32[]{:S(2)}) %collective-permute-start.6) | collective-permute-done | bytes 589856 | tf_op jit(solution)/shard_map/ppermute | solution.py:34
  96.7 1.3 collective-permute-start.7
  98.3 18.9 %all_to_all.15.parts = bf16[16,72,72]{2,1,0:T(8,128)(2,1)S(1)} all-to-all(bf16[16,72,72]{2,1,0:T(8,128)(2,1)S(1)} %shard_map.86), channel_id=1, replica_groups=mesh['yh'=2,'x'=4,'core'=2,'z'=8,'yl'=2] {'z','yl'}, dimensions={0} | all-to-all | bytes 331776 | tf_op jit(solution)/shard_map/all_to_all | solution.py:240
  118.0 9.4 %all-to-all-start.2 = ((bf16[16,72,72]{2,1,0:T(8,128)(2,1)}), bf16[16,72,72]{2,1,0:T(8,128)(2,1)S(1)}, u32[]{:S(2)}, u32[]{:S(2)}) async-start(bf16[16,72,72]{2,1,0:T(8,128)(2,1)} %shard_map.87), calls=%async_computation.2 | async-start | bytes 589824 | tf_op jit(solution)/shard_map/all_to_all | solution.py:242
  127.4 2.8 %shard_map.83.old = f32[256,1152]{1,0:T(8,128)S(1)} custom-call(f32[2]{0:T(128)S(1)} %pad_maximum_fusion.par, bf16[256,1152]{1,0:T(8,128)(2,1)S(1)} %shard_map.76.txt_b.own, bf16[256,1152]{1,0:T(8,128)(2,1)} %collective-permute-done.5.near, bf16[256,1152]{1,0:T(8,128)(2,1)} %collective-permute-done.8.nears, f32[256,1152]{1,0:T(8,128)S(1)} %copy-done.6), custom_call_target="tpu_custom_call" | custom-call | flops 604000000 | bytes 2949120 | tf_op jit(solution)/shard_map/pallas_call | solution.py:44
  130.2 2.1 %shard_map.82 = f32[256,1152]{1,0:T(8,128)} custom-call(bf16[256,1152]{1,0:T(8,128)(2,1)S(1)} %get-tuple-element.17.dproj, bf16[1152,1152]{1,0:T(8,128)(2,1)S(1)} %copy-done.2), custom_call_target="tpu_custom_call" | custom-call | flops 604000000 | bytes 3244032 | tf_op jit(solution)/shard_map/pallas_call | solution.py:44
  132.3 4.6 %shard_map.84 = f32[256,1152]{1,0:T(8,128)} custom-call(f32[2]{0:T(128)S(1)} %pad_maximum_fusion.par, s32[1]{0:T(128)} %bitcast.core, bf16[256,1152]{1,0:T(8,128)(2,1)S(1)} %shard_map.76.txt_b.own, bf16[256,1152]{1,0:T(8,128)(2,1)} %collective-permute-done.6.i2, bf16[256,1152]{1,0:T(8,128)(2,1)} %collective-permute-done.7.r3, ...), custom_call_target="tpu_custom_call" | custom-call | flops 906000000 | bytes 3538944 | tf_op jit(solution)/shard_map/pallas_call | solution.py:44
  (33 shorter events, 6.6 us)
Async XLA Ops:
  0.6 1.1 copy-start.3
  1.7 17.2 %copy-start.7 = (bf16[256,1152]{1,0:T(8,128)(2,1)S(1)}, bf16[256,1152]{1,0:T(8,128)(2,1)}, u32[]{:S(2)}) copy-start(bf16[256,1152]{1,0:T(8,128)(2,1)} %images.3) | copy-start | bytes 1769476
  1.9 17.0 %collective-permute-start = (bf16[256,1152]{1,0:T(8,128)(2,1)S(1)}, bf16[256,1152]{1,0:T(8,128)(2,1)S(1)}, u32[]{:S(2)}, u32[]{:S(2)}) collective-permute-start(bf16[256,1152]{1,0:T(8,128)(2,1)S(1)} %shard_map.76.txt_b.own), channel_id=1, source_target_pairs={{0,32},{1,33},{2,34},{3,35},{4,36},{5,37},{6,38},{7,39},{8,40},{9,... | collective-permute-start | bytes 1769480 | tf_op jit(solution)/shard_map/ppermute | solution.py:34
  18.9 15.1 %collective-permute-start.1 = (bf16[256,1152]{1,0:T(8,128)(2,1)S(1)}, bf16[256,1152]{1,0:T(8,128)(2,1)S(1)}, u32[]{:S(2)}, u32[]{:S(2)}) collective-permute-start(bf16[256,1152]{1,0:T(8,128)(2,1)S(1)} %collective-permute-done.near), channel_id=1, source_target_pairs={{0,32},{1,33},{2,34},{3,35},{4,36},{5,37},{6,38},{7,39},{8,40},{9,... | collective-permute-start | bytes 1769480 | tf_op jit(solution)/shard_map/ppermute | solution.py:34
  18.9 1.8 %copy-start.1 = (bf16[1152,1152]{1,0:T(8,128)(2,1)S(1)}, bf16[1152,1152]{1,0:T(8,128)(2,1)}, u32[]{:S(2)}) copy-start(bf16[1152,1152]{1,0:T(8,128)(2,1)} %head.3) | copy-start | bytes 7962628
  22.0 19.7 %collective-permute-start.4 = (bf16[256,1152]{1,0:T(8,128)(2,1)S(1)}, bf16[256,1152]{1,0:T(8,128)(2,1)S(1)}, u32[]{:S(2)}, u32[]{:S(2)}) collective-permute-start(bf16[256,1152]{1,0:T(8,128)(2,1)S(1)} %get-tuple-element.13), channel_id=1, source_target_pairs={{0,16},{1,17},{2,18},{3,19},{4,20},{5,21},{6,22},{7,23},{8,24},{9,... | collective-permute-start | bytes 1769480 | tf_op jit(solution)/shard_map/ppermute | solution.py:34
  25.3 20.0 %collective-permute-start.3 = (bf16[256,1152]{1,0:T(8,128)(2,1)S(1)}, bf16[256,1152]{1,0:T(8,128)(2,1)S(1)}, u32[]{:S(2)}, u32[]{:S(2)}) collective-permute-start(bf16[256,1152]{1,0:T(8,128)(2,1)S(1)} %collective-permute-done.near), channel_id=1, source_target_pairs={{0,16},{1,17},{2,18},{3,19},{4,20},{5,21},{6,22},{7,23},{8,24},{9,... | collective-permute-start | bytes 1769480 | tf_op jit(solution)/shard_map/ppermute | solution.py:34
  34.1 14.7 %collective-permute-start.2 = (bf16[256,1152]{1,0:T(8,128)(2,1)S(1)}, bf16[256,1152]{1,0:T(8,128)(2,1)S(1)}, u32[]{:S(2)}, u32[]{:S(2)}) collective-permute-start(bf16[256,1152]{1,0:T(8,128)(2,1)S(1)} %collective-permute-done.1.near), channel_id=1, source_target_pairs={{16,0},{17,1},{18,2},{19,3},{20,4},{21,5},{22,6},{23,7},{24,8},{25... | collective-permute-start | bytes 1769480 | tf_op jit(solution)/shard_map/ppermute | solution.py:34
  40.2 12.2 %collective-permute-start.10 = (bf16[256,1152]{1,0:T(8,128)(2,1)S(1)}, bf16[256,1152]{1,0:T(8,128)(2,1)S(1)}, u32[]{:S(2)}, u32[]{:S(2)}) collective-permute-start(bf16[256,1152]{1,0:T(8,128)(2,1)S(1)} %copy-done.7), channel_id=1, source_target_pairs={{0,16},{1,17},{2,18},{3,19},{4,20},{5,21},{6,22},{7,23},{8,24},{9,... | collective-permute-start | bytes 1769480 | tf_op jit(solution)/shard_map/ppermute | solution.py:34
  44.3 1.0 copy-start.5
  51.1 2.7 %collective-permute-start.9 = (bf16[256,576]{1,0:T(8,128)(2,1)S(1)}, bf16[256,576]{1,0:T(8,128)(2,1)S(1)}, u32[]{:S(2)}, u32[]{:S(2)}) collective-permute-start(bf16[256,576]{1,0:T(8,128)(2,1)S(1)} %get-tuple-element.20), channel_id=1, source_target_pairs={{0,16},{1,17},{2,18},{3,19},{4,20},{5,21},{6,22},{7,23},{8,24},{9,... | collective-permute-start | bytes 884744 | tf_op jit(solution)/shard_map/ppermute | solution.py:34
  52.5 15.1 %collective-permute-start.5 = (bf16[256,1152]{1,0:T(8,128)(2,1)S(1)}, bf16[256,1152]{1,0:T(8,128)(2,1)}, u32[]{:S(2)}, u32[]{:S(2)}) collective-permute-start(bf16[256,1152]{1,0:T(8,128)(2,1)S(1)} %get-tuple-element.12.img_b.own), channel_id=1, source_target_pairs={{0,224},{1,225},{2,226},{3,227},{4,228},{5,229},{6,230},{7,231},{8... | collective-permute-start | bytes 1769480 | tf_op jit(solution)/shard_map/ppermute | solution.py:34
  54.7 1.1 copy-start
  55.8 42.3 %all-to-all-start = ((bf16[8,72,1152]{2,1,0:T(8,128)(2,1)}), bf16[8,72,1152]{2,1,0:T(8,128)(2,1)S(1)}, u32[]{:S(2)}, u32[]{:S(2)}) async-start(bf16[8,72,1152]{2,1,0:T(8,128)(2,1)} %copy-done), calls=%async_computation | async-start | bytes 2654208 | tf_op jit(solution)/shard_map/all_to_all | solution.py:233
  67.5 29.2 %collective-permute-start.6 = (bf16[256,1152]{1,0:T(8,128)(2,1)}, bf16[256,1152]{1,0:T(8,128)(2,1)}, u32[]{:S(2)}, u32[]{:S(2)}) collective-permute-start(bf16[256,1152]{1,0:T(8,128)(2,1)} %collective-permute-done.5.near), channel_id=1, source_target_pairs={{0,224},{1,225},{2,226},{3,227},{4,228},{5,229},{6,230},{7,231},{8... | collective-permute-start | bytes 1769480 | tf_op jit(solution)/shard_map/ppermute | solution.py:34
  71.3 56.0 %collective-permute-start.8 = (bf16[256,1152]{1,0:T(8,128)(2,1)}, bf16[256,1152]{1,0:T(8,128)(2,1)}, u32[]{:S(2)}, u32[]{:S(2)}) collective-permute-start(bf16[256,1152]{1,0:T(8,128)(2,1)} %collective-permute-done.5.near), channel_id=1, source_target_pairs={{0,16},{1,17},{2,18},{3,19},{4,20},{5,21},{6,22},{7,23},{8,24},{9,... | collective-permute-start | bytes 1769480 | tf_op jit(solution)/shard_map/ppermute | solution.py:34
  96.7 35.6 %collective-permute-start.7 = (bf16[256,1152]{1,0:T(8,128)(2,1)}, bf16[256,1152]{1,0:T(8,128)(2,1)}, u32[]{:S(2)}, u32[]{:S(2)}) collective-permute-start(bf16[256,1152]{1,0:T(8,128)(2,1)} %collective-permute-done.6.i2), channel_id=1, source_target_pairs={{0,16},{1,17},{2,18},{3,19},{4,20},{5,21},{6,22},{7,23},{8,24},{9,... | collective-permute-start | bytes 1769480 | tf_op jit(solution)/shard_map/ppermute | solution.py:34
  98.3 29.0 %copy-start.6 = (f32[256,1152]{1,0:T(8,128)S(1)}, f32[256,1152]{1,0:T(8,128)}, u32[]{:S(2)}) copy-start(f32[256,1152]{1,0:T(8,128)} %copy-done.5) | copy-start | bytes 3538948
  118.0 18.9 %all-to-all-start.2 = ((bf16[16,72,72]{2,1,0:T(8,128)(2,1)}), bf16[16,72,72]{2,1,0:T(8,128)(2,1)S(1)}, u32[]{:S(2)}, u32[]{:S(2)}) async-start(bf16[16,72,72]{2,1,0:T(8,128)(2,1)} %shard_map.87), calls=%async_computation.2 | async-start | bytes 589824 | tf_op jit(solution)/shard_map/all_to_all | solution.py:242
  127.4 2.9 %copy-start.2 = (bf16[1152,1152]{1,0:T(8,128)(2,1)S(1)}, bf16[1152,1152]{1,0:T(8,128)(2,1)}, u32[]{:S(2)}) copy-start(bf16[1152,1152]{1,0:T(8,128)(2,1)} %head.3) | copy-start | bytes 7962628
  130.2 2.1 %copy-start.4 = (bf16[256,1152]{1,0:T(8,128)(2,1)S(1)}, bf16[256,1152]{1,0:T(8,128)(2,1)}, u32[]{:S(2)}) copy-start(bf16[256,1152]{1,0:T(8,128)(2,1)} %texts.3) | copy-start | bytes 1769476

commit v3 on v2

v3 whole, which is shorter than its diff:
```python
import functools

import jax
import jax.numpy as jnp
import numpy as np
from jax import lax
from jax.experimental import pallas as pl
from jax.experimental.pallas import tpu as pltpu
from jax.sharding import Mesh, PartitionSpec as P

AXES = ("yh", "x", "core", "z", "yl")
SIZES = (2, 4, 2, 8, 2)
INNER = SIZES[3] * SIZES[4]
COUNT = 16 * INNER
CHIPS = SIZES[0] * SIZES[1]
BLKS = CHIPS * SIZES[2]
BF = jnp.bfloat16
F32 = jnp.float32


def chip_pairs(steps):
    shift = steps * SIZES[2] * INNER
    return [(source, (source + shift) % COUNT) for source in range(COUNT)]


def core_pairs(only=None):
    return [
        (source, source ^ INNER)
        for source in range(COUNT)
        if only is None or (source // INNER) % 2 == only
    ]


def moved(value, pairs):
    return lax.ppermute(value, AXES, pairs)


def mm(a, b, dims):
    return lax.dot_general(a, b, ((dims[:1], dims[1:]), ((), ())), preferred_element_type=F32)


def call(body, outs, *args, scalars=(), pairs=0.0, scratch=(), space=pltpu.VMEM):
    in_specs = [pl.BlockSpec(memory_space=pltpu.SMEM)] * len(scalars)
    in_specs += [pl.BlockSpec(memory_space=space)] * len(args)
    return pl.pallas_call(
        body,
        out_shape=[jax.ShapeDtypeStruct(shape, dtype) for shape, dtype in outs],
        in_specs=in_specs,
        out_specs=[pl.BlockSpec(memory_space=pltpu.VMEM)] * len(outs),
        scratch_shapes=list(scratch),
        cost_estimate=pl.CostEstimate(
            flops=int(pairs * 3.02e8),
            bytes_accessed=sum(int(a.size) * a.dtype.itemsize for a in args),
            transcendentals=0,
        ),
        compiler_params=pltpu.CompilerParams(vmem_limit_bytes=32 * 2**20),
    )(*scalars, *args)


def sigmoid(x):
    return 1.0 / (1.0 + jnp.exp(-x))


def applied(par, rows, cols):
    logit = par[0] * mm(rows, cols, (1, 1)) + par[1]
    return mm(sigmoid(logit).astype(BF), cols, (1, 0))


def text_unit(texts):
    tfloat = texts.astype(F32)
    tnorm = jnp.sqrt(jnp.sum(tfloat * tfloat, -1, keepdims=True) + 1e-06)
    inverse = 1.0 / tnorm
    return tfloat * inverse, inverse


CUTS = (0, 256, 512, 768, 1152)


def start_body(core, images, texts, head, txt_b, unit, norm, img_b, mixed, t_in, i_in, h_in, sems):
    copies = [
        pltpu.make_async_copy(texts, t_in, sems.at[0]),
        pltpu.make_async_copy(images, i_in, sems.at[1]),
    ]
    for k in range(len(CUTS) - 1):
        rows = pl.ds(CUTS[k], CUTS[k + 1] - CUTS[k])
        copies.append(pltpu.make_async_copy(head.at[rows], h_in.at[rows], sems.at[2 + k]))
    for copy in copies:
        copy.start()
    copies[0].wait()
    low_txt = text_unit(t_in[...])[0].astype(BF)
    txt_b[...] = low_txt
    copies[1].wait()
    proj = None
    for k in range(len(CUTS) - 1):
        copies[2 + k].wait()
        cut = slice(CUTS[k], CUTS[k + 1])
        term = jnp.dot(i_in[:, cut], h_in[cut, :], preferred_element_type=F32)
        proj = term if proj is None else proj + term
    pnorm = jnp.sqrt(jnp.sum(proj * proj, -1, keepdims=True) + 1e-06)
    inverse = 1.0 / pnorm
    value = proj * inverse
    unit[...] = value
    norm[...] = inverse
    low = value.astype(BF)
    img_b[...] = low

    @pl.when(core[0] == 0)
    def _():
        mixed[...] = low_txt

    @pl.when(core[0] != 0)
    def _():
        mixed[...] = low


def order_body(images, out):
    own = images.shape[1] // INNER
    for z in range(SIZES[3]):
        for yl in range(SIZES[4]):
            source, target = (z * SIZES[4] + yl) * own, (yl * SIZES[3] + z) * own
            out[:, target : target + own] = images[:, source : source + own]


def home_body(par, core, img_b, txt_b, r1, dimg, dtxt):
    logit = par[0] * mm(img_b[...], txt_b[...], (1, 1)) + par[1]
    eye = lax.broadcasted_iota(jnp.int32, logit.shape, 0) == lax.broadcasted_iota(
        jnp.int32, logit.shape, 1
    )
    away = sigmoid(logit)
    grad = jnp.where(eye, -sigmoid(-logit), away).astype(BF)
    dimg[...] = mm(grad, txt_b[...], (1, 0))
    dtxt[...] = mm(grad, img_b[...], (0, 0))

    @pl.when(core[0] == 0)
    def _():
        dtxt[...] += applied(par, txt_b[...], r1[...])

    @pl.when(core[0] != 0)
    def _():
        dimg[...] += applied(par, img_b[...], r1[...])


def near_body(par, img_b, txt_b, t1, t1s, i1, i1s, dimg, dtxt, dimg_out, dtxt_out):
    dimg_out[...] = dimg[...] + applied(par, img_b[...], t1[...]) + applied(par, img_b[...], t1s[...])
    dtxt_out[...] = dtxt[...] + applied(par, txt_b[...], i1[...]) + applied(par, txt_b[...], i1s[...])


def one_body(par, own, near, old, new):
    new[...] = old[...] + applied(par, own[...], near[...])


def image_end_body(par, core, img_b, r3, old, unit, norm, whole, keep, send, total):
    total[...] = old[...]

    @pl.when(core[0] == 0)
    def _():
        total[...] += applied(par, img_b[...], r3[...])

    dimg = par[0] * total[...]
    value = unit[...]
    dproj = ((dimg - value * jnp.sum(value * dimg, -1, keepdims=True)) * norm[...]).astype(BF)
    whole[...] = dproj
    half = dproj.shape[1] // 2

    @pl.when(core[0] == 0)
    def _():
        keep[...] = dproj[:, :half]
        send[...] = dproj[:, half:]

    @pl.when(core[0] != 0)
    def _():
        keep[...] = dproj[:, half:]
        send[...] = dproj[:, :half]


TURNS = (0, 1, 3, 2)


def turned(place, pieces, outs):
    for turn, out in zip(TURNS, outs):
        out[...] = pieces[lax.rem(place[0] + turn, 4)]


def head_body(core, place, keep, other, images, images2, *rest):
    outs, pieces = rest[:4], rest[4]
    total = mm(keep[...], images[...], (0, 0)) + mm(other[...], images2[...], (0, 0))
    rows, half = pieces.shape[1], total.shape[1] // 2

    @pl.when(core[0] == 0)
    def _():
        for k in range(4):
            pieces[k] = total[k * rows : (k + 1) * rows].astype(BF)

    @pl.when(core[0] != 0)
    def _():
        for k in range(4):
            up, left = 2 * (k // 2) * rows, (k % 2) * half
            first = total[up : up + rows, left : left + half]
            second = total[up + rows : up + 2 * rows, left : left + half]
            pieces[k] = jnp.concatenate([first, second], 1).astype(BF)

    turned(place, pieces, outs)


def quarter_body(core, place, a, b, c, d, *rest):
    outs, pieces = rest[:4], rest[4]
    total = a[...].astype(F32) + b[...].astype(F32) + c[...].astype(F32) + d[...].astype(F32)
    _, rows, half = pieces.shape

    def quadrant(down, right):
        return total[down * rows : (down + 1) * rows, right * half : (right + 1) * half].astype(BF)

    @pl.when(core[0] == 0)
    def _():
        for k in range(4):
            pieces[k] = quadrant(k // 2, k % 2)

    @pl.when(core[0] != 0)
    def _():
        for k in range(4):
            pieces[k] = quadrant(k % 2, k // 2)

    turned(place, pieces, outs)


def text_end_body(par, core, txt_b, i2, r3, old, texts, out):
    out[...] = old[...] + applied(par, txt_b[...], i2[...])

    @pl.when(core[0] != 0)
    def _():
        out[...] += applied(par, txt_b[...], r3[...])

    dtxt = par[0] * out[...]
    value, inverse = text_unit(texts[...])
    out[...] = (dtxt - value * jnp.sum(value * dtxt, -1, keepdims=True)) * inverse


def grad_image_body(dproj, head, out):
    out[...] = mm(dproj[...], head[...], (1, 1))


def split_body(a, b, c, d, out):
    total = a[...].astype(F32) + b[...].astype(F32) + c[...].astype(F32) + d[...].astype(F32)
    own = out.shape[2]
    for k in range(out.shape[0]):
        out[k] = total[:, k * own : (k + 1) * own].astype(BF)


def spread_body(parts, out):
    total = parts[0].astype(F32)
    for k in range(1, parts.shape[0]):
        total = total + parts[k].astype(F32)
    total = total.astype(BF)
    for k in range(out.shape[0]):
        out[k] = total


def join_body(factor, parts, out):
    yhs, xs, cores = SIZES[:3]
    order = [(yh * xs + x) * cores for x in range(xs) for yh in range(yhs)]
    order += [(yh * xs + x) * cores + 1 for yh in range(yhs) for x in range(xs)]
    out[...] = jnp.concatenate([parts[k].astype(F32) for k in order], 0).T * factor


def ring_pairs(turn, first):
    pairs = []
    for source in range(COUNT):
        yh, x, core, z, yl = np.unravel_index(source, SIZES)
        if core == first:
            x = (x + turn) % SIZES[1]
        else:
            y = (yh * SIZES[4] + yl + turn) % 4
            yh, yl = y // SIZES[4], y % SIZES[4]
        pairs.append((source, int(np.ravel_multi_index((yh, x, core, z, yl), SIZES))))
    return pairs


def on_device(images, texts, head, scale, bias):
    par = jnp.concatenate([scale, bias])
    core = lax.axis_index("core").astype(jnp.int32).reshape(1)
    across = lax.axis_index("x").astype(jnp.int32).reshape(1)
    along = lax.axis_index(("yh", "yl")).astype(jnp.int32).reshape(1)
    place_a = jnp.where(core == 0, across, along)
    place_b = jnp.where(core == 0, along, across)
    ahead, back, swap = chip_pairs(1), chip_pairs(-1), core_pairs()
    count, width = images.shape
    half = width // 2
    big = (count, width)
    tie = lax.optimization_barrier

    txt_b, unit_img, pnorm, img_b, mixed = call(
        start_body,
        [(big, BF), (big, F32), ((count, 1), F32), (big, BF), (big, BF)],
        images, texts, head, scalars=(core,), pairs=6, space=pltpu.HBM,
        scratch=[
            pltpu.VMEM(big, BF), pltpu.VMEM(big, BF), pltpu.VMEM(head.shape, BF),
            pltpu.SemaphoreType.DMA((1 + len(CUTS),)),
        ],
    )
    t1 = moved(txt_b, ahead)
    i1 = moved(img_b, back)
    r1 = moved(mixed, swap)
    dimg, dtxt = call(home_body, [(big, F32)] * 2, img_b, txt_b, r1, scalars=(par, core), pairs=6)
    (ordered,) = call(order_body, [(big, BF)], images, pairs=2)

    t2 = moved(t1, ahead)
    i2 = moved(i1, back)
    t1x, i1x, dimg, dtxt, ordered = tie((t1, i1, dimg, dtxt, ordered))
    t1s = moved(t1x, swap)
    i1s = moved(i1x, swap)
    ordered2 = moved(ordered, swap)
    dimg, dtxt = call(
        near_body, [(big, F32)] * 2, img_b, txt_b, t1x, t1s, i1x, i1s, dimg, dtxt,
        scalars=(par,), pairs=8,
    )
    t2, dimg, dtxt, ordered2 = tie((t2, dimg, dtxt, ordered2))

    r3t = moved(t2, core_pairs(1))
    (dimg,) = call(one_body, [(big, F32)], img_b, t2, dimg, scalars=(par,), pairs=3)
    dproj, keep, send = call(
        image_end_body,
        [(big, BF), ((count, half), BF), ((count, half), BF), (big, F32)],
        img_b, r3t, dimg, unit_img, pnorm, scalars=(par, core), pairs=6,
    )[:3]
    other = moved(send, swap)
    quarter = ((half // 4, width), BF)
    parts = call(
        head_body, [quarter] * 4, keep, other, ordered, ordered2, scalars=(core, place_a), pairs=3,
        scratch=[pltpu.VMEM((4, half // 4, width), BF)],
    )
    parts = list(parts[:1]) + [moved(p, ring_pairs(t, 0)) for p, t in zip(parts[1:], TURNS[1:])]
    (grad_image,) = call(grad_image_body, [(big, F32)], dproj, head, pairs=6)
    i2 = tie((i2, keep))[0]
    r3i = moved(i2, core_pairs(0))
    small = ((half // 8, half), BF)
    parts = call(
        quarter_body, [small] * 4, *parts, scalars=(core, place_b), pairs=1,
        scratch=[pltpu.VMEM((4, half // 8, half), BF)],
    )
    parts = list(parts[:1]) + [moved(p, ring_pairs(t, 1)) for p, t in zip(parts[1:], TURNS[1:])]
    (grad_text,) = call(
        text_end_body, [(big, F32)], txt_b, i2, r3i, dtxt, texts, scalars=(par, core), pairs=8
    )
    own = width // INNER
    (part,) = call(split_body, [((SIZES[3], half // 8, own), BF)], *parts)
    part = lax.all_to_all(part, "z", 0, 0)
    (part,) = call(spread_body, [((BLKS, half // 8, own), BF)], part)
    part = lax.all_to_all(part, ("yh", "x", "core"), 0, 0)
    factor = 1.0 / float(count * COUNT) ** 0.5
    (head_grad,) = call(functools.partial(join_body, factor), [((own, width), F32)], part)
    return (grad_image, grad_text, head_grad)


def solution(mesh):
    fine = Mesh(mesh.devices.reshape(SIZES), AXES)
    rows = P(AXES, None)
    return jax.shard_map(
        on_device,
        mesh=fine,
        in_specs=(rows, rows, P(), P(), P()),
        out_specs=(rows, rows, P(("z", "yl"), None)),
        check_vma=False,
    )
```

time: 138 us -> 126 us (0.913)
  blocking collectives: 18.9 us -> 0 us
  local copies, waits for them, and re-layouts: 4.91 us -> 14.6 us
  waiting for transfers between devices: 54.9 us -> 48.2 us
  Pallas kernels: 22.2 us -> 23.8 us
    all_to_all x1 -> x0, blocking collectives: 18.9 us -> none  [on_device(): part = lax.all_to_all(part, ('z', 'yl'), 0, 0)]
    ppermute x11 -> x17, waiting for transfers between devices: 54.9 us -> 41.2 us  [moved(): return lax.ppermute(value, AXES, pairs)]
    unnamed x16 -> x40, local copies, waits for them, and re-layouts: 4.91 us -> 14.6 us
    all_to_all x1, waiting for transfers between devices: 0.01 us -> 5.05 us  [on_device(): part = lax.all_to_all(part, 'z', 0, 0)]
    all_to_all x1, starting transfers between devices: 5.91 us -> 8.19 us  [on_device(): part = lax.all_to_all(part, 'z', 0, 0)]
    all_to_all x1, waiting for transfers between devices: 0.01 us -> 1.96 us  [on_device(): part = lax.all_to_all(part, ('yh', 'x', 'core'), 0, 0)]
    pallas_call x13, Pallas kernels: 22.2 us -> 23.8 us  [call(): pl.pallas_call(body, out_shape=[jax.ShapeDtypeStruct(shape, dtype) for sh...]
    ppermute x11 -> x17, starting transfers between devices: 19.5 us -> 19.3 us  [moved(): return lax.ppermute(value, AXES, pairs)]
  transfers between devices with their start and end apart: 13 -> 19, of which waited for: 5 -> 12; matrix products, arithmetic and copies ran while one was open for 0% -> 0% of each run, Pallas kernels for 15% -> 16%
where the time goes in v3:
time: 126 us; the launch traced here: 125 us
  waiting for transfers between devices  48.2 us (38%)
  starting transfers between devices  36.1 us (29%)
  Pallas kernels  23.8 us (19%)
  local copies, waits for them, and re-layouts  14.6 us (12%)
  between operations  2.13 us (2%)
    ppermute x17, waiting for transfers between devices, moved(): return lax.ppermute(value, AXES, pairs)  41.2 us
    pallas_call x13, Pallas kernels, call(): pl.pallas_call(body, out_shape=[jax.ShapeDtypeStruct(shape, dtype) for sh...  23.8 us
    ppermute x17, starting transfers between devices, moved(): return lax.ppermute(value, AXES, pairs)  19.3 us
    unnamed x40, local copies, waits for them, and re-layouts  14.6 us
    all_to_all x1, starting transfers between devices, on_device(): part = lax.all_to_all(part, ('yh', 'x', 'core'), 0, 0)  8.66 us
    all_to_all x1, starting transfers between devices, on_device(): part = lax.all_to_all(part, 'z', 0, 0)  8.19 us
    all_to_all x1, waiting for transfers between devices, on_device(): part = lax.all_to_all(part, 'z', 0, 0)  5.05 us
  transfers between devices with their start and end apart: 19, of which 12 were waited for; matrix products, arithmetic and copies ran while one was open for 0% of the time, Pallas kernels for 16%

profile of v3, /device:TPU:1, one launch (start us, length us, event | category | flops | bytes accessed | tf_op | source)
XLA Modules:
  0.0 125.0 jit_solution(3204358691018937137)
XLA Ops:
  0.6 1.7 %copy-done = bf16[1152,1152]{1,0:T(8,128)(2,1)S(1)} copy-done((bf16[1152,1152]{1,0:T(8,128)(2,1)S(1)}, bf16[1152,1152]{1,0:T(8,128)(2,1)}, u32[]{:S(2)}) %copy-start) | copy-done | bytes 2654232
  4.5 2.7 %shard_map.76 = (bf16[256,1152]{1,0:T(8,128)(2,1)S(1)}, f32[256,1152]{1,0:T(8,128)S(1)}, f32[256,1]{1,0:T(8,128)S(1)}, bf16[256,1152]{1,0:T(8,128)(2,1)S(1)}, bf16[256,1152]{1,0:T(8,128)(2,1)S(1)}) custom-call(s32[1]{0:T(128)} %bitcast.core, bf16[256,1152]{1,0:T(8,128)(2,1)S(1)} %copy-done.2, bf16[256,1152]{1,0:T(8,128)(2,1)S(1)} %copy-done.4, ...), custom_call_target="tpu_custom_call" | custom-call | flops 1812000000 | bytes 3833856 | tf_op jit(solution)/shard_map/pallas_call | solution.py:45
  7.3 3.3 %collective-permute-start.3 = (bf16[256,1152]{1,0:T(8,128)(2,1)S(1)}, bf16[256,1152]{1,0:T(8,128)(2,1)S(1)}, u32[]{:S(2)}, u32[]{:S(2)}) collective-permute-start(bf16[256,1152]{1,0:T(8,128)(2,1)S(1)} %get-tuple-element.35), channel_id=1, source_target_pairs={{0,16},{1,17},{2,18},{3,19},{4,20},{5,21},{6,22},{7,23},{8,24},{9,... | collective-permute-start | bytes 1769480 | tf_op jit(solution)/shard_map/ppermute | solution.py:35
  10.6 3.4 %collective-permute-start.2 = (bf16[256,1152]{1,0:T(8,128)(2,1)S(1)}, bf16[256,1152]{1,0:T(8,128)(2,1)S(1)}, u32[]{:S(2)}, u32[]{:S(2)}) collective-permute-start(bf16[256,1152]{1,0:T(8,128)(2,1)S(1)} %get-tuple-element.33.img_b.own), channel_id=1, source_target_pairs={{0,224},{1,225},{2,226},{3,227},{4,228},{5,229},{6,230},{7,231},{8... | collective-permute-start | bytes 1769480 | tf_op jit(solution)/shard_map/ppermute | solution.py:35
  15.9 2.6 %shard_map.77 = (f32[256,1152]{1,0:T(8,128)S(1)}, f32[256,1152]{1,0:T(8,128)S(1)}) custom-call(f32[2]{0:T(128)S(1)} %pad_maximum_fusion.par, s32[1]{0:T(128)} %bitcast.core, bf16[256,1152]{1,0:T(8,128)(2,1)S(1)} %get-tuple-element.33.img_b.own, bf16[256,1152]{1,0:T(8,128)(2,1)S(1)} %get-tuple-element.34.txt_b, bf16[256,1152]{1,0:T(8,128)(2,1)S(1)} %collective-permute-done.3.r1), custom_call_target="tpu_custom_call" | custom-call | flops 1812000000 | bytes 1769472 | tf_op jit(solution)/shard_map/pallas_call | solution.py:45
  18.6 8.1 %collective-permute-done.2.i1 = bf16[256,1152]{1,0:T(8,128)(2,1)S(1)} collective-permute-done((bf16[256,1152]{1,0:T(8,128)(2,1)S(1)}, bf16[256,1152]{1,0:T(8,128)(2,1)S(1)}, u32[]{:S(2)}, u32[]{:S(2)}) %collective-permute-start.2) | collective-permute-done | bytes 589856 | tf_op jit(solution)/shard_map/ppermute | solution.py:35
  26.7 5.5 %collective-permute-done.t1 = bf16[256,1152]{1,0:T(8,128)(2,1)S(1)} collective-permute-done((bf16[256,1152]{1,0:T(8,128)(2,1)S(1)}, bf16[256,1152]{1,0:T(8,128)(2,1)S(1)}, u32[]{:S(2)}, u32[]{:S(2)}) %collective-permute-start) | collective-permute-done | bytes 589856 | tf_op jit(solution)/shard_map/ppermute | solution.py:35
  35.8 3.2 %shard_map.79 = (f32[256,1152]{1,0:T(8,128)S(1)}, f32[256,1152]{1,0:T(8,128)S(1)}) custom-call(f32[2]{0:T(128)S(1)} %pad_maximum_fusion.par, bf16[256,1152]{1,0:T(8,128)(2,1)S(1)} %get-tuple-element.33.img_b.own, bf16[256,1152]{1,0:T(8,128)(2,1)S(1)} %get-tuple-element.34.txt_b, bf16[256,1152]{1,0:T(8,128)(2,1)S(1)} %collective-permute-done.t1, ...), custom_call_target="tpu_custom_call" | custom-call | flops 2416000000 | bytes 5898240 | tf_op jit(solution)/shard_map/pallas_call | solution.py:45
  40.1 12.4 %collective-permute-done.1.near = bf16[256,1152]{1,0:T(8,128)(2,1)S(1)} collective-permute-done((bf16[256,1152]{1,0:T(8,128)(2,1)S(1)}, bf16[256,1152]{1,0:T(8,128)(2,1)S(1)}, u32[]{:S(2)}, u32[]{:S(2)}) %collective-permute-start.1) | collective-permute-done | bytes 589856 | tf_op jit(solution)/shard_map/ppermute | solution.py:35
  52.4 2.7 %collective-permute-start.7 = (bf16[256,1152]{1,0:T(8,128)(2,1)S(1)}, bf16[256,1152]{1,0:T(8,128)(2,1)S(1)}, u32[]{:S(2)}, u32[]{:S(2)}) collective-permute-start(bf16[256,1152]{1,0:T(8,128)(2,1)S(1)} %collective-permute-done.1.near), channel_id=1, source_target_pairs={{16,0},{17,1},{18,2},{19,3},{20,4},{21,5},{22,6},{23,7},{24,8},{25... | collective-permute-start | bytes 1769480 | tf_op jit(solution)/shard_map/ppermute | solution.py:35
  55.3 1.5 %shard_map.80.old = f32[256,1152]{1,0:T(8,128)S(1)} custom-call(f32[2]{0:T(128)S(1)} %pad_maximum_fusion.par, bf16[256,1152]{1,0:T(8,128)(2,1)S(1)} %get-tuple-element.33.img_b.own, bf16[256,1152]{1,0:T(8,128)(2,1)S(1)} %collective-permute-done.1.near, f32[256,1152]{1,0:T(8,128)S(1)} %get-tuple-element.46.old), custom_call_target="tpu_custom_call" | custom-call | flops 906000000 | bytes 2359296 | tf_op jit(solution)/shard_map/pallas_call | solution.py:45
  56.8 2.4 %shard_map.81 = (bf16[256,1152]{1,0:T(8,128)(2,1)S(1)}, bf16[256,576]{1,0:T(8,128)(2,1)S(1)}, bf16[256,576]{1,0:T(8,128)(2,1)S(1)}, f32[256,1152]{1,0:T(8,128)}) custom-call(f32[2]{0:T(128)S(1)} %pad_maximum_fusion.par, s32[1]{0:T(128)} %bitcast.core, bf16[256,1152]{1,0:T(8,128)(2,1)S(1)} %get-tuple-element.33.img_b.own, ...), custom_call_target="tpu_custom_call" | custom-call | flops 1812000000 | bytes 3539968 | tf_op jit(solution)/shard_map/pallas_call | solution.py:45
  68.0 1.3 %shard_map.84 = (bf16[144,1152]{1,0:T(8,128)(2,1)S(1)}, bf16[144,1152]{1,0:T(8,128)(2,1)S(1)}, bf16[144,1152]{1,0:T(8,128)(2,1)S(1)}, bf16[144,1152]{1,0:T(8,128)(2,1)S(1)}) custom-call(s32[1]{0:T(128)} %bitcast.core, s32[1]{0:T(128)S(6)} %select_n.8.place, bf16[256,576]{1,0:T(8,128)(2,1)S(1)} %copy-done.15, bf16[256,576]{1,0:T(8,128)(2,1)S(1)} %copy-done.13, ...), custom_call_target="tpu_custom_call" | custom-call | flops 906000000 | bytes 1769472 | tf_op jit(solution)/shard_map/pallas_call | solution.py:45
  69.8 2.3 %collective-permute-start.12 = (bf16[144,1152]{1,0:T(8,128)(2,1)S(1)}, bf16[144,1152]{1,0:T(8,128)(2,1)S(1)}, u32[]{:S(2)}, u32[]{:S(2)}) collective-permute-start(bf16[144,1152]{1,0:T(8,128)(2,1)S(1)} %get-tuple-element.57), channel_id=1, source_target_pairs={{0,96},{1,97},{2,98},{3,99},{4,100},{5,101},{6,102},{7,103},{8,104... | collective-permute-start | bytes 995336 | tf_op jit(solution)/shard_map/ppermute | solution.py:35
  73.4 7.1 %collective-permute-done.11.b = bf16[144,1152]{1,0:T(8,128)(2,1)S(1)} collective-permute-done((bf16[144,1152]{1,0:T(8,128)(2,1)S(1)}, bf16[144,1152]{1,0:T(8,128)(2,1)S(1)}, u32[]{:S(2)}, u32[]{:S(2)}) %collective-permute-start.11) | collective-permute-done | bytes 331808 | tf_op jit(solution)/shard_map/ppermute | solution.py:35
  81.6 2.1 %collective-permute-start.15 = (bf16[72,576]{1,0:T(8,128)(2,1)S(1)}, bf16[72,576]{1,0:T(8,128)(2,1)S(1)}, u32[]{:S(2)}, u32[]{:S(2)}) collective-permute-start(bf16[72,576]{1,0:T(8,128)(2,1)S(1)} %get-tuple-element.61), channel_id=1, source_target_pairs={{0,129},{1,0},{2,131},{3,2},{4,133},{5,4},{6,135},{7,6},{8,137},{9... | collective-permute-start | bytes 248840 | tf_op jit(solution)/shard_map/ppermute | solution.py:35
  83.7 1.9 %collective-permute-done.14.b = bf16[72,576]{1,0:T(8,128)(2,1)S(1)} collective-permute-done((bf16[72,576]{1,0:T(8,128)(2,1)S(1)}, bf16[72,576]{1,0:T(8,128)(2,1)S(1)}, u32[]{:S(2)}, u32[]{:S(2)}) %collective-permute-start.14) | collective-permute-done | bytes 82976 | tf_op jit(solution)/shard_map/ppermute | solution.py:35
  86.2 2.4 %collective-permute-done.16.d = bf16[72,576]{1,0:T(8,128)(2,1)S(1)} collective-permute-done((bf16[72,576]{1,0:T(8,128)(2,1)S(1)}, bf16[72,576]{1,0:T(8,128)(2,1)S(1)}, u32[]{:S(2)}, u32[]{:S(2)}) %collective-permute-start.16) | collective-permute-done | bytes 82976 | tf_op jit(solution)/shard_map/ppermute | solution.py:35
  89.4 8.2 %all-to-all-start = ((bf16[8,72,72]{2,1,0:T(8,128)(2,1)}), bf16[8,72,72]{2,1,0:T(8,128)(2,1)S(1)}, u32[]{:S(2)}, u32[]{:S(2)}) async-start(bf16[8,72,72]{2,1,0:T(8,128)(2,1)} %shard_map.86), calls=%async_computation | async-start | bytes 294912 | tf_op jit(solution)/shard_map/all_to_all | solution.py:346
  98.6 2.1 %shard_map.82 = f32[256,1152]{1,0:T(8,128)} custom-call(bf16[256,1152]{1,0:T(8,128)(2,1)S(1)} %copy-done.19, bf16[1152,1152]{1,0:T(8,128)(2,1)S(1)} %copy-done.1), custom_call_target="tpu_custom_call" | custom-call | flops 1812000000 | bytes 3244032 | tf_op jit(solution)/shard_map/pallas_call | solution.py:45
  100.7 5.1 %all-to-all-done.parts = bf16[8,72,72]{2,1,0:T(8,128)(2,1)S(1)} async-done(((bf16[8,72,72]{2,1,0:T(8,128)(2,1)}), bf16[8,72,72]{2,1,0:T(8,128)(2,1)S(1)}, u32[]{:S(2)}, u32[]{:S(2)}) %all-to-all-start) | async-done | bytes 82976 | tf_op jit(solution)/shard_map/all_to_all | solution.py:346
  106.5 8.7 %all-to-all-start.1 = ((bf16[16,72,72]{2,1,0:T(8,128)(2,1)}), bf16[16,72,72]{2,1,0:T(8,128)(2,1)S(1)}, u32[]{:S(2)}, u32[]{:S(2)}) async-start(bf16[16,72,72]{2,1,0:T(8,128)(2,1)} %shard_map.87), calls=%async_computation.1 | async-start | bytes 589824 | tf_op jit(solution)/shard_map/all_to_all | solution.py:348
  117.6 4.6 %shard_map.83 = f32[256,1152]{1,0:T(8,128)} custom-call(f32[2]{0:T(128)S(1)} %pad_maximum_fusion.par, s32[1]{0:T(128)} %bitcast.core, bf16[256,1152]{1,0:T(8,128)(2,1)S(1)} %copy-done.7, bf16[256,1152]{1,0:T(8,128)(2,1)} %collective-permute-done.8.i2, bf16[256,1152]{1,0:T(8,128)(2,1)} %collective-permute-done.9.r3, f32[256,1152]{1,0:T(8,128)S(1)} %copy-done.17, ...), custom_call_target="tpu_custom_call" | custom-call | flops 2416000000 | bytes 3538944 | tf_op jit(solution)/shard_map/pallas_call | solution.py:45
  122.1 2.0 %all-to-all-done.1.parts = bf16[16,72,72]{2,1,0:T(8,128)(2,1)S(1)} async-done(((bf16[16,72,72]{2,1,0:T(8,128)(2,1)}), bf16[16,72,72]{2,1,0:T(8,128)(2,1)S(1)}, u32[]{:S(2)}, u32[]{:S(2)}) %all-to-all-start.1) | async-done | bytes 165920 | tf_op jit(solution)/shard_map/all_to_all | solution.py:348
  (68 shorter events, 25.6 us)
Async XLA Ops:
  7.3 28.6 %copy-start.6 = (bf16[256,1152]{1,0:T(8,128)(2,1)}, bf16[256,1152]{1,0:T(8,128)(2,1)S(1)}, u32[]{:S(2)}) copy-start(bf16[256,1152]{1,0:T(8,128)(2,1)S(1)} %get-tuple-element.34.txt_b) | copy-start | bytes 1769476
  7.3 8.7 %collective-permute-start.3 = (bf16[256,1152]{1,0:T(8,128)(2,1)S(1)}, bf16[256,1152]{1,0:T(8,128)(2,1)S(1)}, u32[]{:S(2)}, u32[]{:S(2)}) collective-permute-start(bf16[256,1152]{1,0:T(8,128)(2,1)S(1)} %get-tuple-element.35), channel_id=1, source_target_pairs={{0,16},{1,17},{2,18},{3,19},{4,20},{5,21},{6,22},{7,23},{8,24},{9,... | collective-permute-start | bytes 1769480 | tf_op jit(solution)/shard_map/ppermute | solution.py:35
  10.6 16.1 %collective-permute-start.2 = (bf16[256,1152]{1,0:T(8,128)(2,1)S(1)}, bf16[256,1152]{1,0:T(8,128)(2,1)S(1)}, u32[]{:S(2)}, u32[]{:S(2)}) collective-permute-start(bf16[256,1152]{1,0:T(8,128)(2,1)S(1)} %get-tuple-element.33.img_b.own), channel_id=1, source_target_pairs={{0,224},{1,225},{2,226},{3,227},{4,228},{5,229},{6,230},{7,231},{8... | collective-permute-start | bytes 1769480 | tf_op jit(solution)/shard_map/ppermute | solution.py:35
  14.0 18.2 %collective-permute-start = (bf16[256,1152]{1,0:T(8,128)(2,1)S(1)}, bf16[256,1152]{1,0:T(8,128)(2,1)S(1)}, u32[]{:S(2)}, u32[]{:S(2)}) collective-permute-start(bf16[256,1152]{1,0:T(8,128)(2,1)S(1)} %get-tuple-element.34.txt_b), channel_id=1, source_target_pairs={{0,32},{1,33},{2,34},{3,35},{4,36},{5,37},{6,38},{7,39},{8,40},{9,... | collective-permute-start | bytes 1769480 | tf_op jit(solution)/shard_map/ppermute | solution.py:35
  15.9 17.5 %copy-start.8 = (bf16[256,1152]{1,0:T(8,128)(2,1)}, bf16[256,1152]{1,0:T(8,128)(2,1)S(1)}, u32[]{:S(2)}) copy-start(bf16[256,1152]{1,0:T(8,128)(2,1)S(1)} %shard_map.78.images) | copy-start | bytes 1769476
  32.2 2.8 %collective-permute-start.4 = (bf16[256,1152]{1,0:T(8,128)(2,1)S(1)}, bf16[256,1152]{1,0:T(8,128)(2,1)S(1)}, u32[]{:S(2)}, u32[]{:S(2)}) collective-permute-start(bf16[256,1152]{1,0:T(8,128)(2,1)S(1)} %collective-permute-done.t1), channel_id=1, source_target_pairs={{0,16},{1,17},{2,18},{3,19},{4,20},{5,21},{6,22},{7,23},{8,24},{9,... | collective-permute-start | bytes 1769480 | tf_op jit(solution)/shard_map/ppermute | solution.py:35
  33.4 2.5 %collective-permute-start.5 = (bf16[256,1152]{1,0:T(8,128)(2,1)S(1)}, bf16[256,1152]{1,0:T(8,128)(2,1)S(1)}, u32[]{:S(2)}, u32[]{:S(2)}) collective-permute-start(bf16[256,1152]{1,0:T(8,128)(2,1)S(1)} %collective-permute-done.2.i1), channel_id=1, source_target_pairs={{0,16},{1,17},{2,18},{3,19},{4,20},{5,21},{6,22},{7,23},{8,24},{9,... | collective-permute-start | bytes 1769480 | tf_op jit(solution)/shard_map/ppermute | solution.py:35
  33.4 6.7 %collective-permute-start.6 = (bf16[256,1152]{1,0:T(8,128)(2,1)S(1)}, bf16[256,1152]{1,0:T(8,128)(2,1)S(1)}, u32[]{:S(2)}, u32[]{:S(2)}) collective-permute-start(bf16[256,1152]{1,0:T(8,128)(2,1)S(1)} %shard_map.78.images), channel_id=1, source_target_pairs={{0,16},{1,17},{2,18},{3,19},{4,20},{5,21},{6,22},{7,23},{8,24},{9,... | collective-permute-start | bytes 1769480 | tf_op jit(solution)/shard_map/ppermute | solution.py:35
  33.9 18.6 %collective-permute-start.1 = (bf16[256,1152]{1,0:T(8,128)(2,1)S(1)}, bf16[256,1152]{1,0:T(8,128)(2,1)S(1)}, u32[]{:S(2)}, u32[]{:S(2)}) collective-permute-start(bf16[256,1152]{1,0:T(8,128)(2,1)S(1)} %collective-permute-done.t1), channel_id=1, source_target_pairs={{0,32},{1,33},{2,34},{3,35},{4,36},{5,37},{6,38},{7,39},{8,40},{9,... | collective-permute-start | bytes 1769480 | tf_op jit(solution)/shard_map/ppermute | solution.py:35
  40.1 16.7 %copy-start.10 = (bf16[256,1152]{1,0:T(8,128)(2,1)}, bf16[256,1152]{1,0:T(8,128)(2,1)S(1)}, u32[]{:S(2)}) copy-start(bf16[256,1152]{1,0:T(8,128)(2,1)S(1)} %collective-permute-done.6.images2) | copy-start | bytes 1769476
  52.4 4.3 %collective-permute-start.7 = (bf16[256,1152]{1,0:T(8,128)(2,1)S(1)}, bf16[256,1152]{1,0:T(8,128)(2,1)S(1)}, u32[]{:S(2)}, u32[]{:S(2)}) collective-permute-start(bf16[256,1152]{1,0:T(8,128)(2,1)S(1)} %collective-permute-done.1.near), channel_id=1, source_target_pairs={{16,0},{17,1},{18,2},{19,3},{20,4},{21,5},{22,6},{23,7},{24,8},{25... | collective-permute-start | bytes 1769480 | tf_op jit(solution)/shard_map/ppermute | solution.py:35
  55.2 17.0 %collective-permute-start.8 = (bf16[256,1152]{1,0:T(8,128)(2,1)S(1)}, bf16[256,1152]{1,0:T(8,128)(2,1)}, u32[]{:S(2)}, u32[]{:S(2)}) collective-permute-start(bf16[256,1152]{1,0:T(8,128)(2,1)S(1)} %collective-permute-done.2.i1), channel_id=1, source_target_pairs={{0,224},{1,225},{2,226},{3,227},{4,228},{5,229},{6,230},{7,231},{8... | collective-permute-start | bytes 1769480 | tf_op jit(solution)/shard_map/ppermute | solution.py:35
  60.7 2.5 %collective-permute-start.10 = (bf16[256,576]{1,0:T(8,128)(2,1)S(1)}, bf16[256,576]{1,0:T(8,128)(2,1)S(1)}, u32[]{:S(2)}, u32[]{:S(2)}) collective-permute-start(bf16[256,576]{1,0:T(8,128)(2,1)S(1)} %get-tuple-element.53), channel_id=1, source_target_pairs={{0,16},{1,17},{2,18},{3,19},{4,20},{5,21},{6,22},{7,23},{8,24},{9,... | collective-permute-start | bytes 884744 | tf_op jit(solution)/shard_map/ppermute | solution.py:35
  68.0 29.5 %copy-start.1 = (bf16[1152,1152]{1,0:T(8,128)(2,1)S(1)}, bf16[1152,1152]{1,0:T(8,128)(2,1)}, u32[]{:S(2)}) copy-start(bf16[1152,1152]{1,0:T(8,128)(2,1)} %head.3) | copy-start | bytes 7962628
  69.4 11.1 %collective-permute-start.11 = (bf16[144,1152]{1,0:T(8,128)(2,1)S(1)}, bf16[144,1152]{1,0:T(8,128)(2,1)S(1)}, u32[]{:S(2)}, u32[]{:S(2)}) collective-permute-start(bf16[144,1152]{1,0:T(8,128)(2,1)S(1)} %get-tuple-element.56), channel_id=1, source_target_pairs={{0,32},{1,33},{2,34},{3,35},{4,36},{5,37},{6,38},{7,39},{8,40},{9,... | collective-permute-start | bytes 995336 | tf_op jit(solution)/shard_map/ppermute | solution.py:35
  69.8 10.6 %collective-permute-start.12 = (bf16[144,1152]{1,0:T(8,128)(2,1)S(1)}, bf16[144,1152]{1,0:T(8,128)(2,1)S(1)}, u32[]{:S(2)}, u32[]{:S(2)}) collective-permute-start(bf16[144,1152]{1,0:T(8,128)(2,1)S(1)} %get-tuple-element.57), channel_id=1, source_target_pairs={{0,96},{1,97},{2,98},{3,99},{4,100},{5,101},{6,102},{7,103},{8,104... | collective-permute-start | bytes 995336 | tf_op jit(solution)/shard_map/ppermute | solution.py:35
  72.1 8.4 %collective-permute-start.13 = (bf16[144,1152]{1,0:T(8,128)(2,1)S(1)}, bf16[144,1152]{1,0:T(8,128)(2,1)S(1)}, u32[]{:S(2)}, u32[]{:S(2)}) collective-permute-start(bf16[144,1152]{1,0:T(8,128)(2,1)S(1)} %get-tuple-element.58), channel_id=1, source_target_pairs={{0,64},{1,65},{2,66},{3,67},{4,68},{5,69},{6,70},{7,71},{8,72},{9,... | collective-permute-start | bytes 995336 | tf_op jit(solution)/shard_map/ppermute | solution.py:35
  72.1 43.1 %collective-permute-start.9 = (bf16[256,1152]{1,0:T(8,128)(2,1)}, bf16[256,1152]{1,0:T(8,128)(2,1)}, u32[]{:S(2)}, u32[]{:S(2)}) collective-permute-start(bf16[256,1152]{1,0:T(8,128)(2,1)} %collective-permute-done.8.i2), channel_id=1, source_target_pairs={{0,16},{1,17},{2,18},{3,19},{4,20},{5,21},{6,22},{7,23},{8,24},{9,... | collective-permute-start | bytes 1769480 | tf_op jit(solution)/shard_map/ppermute | solution.py:35
  80.9 4.7 %collective-permute-start.14 = (bf16[72,576]{1,0:T(8,128)(2,1)S(1)}, bf16[72,576]{1,0:T(8,128)(2,1)S(1)}, u32[]{:S(2)}, u32[]{:S(2)}) collective-permute-start(bf16[72,576]{1,0:T(8,128)(2,1)S(1)} %get-tuple-element.60), channel_id=1, source_target_pairs={{0,1},{1,128},{2,3},{3,130},{4,5},{5,132},{6,7},{7,134},{8,9},{9,1... | collective-permute-start | bytes 248840 | tf_op jit(solution)/shard_map/ppermute | solution.py:35
  81.6 4.6 %collective-permute-start.15 = (bf16[72,576]{1,0:T(8,128)(2,1)S(1)}, bf16[72,576]{1,0:T(8,128)(2,1)S(1)}, u32[]{:S(2)}, u32[]{:S(2)}) collective-permute-start(bf16[72,576]{1,0:T(8,128)(2,1)S(1)} %get-tuple-element.61), channel_id=1, source_target_pairs={{0,129},{1,0},{2,131},{3,2},{4,133},{5,4},{6,135},{7,6},{8,137},{9... | collective-permute-start | bytes 248840 | tf_op jit(solution)/shard_map/ppermute | solution.py:35
  83.7 4.9 %collective-permute-start.16 = (bf16[72,576]{1,0:T(8,128)(2,1)S(1)}, bf16[72,576]{1,0:T(8,128)(2,1)S(1)}, u32[]{:S(2)}, u32[]{:S(2)}) collective-permute-start(bf16[72,576]{1,0:T(8,128)(2,1)S(1)} %get-tuple-element.62), channel_id=1, source_target_pairs={{0,128},{1,129},{2,130},{3,131},{4,132},{5,133},{6,134},{7,135},{8... | collective-permute-start | bytes 248840 | tf_op jit(solution)/shard_map/ppermute | solution.py:35
  89.4 16.4 %all-to-all-start = ((bf16[8,72,72]{2,1,0:T(8,128)(2,1)}), bf16[8,72,72]{2,1,0:T(8,128)(2,1)S(1)}, u32[]{:S(2)}, u32[]{:S(2)}) async-start(bf16[8,72,72]{2,1,0:T(8,128)(2,1)} %shard_map.86), calls=%async_computation | async-start | bytes 294912 | tf_op jit(solution)/shard_map/all_to_all | solution.py:346
  98.6 16.6 %copy-start.5 = (bf16[256,1152]{1,0:T(8,128)(2,1)S(1)}, bf16[256,1152]{1,0:T(8,128)(2,1)}, u32[]{:S(2)}) copy-start(bf16[256,1152]{1,0:T(8,128)(2,1)} %texts.3) | copy-start | bytes 1769476
  106.5 17.6 %all-to-all-start.1 = ((bf16[16,72,72]{2,1,0:T(8,128)(2,1)}), bf16[16,72,72]{2,1,0:T(8,128)(2,1)S(1)}, u32[]{:S(2)}, u32[]{:S(2)}) async-start(bf16[16,72,72]{2,1,0:T(8,128)(2,1)} %shard_map.87), calls=%async_computation.1 | async-start | bytes 589824 | tf_op jit(solution)/shard_map/all_to_all | solution.py:348
  (15 other events, 25.4 us)

commit v4 on v3

v4 whole, which is shorter than its diff:
```python
import functools

import jax
import jax.numpy as jnp
import numpy as np
from jax import lax
from jax.experimental import pallas as pl
from jax.experimental.pallas import tpu as pltpu
from jax.sharding import Mesh, PartitionSpec as P

AXES = ("yh", "x", "core", "z", "yl")
SIZES = (2, 4, 2, 8, 2)
INNER = SIZES[3] * SIZES[4]
COUNT = 16 * INNER
CHIPS = SIZES[0] * SIZES[1]
BLKS = CHIPS * SIZES[2]
BF = jnp.bfloat16
F32 = jnp.float32


def chip_pairs(steps):
    shift = steps * SIZES[2] * INNER
    return [(source, (source + shift) % COUNT) for source in range(COUNT)]


def core_pairs(only=None):
    return [
        (source, source ^ INNER)
        for source in range(COUNT)
        if only is None or (source // INNER) % 2 == only
    ]


def moved(value, pairs):
    return lax.ppermute(value, AXES, pairs)


def mm(a, b, dims):
    return lax.dot_general(a, b, ((dims[:1], dims[1:]), ((), ())), preferred_element_type=F32)


def call(body, outs, *args, scalars=(), scratch=(), limit=8, space=pltpu.VMEM, small=0):
    in_specs = [pl.BlockSpec(memory_space=pltpu.SMEM)] * len(scalars)
    in_specs += [pl.BlockSpec(memory_space=space)] * len(args)
    shapes = [jax.ShapeDtypeStruct(shape, dtype) for shape, dtype in outs]
    if space is pltpu.HBM:
        args = [pltpu.with_memory_space_constraint(a, space) for a in args]
    return pl.pallas_call(
        body,
        out_shape=shapes,
        in_specs=in_specs,
        out_specs=[pl.BlockSpec(memory_space=pltpu.SMEM)] * small
        + [pl.BlockSpec(memory_space=pltpu.VMEM)] * (len(outs) - small),
        scratch_shapes=list(scratch),
        cost_estimate=pl.CostEstimate(
            flops=0,
            bytes_accessed=sum(int(np.prod(a.shape)) * a.dtype.itemsize for a in (*args, *shapes)),
            transcendentals=0,
        ),
        compiler_params=pltpu.CompilerParams(vmem_limit_bytes=limit * 2**20),
    )(*scalars, *args)


def sigmoid(x):
    return 1.0 / (1.0 + jnp.exp(-x))


def applied(par, rows, cols):
    logit = par[0] * mm(rows, cols, (1, 1)) + par[1]
    return mm(sigmoid(logit).astype(BF), cols, (1, 0))


def text_unit(texts):
    tfloat = texts.astype(F32)
    tnorm = jnp.sqrt(jnp.sum(tfloat * tfloat, -1, keepdims=True) + 1e-06)
    inverse = 1.0 / tnorm
    return tfloat * inverse, inverse


def halved(value, first, second):
    rows = value.shape[0] // 2
    first[...] = value[:rows]
    second[...] = value[rows:]


CUTS = (0, 256, 512, 768, 1152)


def start_body(
    here, scale, bias, images, texts, head, info, par,
    ta, tb, ia, ib, both, unit, norm, t_in, i_in, h_in, sems,
):
    copies = [
        pltpu.make_async_copy(texts, t_in, sems.at[0]),
        pltpu.make_async_copy(images, i_in, sems.at[1]),
    ]
    for k in range(len(CUTS) - 1):
        rows = pl.ds(CUTS[k], CUTS[k + 1] - CUTS[k])
        copies.append(pltpu.make_async_copy(head.at[rows], h_in.at[rows], sems.at[2 + k]))
    for copy in copies:
        copy.start()
    for k in range(here.shape[0]):
        info[k] = here[k]
    par[0] = scale[0]
    par[1] = bias[0]
    copies[0].wait()
    count = t_in.shape[0]
    low = text_unit(t_in[...])[0].astype(BF)
    halved(low, ta, tb)
    both[:count] = low
    copies[1].wait()
    both[2 * count :] = i_in[...]
    proj = None
    for k in range(len(CUTS) - 1):
        copies[2 + k].wait()
        cut = slice(CUTS[k], CUTS[k + 1])
        term = jnp.dot(i_in[:, cut], h_in[cut, :], preferred_element_type=F32)
        proj = term if proj is None else proj + term
    inverse = 1.0 / jnp.sqrt(jnp.sum(proj * proj, -1, keepdims=True) + 1e-06)
    value = proj * inverse
    unit[...] = value
    norm[...] = inverse
    low = value.astype(BF)
    halved(low, ia, ib)
    both[count : 2 * count] = low


def text_of(both):
    return both[: both.shape[0] // 3]


def image_of(both):
    count = both.shape[0] // 3
    return both[count : 2 * count]


def order_body(both, both_s, out, out2):
    own = both.shape[1] // INNER
    count = both.shape[0] // 3
    for z in range(SIZES[3]):
        for yl in range(SIZES[4]):
            source, target = (z * SIZES[4] + yl) * own, (yl * SIZES[3] + z) * own
            out[:, target : target + own] = both[2 * count :, source : source + own]
            out2[:, target : target + own] = both_s[2 * count :, source : source + own]


def home_body(par, both, dimg, dtxt):
    img_b, txt_b = image_of(both), text_of(both)
    logit = par[0] * mm(img_b, txt_b, (1, 1)) + par[1]
    eye = lax.broadcasted_iota(jnp.int32, logit.shape, 0) == lax.broadcasted_iota(
        jnp.int32, logit.shape, 1
    )
    grad = jnp.where(eye, -sigmoid(-logit), sigmoid(logit)).astype(BF)
    dimg[...] = mm(grad, txt_b, (1, 0))
    dtxt[...] = mm(grad, img_b, (0, 0))


def joined(first, second):
    return jnp.concatenate([first[...], second[...]], 0)


def near_body(par, core, t1a, t1b, i1a, i1b, both, both_s, dimg, dtxt, dimg_o, dtxt_o, dimg_s, dtxt_s):
    t1, i1 = joined(t1a, t1b), joined(i1a, i1b)
    dimg_o[...] = dimg[...] + applied(par, image_of(both), t1)
    dtxt_o[...] = dtxt[...] + applied(par, text_of(both), i1)
    dimg_s[...] = applied(par, image_of(both_s), t1)
    dtxt_s[...] = applied(par, text_of(both_s), i1)

    @pl.when(core[0] == 0)
    def _():
        dtxt_o[...] += applied(par, text_of(both), image_of(both_s))

    @pl.when(core[0] != 0)
    def _():
        dimg_o[...] += applied(par, image_of(both), text_of(both_s))


def give_body(giver, rows_of, par, core, first, second, both_s, old, out):
    @pl.when(core[0] == giver)
    def _():
        out[...] = (old[...] + applied(par, rows_of(both_s), joined(first, second))).astype(BF)

    @pl.when(core[0] != giver)
    def _():
        out[...] = old[...].astype(BF)


def far_body(rows_of, par, first, second, both, old, out):
    out[...] = old[...] + applied(par, rows_of(both), joined(first, second))


def image_end_body(par, core, old, given, unit, norm, whole, keep, send):
    dimg = par[0] * (old[...] + given[...].astype(F32))
    value = unit[...]
    dproj = ((dimg - value * jnp.sum(value * dimg, -1, keepdims=True)) * norm[...]).astype(BF)
    whole[...] = dproj
    half = dproj.shape[1] // 2

    @pl.when(core[0] == 0)
    def _():
        keep[...] = dproj[:, :half]
        send[...] = dproj[:, half:]

    @pl.when(core[0] != 0)
    def _():
        keep[...] = dproj[:, half:]
        send[...] = dproj[:, :half]


def text_end_body(par, old, given, texts, out):
    dtxt = par[0] * (old[...] + given[...].astype(F32))
    value, inverse = text_unit(texts[...])
    out[...] = (dtxt - value * jnp.sum(value * dtxt, -1, keepdims=True)) * inverse


TURNS = (0, 1, 3, 2)


def turned(place, pieces, outs):
    for turn, out in zip(TURNS, outs):
        out[...] = pieces[lax.rem(place + turn, 4)]


def head_body(core, keep, other, images, images2, *rest):
    outs, pieces = rest[:4], rest[4]
    total = mm(keep[...], images[...], (0, 0)) + mm(other[...], images2[...], (0, 0))
    rows, half = pieces.shape[1], total.shape[1] // 2

    @pl.when(core[0] == 0)
    def _():
        for k in range(4):
            pieces[k] = total[k * rows : (k + 1) * rows].astype(BF)

    @pl.when(core[0] != 0)
    def _():
        for k in range(4):
            up, left = 2 * (k // 2) * rows, (k % 2) * half
            first = total[up : up + rows, left : left + half]
            second = total[up + rows : up + 2 * rows, left : left + half]
            pieces[k] = jnp.concatenate([first, second], 1).astype(BF)

    turned(core[1], pieces, outs)


def quarter_body(core, a, b, c, d, *rest):
    outs, pieces = rest[:4], rest[4]
    total = a[...].astype(F32) + b[...].astype(F32) + c[...].astype(F32) + d[...].astype(F32)
    _, rows, half = pieces.shape

    def quadrant(down, right):
        return total[down * rows : (down + 1) * rows, right * half : (right + 1) * half].astype(BF)

    @pl.when(core[0] == 0)
    def _():
        for k in range(4):
            pieces[k] = quadrant(k // 2, k % 2)

    @pl.when(core[0] != 0)
    def _():
        for k in range(4):
            pieces[k] = quadrant(k % 2, k // 2)

    turned(core[2], pieces, outs)


def grad_image_body(dproj, head, out):
    out[...] = mm(dproj[...], head[...], (1, 1))


def split_body(a, b, c, d, out):
    total = a[...].astype(F32) + b[...].astype(F32) + c[...].astype(F32) + d[...].astype(F32)
    own = out.shape[2]
    for k in range(out.shape[0]):
        out[k] = total[:, k * own : (k + 1) * own].astype(BF)


def spread_body(parts, out):
    total = parts[0].astype(F32)
    for k in range(1, parts.shape[0]):
        total = total + parts[k].astype(F32)
    total = total.astype(BF)
    for k in range(out.shape[0]):
        out[k] = total


def join_body(factor, parts, out):
    yhs, xs, cores = SIZES[:3]
    order = [(yh * xs + x) * cores for x in range(xs) for yh in range(yhs)]
    order += [(yh * xs + x) * cores + 1 for yh in range(yhs) for x in range(xs)]
    out[...] = jnp.concatenate([parts[k].astype(F32) for k in order], 0).T * factor


def ring_pairs(turn, first):
    pairs = []
    for source in range(COUNT):
        yh, x, core, z, yl = np.unravel_index(source, SIZES)
        if core == first:
            x = (x + turn) % SIZES[1]
        else:
            y = (yh * SIZES[4] + yl + turn) % 4
            yh, yl = y // SIZES[4], y % SIZES[4]
        pairs.append((source, int(np.ravel_multi_index((yh, x, core, z, yl), SIZES))))
    return pairs


def on_device(images, texts, head, scale, bias):
    core = lax.axis_index("core")
    across, along = lax.axis_index("x"), lax.axis_index(("yh", "yl"))
    here = jnp.stack(
        [core, jnp.where(core == 0, across, along), jnp.where(core == 0, along, across)]
    ).astype(jnp.int32)
    ahead, back, swap = chip_pairs(1), chip_pairs(-1), core_pairs()
    count, width = images.shape
    half = width // 2
    big = (count, width)
    tie = lax.optimization_barrier

    part_of = ((count // 2, width), BF)
    info, par, ta, tb, ia, ib, both, unit_img, pnorm = call(
        start_body,
        [((3,), jnp.int32), ((2,), F32)] + [part_of] * 4 + [((3 * count, width), BF), (big, F32), ((count, 1), F32)],
        images, texts, head, scalars=(here, scale, bias), small=2, space=pltpu.HBM, limit=16,
        scratch=[
            pltpu.VMEM(big, BF), pltpu.VMEM(big, BF), pltpu.VMEM(head.shape, BF),
            pltpu.SemaphoreType.DMA((1 + len(CUTS),)),
        ],
    )
    t1 = [moved(ta, ahead), moved(tb, ahead)]
    i1 = [moved(ia, back), moved(ib, back)]
    both_s = moved(both, swap)
    dimg, dtxt = call(home_body, [(big, F32)] * 2, both, scalars=(par,))
    t2 = [moved(t, ahead) for t in t1]
    i2 = [moved(i, back) for i in i1]
    dimg, dtxt, dimg_s, dtxt_s = call(
        near_body, [(big, F32)] * 4, *t1, *i1, both, both_s, dimg, dtxt, scalars=(par, info)
    )
    ordered, ordered2 = call(order_body, [(big, BF)] * 2, both, both_s)
    *t2, i2[0], i2[1], dimg, dtxt, dimg_s, dtxt_s, ordered, ordered2 = tie(
        (*t2, *i2, dimg, dtxt, dimg_s, dtxt_s, ordered, ordered2)
    )

    (give,) = call(
        functools.partial(give_body, 1, image_of), [(big, BF)], *t2, both_s, dimg_s,
        scalars=(par, info),
    )
    given = moved(give, swap)
    (dimg,) = call(
        functools.partial(far_body, image_of), [(big, F32)], *t2, both, dimg, scalars=(par,)
    )
    dproj, keep, send = call(
        image_end_body, [(big, BF), ((count, half), BF), ((count, half), BF)],
        dimg, given, unit_img, pnorm, scalars=(par, info),
    )
    other = moved(send, swap)
    quarter = ((half // 4, width), BF)
    parts = call(
        head_body, [quarter] * 4, keep, other, ordered, ordered2, scalars=(info,),
        scratch=[pltpu.VMEM((4, half // 4, width), BF)],
    )
    parts = list(parts)
    *i2, parts[0] = tie((*i2, parts[0]))
    parts = parts[:1] + [moved(p, ring_pairs(t, 0)) for p, t in zip(parts[1:], TURNS[1:])]
    (grad_image,) = call(grad_image_body, [(big, F32)], dproj, head)
    (give,) = call(
        functools.partial(give_body, 0, text_of), [(big, BF)], *i2, both_s, dtxt_s,
        scalars=(par, info),
    )
    (dtxt,) = call(
        functools.partial(far_body, text_of), [(big, F32)], *i2, both, dtxt, scalars=(par,)
    )
    *parts, grad_image, give, dtxt = tie((*parts, grad_image, give, dtxt))
    small = ((half // 8, half), BF)
    parts = call(
        quarter_body, [small] * 4, *parts, scalars=(info,),
        scratch=[pltpu.VMEM((4, half // 8, half), BF)],
    )
    parts = list(parts)
    given = moved(give, swap)
    parts = parts[:1] + [moved(p, ring_pairs(t, 1)) for p, t in zip(parts[1:], TURNS[1:])]
    (grad_text,) = call(text_end_body, [(big, F32)], dtxt, given, texts, scalars=(par,))
    *parts, grad_text = tie((*parts, grad_text))
    own = width // INNER
    (part,) = call(split_body, [((SIZES[3], half // 8, own), BF)], *parts)
    part = lax.all_to_all(part, "z", 0, 0)
    (part,) = call(spread_body, [((BLKS, half // 8, own), BF)], part)
    part = lax.all_to_all(part, ("yh", "x", "core"), 0, 0)
    factor = 1.0 / float(count * COUNT) ** 0.5
    (head_grad,) = call(functools.partial(join_body, factor), [((own, width), F32)], part)
    return (grad_image, grad_text, head_grad)


def solution(mesh):
    fine = Mesh(mesh.devices.reshape(SIZES), AXES)
    rows = P(AXES, None)
    return jax.shard_map(
        on_device,
        mesh=fine,
        in_specs=(rows, rows, P(), P(), P()),
        out_specs=(rows, rows, P(("z", "yl"), None)),
        check_vma=False,
    )
```

time: 126 us -> 109 us (0.87)
  blocking collectives: 0 us -> 31.1 us
  waiting for transfers between devices: 48.2 us -> 24.2 us
  local copies, waits for them, and re-layouts: 14.6 us -> 0.01 us
  starting transfers between devices: 36.1 us -> 26.9 us
    all_to_all x0 -> x2, blocking collectives: none -> 31.1 us  [the longest x1 16.2 us: on_device(): part = lax.all_to_all(part, 'z', 0, 0)]
    ppermute x17 -> x18, waiting for transfers between devices: 41.2 us -> 24.2 us  [moved(): return lax.ppermute(value, AXES, pairs)]
    all_to_all x2 -> x0, starting transfers between devices: 16.8 us -> none  [the longest x1 8.66 us: on_device(): part = lax.all_to_all(part, ('yh', 'x', 'core'), 0, 0)]
    unnamed x40 -> x4, local copies, waits for them, and re-layouts: 14.6 us -> 0.01 us
    ppermute x17 -> x18, starting transfers between devices: 19.3 us -> 26.9 us  [moved(): return lax.ppermute(value, AXES, pairs)]
    all_to_all x2 -> x0, waiting for transfers between devices: 7.02 us -> none  [the longest x1 5.05 us: on_device(): part = lax.all_to_all(part, 'z', 0, 0)]
    pallas_call x13 -> x16, Pallas kernels: 23.8 us -> 24.8 us  [call(): pl.pallas_call(body, out_shape=shapes, in_specs=in_specs, out_specs=[pl.B...]
  transfers between devices with their start and end apart: 19 -> 18, of which waited for: 12 -> 7; matrix products, arithmetic and copies ran while one was open for 0% -> 0% of each run, Pallas kernels for 16% -> 14%
where the time goes in v4:
time: 109 us
  blocking collectives  31.1 us (29%)
  starting transfers between devices  26.9 us (25%)
  Pallas kernels  24.8 us (23%)
  waiting for transfers between devices  24.2 us (22%)
  between operations  2.08 us (2%)
    ppermute x18, starting transfers between devices, moved(): return lax.ppermute(value, AXES, pairs)  26.9 us
    pallas_call x16, Pallas kernels, call(): pl.pallas_call(body, out_shape=shapes, in_specs=in_specs, out_specs=[pl.B...  24.8 us
    ppermute x18, waiting for transfers between devices, moved(): return lax.ppermute(value, AXES, pairs)  24.2 us
    all_to_all x1, blocking collectives, on_device(): part = lax.all_to_all(part, 'z', 0, 0)  16.2 us
    all_to_all x1, blocking collectives, on_device(): part = lax.all_to_all(part, ('yh', 'x', 'core'), 0, 0)  14.9 us
  transfers between devices with their start and end apart: 18, of which 7 were waited for; matrix products, arithmetic and copies ran while one was open for 0% of the time, Pallas kernels for 14%

profile of v4, /device:TPU:1, one launch (start us, length us, event | category | flops | bytes accessed | tf_op | source)
XLA Modules:
  0.0 109.2 jit_solution(1497950216838809503)
XLA Ops:
  2.0 3.8 %shard_map.76 = (s32[3]{0:T(128)S(1)}, f32[2]{0:T(128)S(1)}, bf16[128,1152]{1,0:T(8,128)(2,1)S(1)}, bf16[128,1152]{1,0:T(8,128)(2,1)S(1)}, bf16[128,1152]{1,0:T(...) custom-call(s32[3]{0:T(128)S(1)} %pad_add_fusion.here, ...), custom_call_target="tpu_custom_call" | custom-call | bytes 7963668 | tf_op jit(solution)/shard_map/pallas_call | solution.py:48
  5.8 3.3 %collective-permute-start.8 = (bf16[768,1152]{1,0:T(8,128)(2,1)S(1)}, bf16[768,1152]{1,0:T(8,128)(2,1)S(1)}, u32[]{:S(2)}, u32[]{:S(2)}) collective-permute-start(bf16[768,1152]{1,0:T(8,128)(2,1)S(1)} %get-tuple-element.62.both), channel_id=1, source_target_pairs={{0,16},{1,17},{2,18},{3,19},{4,20},{5,21},{6,22},{7,23},{8,24},{9,... | collective-permute-start | bytes 5308424 | tf_op jit(solution)/shard_map/ppermute | solution.py:35
  9.8 4.4 %collective-permute-start.4 = (bf16[128,1152]{1,0:T(8,128)(2,1)S(1)}, bf16[128,1152]{1,0:T(8,128)(2,1)S(1)}, u32[]{:S(2)}, u32[]{:S(2)}) collective-permute-start(bf16[128,1152]{1,0:T(8,128)(2,1)S(1)} %get-tuple-element.58), channel_id=1, source_target_pairs={{0,224},{1,225},{2,226},{3,227},{4,228},{5,229},{6,230},{7,231},{8... | collective-permute-start | bytes 884744 | tf_op jit(solution)/shard_map/ppermute | solution.py:35
  14.2 1.4 %collective-permute-start.6 = (bf16[128,1152]{1,0:T(8,128)(2,1)S(1)}, bf16[128,1152]{1,0:T(8,128)(2,1)S(1)}, u32[]{:S(2)}, u32[]{:S(2)}) collective-permute-start(bf16[128,1152]{1,0:T(8,128)(2,1)S(1)} %get-tuple-element.59), channel_id=1, source_target_pairs={{0,224},{1,225},{2,226},{3,227},{4,228},{5,229},{6,230},{7,231},{8... | collective-permute-start | bytes 884744 | tf_op jit(solution)/shard_map/ppermute | solution.py:35
  15.7 5.6 %collective-permute-done.t1a = bf16[128,1152]{1,0:T(8,128)(2,1)S(1)} collective-permute-done((bf16[128,1152]{1,0:T(8,128)(2,1)S(1)}, bf16[128,1152]{1,0:T(8,128)(2,1)S(1)}, u32[]{:S(2)}, u32[]{:S(2)}) %collective-permute-start) | collective-permute-done | bytes 294944 | tf_op jit(solution)/shard_map/ppermute | solution.py:35
  21.3 6.3 %collective-permute-done.2.t1b = bf16[128,1152]{1,0:T(8,128)(2,1)S(1)} collective-permute-done((bf16[128,1152]{1,0:T(8,128)(2,1)S(1)}, bf16[128,1152]{1,0:T(8,128)(2,1)S(1)}, u32[]{:S(2)}, u32[]{:S(2)}) %collective-permute-start.2) | collective-permute-done | bytes 294944 | tf_op jit(solution)/shard_map/ppermute | solution.py:35
  27.6 5.1 %collective-permute-start.5 = (bf16[128,1152]{1,0:T(8,128)(2,1)S(1)}, bf16[128,1152]{1,0:T(8,128)(2,1)S(1)}, u32[]{:S(2)}, u32[]{:S(2)}) collective-permute-start(bf16[128,1152]{1,0:T(8,128)(2,1)S(1)} %collective-permute-done.4.i1a), channel_id=1, source_target_pairs={{0,224},{1,225},{2,226},{3,227},{4,228},{5,229},{6,230},{7,231},{8... | collective-permute-start | bytes 884744 | tf_op jit(solution)/shard_map/ppermute | solution.py:35
  32.8 1.7 %shard_map.77 = (f32[256,1152]{1,0:T(8,128)S(1)}, f32[256,1152]{1,0:T(8,128)S(1)}) custom-call(f32[2]{0:T(128)S(1)} %get-tuple-element.60.par, bf16[768,1152]{1,0:T(8,128)(2,1)S(1)} %get-tuple-element.62.both), custom_call_target="tpu_custom_call" | custom-call | bytes 4128768 | tf_op jit(solution)/shard_map/pallas_call | solution.py:48
  35.5 4.0 %shard_map.78 = (f32[256,1152]{1,0:T(8,128)S(1)}, f32[256,1152]{1,0:T(8,128)S(1)}, f32[256,1152]{1,0:T(8,128)S(1)}, f32[256,1152]{1,0:T(8,128)S(1)}) custom-call(f32[2]{0:T(128)S(1)} %get-tuple-element.60.par, s32[3]{0:T(128)S(1)} %get-tuple-element.61.core, bf16[128,1152]{1,0:T(8,128)(2,1)S(1)} %collective-permute-done.t1a, ...), custom_call_target="tpu_custom_call" | custom-call | bytes 11796480 | tf_op jit(solution)/shard_map/pallas_call | solution.py:48
  39.6 4.2 %collective-permute-done.7.second = bf16[128,1152]{1,0:T(8,128)(2,1)S(1)} collective-permute-done((bf16[128,1152]{1,0:T(8,128)(2,1)S(1)}, bf16[128,1152]{1,0:T(8,128)(2,1)S(1)}, u32[]{:S(2)}, u32[]{:S(2)}) %collective-permute-start.7) | collective-permute-done | bytes 294944 | tf_op jit(solution)/shard_map/ppermute | solution.py:35
  43.8 1.5 %shard_map.81 = bf16[256,1152]{1,0:T(8,128)(2,1)S(1)} custom-call(f32[2]{0:T(128)S(1)} %get-tuple-element.60.par, s32[3]{0:T(128)S(1)} %get-tuple-element.61.core, bf16[128,1152]{1,0:T(8,128)(2,1)S(1)} %collective-permute-done.1.first, bf16[128,1152]{1,0:T(8,128)(2,1)S(1)} %collective-permute-done.3.second, ...), custom_call_target="tpu_custom_call" | custom-call | bytes 4128768 | tf_op jit(solution)/shard_map/pallas_call | solution.py:48
  45.3 1.7 %collective-permute-start.9 = (bf16[256,1152]{1,0:T(8,128)(2,1)S(1)}, bf16[256,1152]{1,0:T(8,128)(2,1)S(1)}, u32[]{:S(2)}, u32[]{:S(2)}) collective-permute-start(bf16[256,1152]{1,0:T(8,128)(2,1)S(1)} %shard_map.81), channel_id=1, source_target_pairs={{0,16},{1,17},{2,18},{3,19},{4,20},{5,21},{6,22},{7,23},{8,24},{9,... | collective-permute-start | bytes 1769480 | tf_op jit(solution)/shard_map/ppermute | solution.py:35
  47.0 1.5 %shard_map.80.old = f32[256,1152]{1,0:T(8,128)S(1)} custom-call(f32[2]{0:T(128)S(1)} %get-tuple-element.60.par, bf16[128,1152]{1,0:T(8,128)(2,1)S(1)} %collective-permute-done.1.first, bf16[128,1152]{1,0:T(8,128)(2,1)S(1)} %collective-permute-done.3.second, bf16[768,1152]{1,0:T(8,128)(2,1)S(1)} %get-tuple-element.62.both, f32[256,1152]{1,0:T(8,128)S(1)} %get-tuple-element.75.old), custom_call_target="tpu_custom_call" | custom-call | bytes 4718592 | tf_op jit(solution)/shard_map/pallas_call | solution.py:48
  51.5 1.9 %shard_map.83 = (bf16[144,1152]{1,0:T(8,128)(2,1)S(1)}, bf16[144,1152]{1,0:T(8,128)(2,1)S(1)}, bf16[144,1152]{1,0:T(8,128)(2,1)S(1)}, bf16[144,1152]{1,0:T(8,128)(2,1)S(1)}) custom-call(s32[3]{0:T(128)S(1)} %get-tuple-element.61.core, bf16[256,576]{1,0:T(8,128)(2,1)S(1)} %get-tuple-element.79.keep, bf16[256,576]{1,0:T(8,128)(2,1)S(1)} %collective-permute-done.10.other, ...), custom_call_target="tpu_custom_call" | custom-call | bytes 3096576 | tf_op jit(solution)/shard_map/pallas_call | solution.py:48
  53.4 2.7 %collective-permute-start.12 = (bf16[144,1152]{1,0:T(8,128)(2,1)S(1)}, bf16[144,1152]{1,0:T(8,128)(2,1)S(1)}, u32[]{:S(2)}, u32[]{:S(2)}) collective-permute-start(bf16[144,1152]{1,0:T(8,128)(2,1)S(1)} %get-tuple-element.86), channel_id=1, source_target_pairs={{0,96},{1,97},{2,98},{3,99},{4,100},{5,101},{6,102},{7,103},{8,104... | collective-permute-start | bytes 995336 | tf_op jit(solution)/shard_map/ppermute | solution.py:35
  56.1 2.0 %shard_map.84 = f32[256,1152]{1,0:T(8,128)} custom-call(bf16[256,1152]{1,0:T(8,128)(2,1)S(1)} %get-tuple-element.88.dproj, bf16[1152,1152]{1,0:T(8,128)(2,1)S(1)} %copy-done), custom_call_target="tpu_custom_call" | custom-call | bytes 4423680 | tf_op jit(solution)/shard_map/pallas_call | solution.py:48
  58.2 1.5 %shard_map.86.old = f32[256,1152]{1,0:T(8,128)S(1)} custom-call(f32[2]{0:T(128)S(1)} %get-tuple-element.60.par, bf16[128,1152]{1,0:T(8,128)(2,1)S(1)} %collective-permute-done.5.first, bf16[128,1152]{1,0:T(8,128)(2,1)S(1)} %collective-permute-done.7.second, bf16[768,1152]{1,0:T(8,128)(2,1)S(1)} %get-tuple-element.62.both, f32[256,1152]{1,0:T(8,128)S(1)} %get-tuple-element.92.old), custom_call_target="tpu_custom_call" | custom-call | bytes 4718592 | tf_op jit(solution)/shard_map/pallas_call | solution.py:48
  60.3 4.2 %collective-permute-done.11.b = bf16[144,1152]{1,0:T(8,128)(2,1)S(1)} collective-permute-done((bf16[144,1152]{1,0:T(8,128)(2,1)S(1)}, bf16[144,1152]{1,0:T(8,128)(2,1)S(1)}, u32[]{:S(2)}, u32[]{:S(2)}) %collective-permute-start.11) | collective-permute-done | bytes 331808 | tf_op jit(solution)/shard_map/ppermute | solution.py:35
  64.5 3.9 %collective-permute-start.17 = (bf16[256,1152]{1,0:T(8,128)(2,1)S(1)}, bf16[256,1152]{1,0:T(8,128)(2,1)S(1)}, u32[]{:S(2)}, u32[]{:S(2)}) collective-permute-start(bf16[256,1152]{1,0:T(8,128)(2,1)S(1)} %shard_map.85), channel_id=1, source_target_pairs={{0,16},{1,17},{2,18},{3,19},{4,20},{5,21},{6,22},{7,23},{8,24},{9,... | collective-permute-start | bytes 1769480 | tf_op jit(solution)/shard_map/ppermute | solution.py:35
  70.6 1.5 %collective-permute-start.15 = (bf16[72,576]{1,0:T(8,128)(2,1)S(1)}, bf16[72,576]{1,0:T(8,128)(2,1)S(1)}, u32[]{:S(2)}, u32[]{:S(2)}) collective-permute-start(bf16[72,576]{1,0:T(8,128)(2,1)S(1)} %get-tuple-element.100), channel_id=1, source_target_pairs={{0,129},{1,0},{2,131},{3,2},{4,133},{5,4},{6,135},{7,6},{8,137},{9... | collective-permute-start | bytes 248840 | tf_op jit(solution)/shard_map/ppermute | solution.py:35
  72.4 2.1 %shard_map.88 = f32[256,1152]{1,0:T(8,128)} custom-call(f32[2]{0:T(128)S(1)} %get-tuple-element.60.par, f32[256,1152]{1,0:T(8,128)S(1)} %shard_map.86.old, bf16[256,1152]{1,0:T(8,128)(2,1)S(1)} %collective-permute-done.17.given, bf16[256,1152]{1,0:T(8,128)(2,1)S(1)} %copy-done.1), custom_call_target="tpu_custom_call" | custom-call | bytes 3538944 | tf_op jit(solution)/shard_map/pallas_call | solution.py:48
  74.6 2.4 %collective-permute-done.16.d = bf16[72,576]{1,0:T(8,128)(2,1)S(1)} collective-permute-done((bf16[72,576]{1,0:T(8,128)(2,1)S(1)}, bf16[72,576]{1,0:T(8,128)(2,1)S(1)}, u32[]{:S(2)}, u32[]{:S(2)}) %collective-permute-start.16) | collective-permute-done | bytes 82976 | tf_op jit(solution)/shard_map/ppermute | solution.py:35
  77.2 16.2 %all_to_all.10.parts = bf16[8,72,72]{2,1,0:T(8,128)(2,1)S(1)} all-to-all(bf16[8,72,72]{2,1,0:T(8,128)(2,1)S(1)} %shard_map.89), channel_id=1, replica_groups=mesh['yh'=2,'x'=4,'core'=2,'z'=8,'yl'=2] {'z'}, dimensions={0} | all-to-all | bytes 165888 | tf_op jit(solution)/shard_map/all_to_all | solution.py:384
  93.4 14.9 %all_to_all.11.parts = bf16[16,72,72]{2,1,0:T(8,128)(2,1)S(1)} all-to-all(bf16[16,72,72]{2,1,0:T(8,128)(2,1)S(1)} %shard_map.90), channel_id=1, replica_groups=mesh['yh'=2,'x'=4,'core'=2,'z'=8,'yl'=2] {'yh','x','core'}, dimensions={0} | all-to-all | bytes 331776 | tf_op jit(solution)/shard_map/all_to_all | solution.py:386
  (35 shorter events, 9.3 us)
Async XLA Ops:
  5.8 28.7 %collective-permute-start.8 = (bf16[768,1152]{1,0:T(8,128)(2,1)S(1)}, bf16[768,1152]{1,0:T(8,128)(2,1)S(1)}, u32[]{:S(2)}, u32[]{:S(2)}) collective-permute-start(bf16[768,1152]{1,0:T(8,128)(2,1)S(1)} %get-tuple-element.62.both), channel_id=1, source_target_pairs={{0,16},{1,17},{2,18},{3,19},{4,20},{5,21},{6,22},{7,23},{8,24},{9,... | collective-permute-start | bytes 5308424 | tf_op jit(solution)/shard_map/ppermute | solution.py:35
  9.1 12.2 %collective-permute-start = (bf16[128,1152]{1,0:T(8,128)(2,1)S(1)}, bf16[128,1152]{1,0:T(8,128)(2,1)S(1)}, u32[]{:S(2)}, u32[]{:S(2)}) collective-permute-start(bf16[128,1152]{1,0:T(8,128)(2,1)S(1)} %get-tuple-element.56), channel_id=1, source_target_pairs={{0,32},{1,33},{2,34},{3,35},{4,36},{5,37},{6,38},{7,39},{8,40},{9,... | collective-permute-start | bytes 884744 | tf_op jit(solution)/shard_map/ppermute | solution.py:35
  9.1 18.5 %collective-permute-start.2 = (bf16[128,1152]{1,0:T(8,128)(2,1)S(1)}, bf16[128,1152]{1,0:T(8,128)(2,1)S(1)}, u32[]{:S(2)}, u32[]{:S(2)}) collective-permute-start(bf16[128,1152]{1,0:T(8,128)(2,1)S(1)} %get-tuple-element.57), channel_id=1, source_target_pairs={{0,32},{1,33},{2,34},{3,35},{4,36},{5,37},{6,38},{7,39},{8,40},{9,... | collective-permute-start | bytes 884744 | tf_op jit(solution)/shard_map/ppermute | solution.py:35
  9.8 17.8 %collective-permute-start.4 = (bf16[128,1152]{1,0:T(8,128)(2,1)S(1)}, bf16[128,1152]{1,0:T(8,128)(2,1)S(1)}, u32[]{:S(2)}, u32[]{:S(2)}) collective-permute-start(bf16[128,1152]{1,0:T(8,128)(2,1)S(1)} %get-tuple-element.58), channel_id=1, source_target_pairs={{0,224},{1,225},{2,226},{3,227},{4,228},{5,229},{6,230},{7,231},{8... | collective-permute-start | bytes 884744 | tf_op jit(solution)/shard_map/ppermute | solution.py:35
  14.2 18.5 %collective-permute-start.6 = (bf16[128,1152]{1,0:T(8,128)(2,1)S(1)}, bf16[128,1152]{1,0:T(8,128)(2,1)S(1)}, u32[]{:S(2)}, u32[]{:S(2)}) collective-permute-start(bf16[128,1152]{1,0:T(8,128)(2,1)S(1)} %get-tuple-element.59), channel_id=1, source_target_pairs={{0,224},{1,225},{2,226},{3,227},{4,228},{5,229},{6,230},{7,231},{8... | collective-permute-start | bytes 884744 | tf_op jit(solution)/shard_map/ppermute | solution.py:35
  21.3 18.3 %collective-permute-start.1 = (bf16[128,1152]{1,0:T(8,128)(2,1)S(1)}, bf16[128,1152]{1,0:T(8,128)(2,1)S(1)}, u32[]{:S(2)}, u32[]{:S(2)}) collective-permute-start(bf16[128,1152]{1,0:T(8,128)(2,1)S(1)} %collective-permute-done.t1a), channel_id=1, source_target_pairs={{0,32},{1,33},{2,34},{3,35},{4,36},{5,37},{6,38},{7,39},{8,40},{9,... | collective-permute-start | bytes 884744 | tf_op jit(solution)/shard_map/ppermute | solution.py:35
  27.6 12.0 %collective-permute-start.3 = (bf16[128,1152]{1,0:T(8,128)(2,1)S(1)}, bf16[128,1152]{1,0:T(8,128)(2,1)S(1)}, u32[]{:S(2)}, u32[]{:S(2)}) collective-permute-start(bf16[128,1152]{1,0:T(8,128)(2,1)S(1)} %collective-permute-done.2.t1b), channel_id=1, source_target_pairs={{0,32},{1,33},{2,34},{3,35},{4,36},{5,37},{6,38},{7,39},{8,40},{9,... | collective-permute-start | bytes 884744 | tf_op jit(solution)/shard_map/ppermute | solution.py:35
  27.6 12.0 %collective-permute-start.5 = (bf16[128,1152]{1,0:T(8,128)(2,1)S(1)}, bf16[128,1152]{1,0:T(8,128)(2,1)S(1)}, u32[]{:S(2)}, u32[]{:S(2)}) collective-permute-start(bf16[128,1152]{1,0:T(8,128)(2,1)S(1)} %collective-permute-done.4.i1a), channel_id=1, source_target_pairs={{0,224},{1,225},{2,226},{3,227},{4,228},{5,229},{6,230},{7,231},{8... | collective-permute-start | bytes 884744 | tf_op jit(solution)/shard_map/ppermute | solution.py:35
  32.7 11.1 %collective-permute-start.7 = (bf16[128,1152]{1,0:T(8,128)(2,1)S(1)}, bf16[128,1152]{1,0:T(8,128)(2,1)S(1)}, u32[]{:S(2)}, u32[]{:S(2)}) collective-permute-start(bf16[128,1152]{1,0:T(8,128)(2,1)S(1)} %collective-permute-done.6.i1b), channel_id=1, source_target_pairs={{0,224},{1,225},{2,226},{3,227},{4,228},{5,229},{6,230},{7,231},{8... | collective-permute-start | bytes 884744 | tf_op jit(solution)/shard_map/ppermute | solution.py:35
  45.3 3.3 %collective-permute-start.9 = (bf16[256,1152]{1,0:T(8,128)(2,1)S(1)}, bf16[256,1152]{1,0:T(8,128)(2,1)S(1)}, u32[]{:S(2)}, u32[]{:S(2)}) collective-permute-start(bf16[256,1152]{1,0:T(8,128)(2,1)S(1)} %shard_map.81), channel_id=1, source_target_pairs={{0,16},{1,17},{2,18},{3,19},{4,20},{5,21},{6,22},{7,23},{8,24},{9,... | collective-permute-start | bytes 1769480 | tf_op jit(solution)/shard_map/ppermute | solution.py:35
  48.6 7.5 %copy-start = (bf16[1152,1152]{1,0:T(8,128)(2,1)S(1)}, bf16[1152,1152]{1,0:T(8,128)(2,1)}, u32[]{:S(2)}) copy-start(bf16[1152,1152]{1,0:T(8,128)(2,1)} %head.3) | copy-start | bytes 7962628
  49.8 1.7 %collective-permute-start.10 = (bf16[256,576]{1,0:T(8,128)(2,1)S(1)}, bf16[256,576]{1,0:T(8,128)(2,1)S(1)}, u32[]{:S(2)}, u32[]{:S(2)}) collective-permute-start(bf16[256,576]{1,0:T(8,128)(2,1)S(1)} %get-tuple-element.80), channel_id=1, source_target_pairs={{0,16},{1,17},{2,18},{3,19},{4,20},{5,21},{6,22},{7,23},{8,24},{9,... | collective-permute-start | bytes 884744 | tf_op jit(solution)/shard_map/ppermute | solution.py:35
  53.4 11.1 %collective-permute-start.11 = (bf16[144,1152]{1,0:T(8,128)(2,1)S(1)}, bf16[144,1152]{1,0:T(8,128)(2,1)S(1)}, u32[]{:S(2)}, u32[]{:S(2)}) collective-permute-start(bf16[144,1152]{1,0:T(8,128)(2,1)S(1)} %get-tuple-element.85), channel_id=1, source_target_pairs={{0,32},{1,33},{2,34},{3,35},{4,36},{5,37},{6,38},{7,39},{8,40},{9,... | collective-permute-start | bytes 995336 | tf_op jit(solution)/shard_map/ppermute | solution.py:35
  53.4 11.0 %collective-permute-start.12 = (bf16[144,1152]{1,0:T(8,128)(2,1)S(1)}, bf16[144,1152]{1,0:T(8,128)(2,1)S(1)}, u32[]{:S(2)}, u32[]{:S(2)}) collective-permute-start(bf16[144,1152]{1,0:T(8,128)(2,1)S(1)} %get-tuple-element.86), channel_id=1, source_target_pairs={{0,96},{1,97},{2,98},{3,99},{4,100},{5,101},{6,102},{7,103},{8,104... | collective-permute-start | bytes 995336 | tf_op jit(solution)/shard_map/ppermute | solution.py:35
  56.1 8.4 %collective-permute-start.13 = (bf16[144,1152]{1,0:T(8,128)(2,1)S(1)}, bf16[144,1152]{1,0:T(8,128)(2,1)S(1)}, u32[]{:S(2)}, u32[]{:S(2)}) collective-permute-start(bf16[144,1152]{1,0:T(8,128)(2,1)S(1)} %get-tuple-element.87), channel_id=1, source_target_pairs={{0,64},{1,65},{2,66},{3,67},{4,68},{5,69},{6,70},{7,71},{8,72},{9,... | collective-permute-start | bytes 995336 | tf_op jit(solution)/shard_map/ppermute | solution.py:35
  60.3 12.2 %copy-start.1 = (bf16[256,1152]{1,0:T(8,128)(2,1)S(1)}, bf16[256,1152]{1,0:T(8,128)(2,1)}, u32[]{:S(2)}) copy-start(bf16[256,1152]{1,0:T(8,128)(2,1)} %texts.3) | copy-start | bytes 1769476
  64.5 8.0 %collective-permute-start.17 = (bf16[256,1152]{1,0:T(8,128)(2,1)S(1)}, bf16[256,1152]{1,0:T(8,128)(2,1)S(1)}, u32[]{:S(2)}, u32[]{:S(2)}) collective-permute-start(bf16[256,1152]{1,0:T(8,128)(2,1)S(1)} %shard_map.85), channel_id=1, source_target_pairs={{0,16},{1,17},{2,18},{3,19},{4,20},{5,21},{6,22},{7,23},{8,24},{9,... | collective-permute-start | bytes 1769480 | tf_op jit(solution)/shard_map/ppermute | solution.py:35
  69.3 5.2 %collective-permute-start.14 = (bf16[72,576]{1,0:T(8,128)(2,1)S(1)}, bf16[72,576]{1,0:T(8,128)(2,1)S(1)}, u32[]{:S(2)}, u32[]{:S(2)}) collective-permute-start(bf16[72,576]{1,0:T(8,128)(2,1)S(1)} %get-tuple-element.99), channel_id=1, source_target_pairs={{0,1},{1,128},{2,3},{3,130},{4,5},{5,132},{6,7},{7,134},{8,9},{9,1... | collective-permute-start | bytes 248840 | tf_op jit(solution)/shard_map/ppermute | solution.py:35
  70.6 4.0 %collective-permute-start.15 = (bf16[72,576]{1,0:T(8,128)(2,1)S(1)}, bf16[72,576]{1,0:T(8,128)(2,1)S(1)}, u32[]{:S(2)}, u32[]{:S(2)}) collective-permute-start(bf16[72,576]{1,0:T(8,128)(2,1)S(1)} %get-tuple-element.100), channel_id=1, source_target_pairs={{0,129},{1,0},{2,131},{3,2},{4,133},{5,4},{6,135},{7,6},{8,137},{9... | collective-permute-start | bytes 248840 | tf_op jit(solution)/shard_map/ppermute | solution.py:35
  72.1 4.9 %collective-permute-start.16 = (bf16[72,576]{1,0:T(8,128)(2,1)S(1)}, bf16[72,576]{1,0:T(8,128)(2,1)S(1)}, u32[]{:S(2)}, u32[]{:S(2)}) collective-permute-start(bf16[72,576]{1,0:T(8,128)(2,1)S(1)} %get-tuple-element.101), channel_id=1, source_target_pairs={{0,128},{1,129},{2,130},{3,131},{4,132},{5,133},{6,134},{7,135},{8... | collective-permute-start | bytes 248840 | tf_op jit(solution)/shard_map/ppermute | solution.py:35

commit v5 on v4

--- a/solution.py
+++ b/solution.py
@@ -87,7 +87,7 @@
 
 
 def start_body(
-    here, scale, bias, images, texts, head, info, par,
+    scale, bias, images, texts, head, par,
     ta, tb, ia, ib, both, unit, norm, t_in, i_in, h_in, sems,
 ):
     copies = [
@@ -99,8 +99,6 @@
         copies.append(pltpu.make_async_copy(head.at[rows], h_in.at[rows], sems.at[2 + k]))
     for copy in copies:
         copy.start()
-    for k in range(here.shape[0]):
-        info[k] = here[k]
     par[0] = scale[0]
     par[1] = bias[0]
     copies[0].wait()
@@ -159,28 +157,28 @@
     return jnp.concatenate([first[...], second[...]], 0)
 
 
-def near_body(par, core, t1a, t1b, i1a, i1b, both, both_s, dimg, dtxt, dimg_o, dtxt_o, dimg_s, dtxt_s):
+def near_body(par, t1a, t1b, i1a, i1b, both, both_s, dimg, dtxt, dimg_o, dtxt_o, dimg_s, dtxt_s):
     t1, i1 = joined(t1a, t1b), joined(i1a, i1b)
     dimg_o[...] = dimg[...] + applied(par, image_of(both), t1)
     dtxt_o[...] = dtxt[...] + applied(par, text_of(both), i1)
     dimg_s[...] = applied(par, image_of(both_s), t1)
     dtxt_s[...] = applied(par, text_of(both_s), i1)
 
-    @pl.when(core[0] == 0)
+    @pl.when(lax.axis_index("core") == 0)
     def _():
         dtxt_o[...] += applied(par, text_of(both), image_of(both_s))
 
-    @pl.when(core[0] != 0)
+    @pl.when(lax.axis_index("core") != 0)
     def _():
         dimg_o[...] += applied(par, image_of(both), text_of(both_s))
 
 
-def give_body(giver, rows_of, par, core, first, second, both_s, old, out):
-    @pl.when(core[0] == giver)
+def give_body(giver, rows_of, par, first, second, both_s, old, out):
+    @pl.when(lax.axis_index("core") == giver)
     def _():
         out[...] = (old[...] + applied(par, rows_of(both_s), joined(first, second))).astype(BF)
 
-    @pl.when(core[0] != giver)
+    @pl.when(lax.axis_index("core") != giver)
     def _():
         out[...] = old[...].astype(BF)
 
@@ -189,19 +187,19 @@
     out[...] = old[...] + applied(par, rows_of(both), joined(first, second))
 
 
-def image_end_body(par, core, old, given, unit, norm, whole, keep, send):
+def image_end_body(par, old, given, unit, norm, whole, keep, send):
     dimg = par[0] * (old[...] + given[...].astype(F32))
     value = unit[...]
     dproj = ((dimg - value * jnp.sum(value * dimg, -1, keepdims=True)) * norm[...]).astype(BF)
     whole[...] = dproj
     half = dproj.shape[1] // 2
 
-    @pl.when(core[0] == 0)
+    @pl.when(lax.axis_index("core") == 0)
     def _():
         keep[...] = dproj[:, :half]
         send[...] = dproj[:, half:]
 
-    @pl.when(core[0] != 0)
+    @pl.when(lax.axis_index("core") != 0)
     def _():
         keep[...] = dproj[:, half:]
         send[...] = dproj[:, :half]
@@ -213,7 +211,19 @@
     out[...] = (dtxt - value * jnp.sum(value * dtxt, -1, keepdims=True)) * inverse
 
 
-TURNS = (0, 1, 3, 2)
+TURNS = (0, 2, 1, 3)
+
+
+def across_place():
+    return lax.axis_index("x")
+
+
+def along_place():
+    return lax.axis_index("yh") * SIZES[4] + lax.axis_index("yl")
+
+
+def place_of(first):
+    return jnp.where(lax.axis_index("core") == first, across_place(), along_place())
 
 
 def turned(place, pieces, outs):
@@ -221,17 +231,17 @@
         out[...] = pieces[lax.rem(place + turn, 4)]
 
 
-def head_body(core, keep, other, images, images2, *rest):
+def head_body(keep, other, images, images2, *rest):
     outs, pieces = rest[:4], rest[4]
     total = mm(keep[...], images[...], (0, 0)) + mm(other[...], images2[...], (0, 0))
     rows, half = pieces.shape[1], total.shape[1] // 2
 
-    @pl.when(core[0] == 0)
+    @pl.when(lax.axis_index("core") == 0)
     def _():
         for k in range(4):
             pieces[k] = total[k * rows : (k + 1) * rows].astype(BF)
 
-    @pl.when(core[0] != 0)
+    @pl.when(lax.axis_index("core") != 0)
     def _():
         for k in range(4):
             up, left = 2 * (k // 2) * rows, (k % 2) * half
@@ -239,10 +249,10 @@
             second = total[up + rows : up + 2 * rows, left : left + half]
             pieces[k] = jnp.concatenate([first, second], 1).astype(BF)
 
-    turned(core[1], pieces, outs)
-
-
-def quarter_body(core, a, b, c, d, *rest):
+    turned(place_of(0), pieces, outs)
+
+
+def quarter_body(a, b, c, d, *rest):
     outs, pieces = rest[:4], rest[4]
     total = a[...].astype(F32) + b[...].astype(F32) + c[...].astype(F32) + d[...].astype(F32)
     _, rows, half = pieces.shape
@@ -250,17 +260,17 @@
     def quadrant(down, right):
         return total[down * rows : (down + 1) * rows, right * half : (right + 1) * half].astype(BF)
 
-    @pl.when(core[0] == 0)
+    @pl.when(lax.axis_index("core") == 0)
     def _():
         for k in range(4):
             pieces[k] = quadrant(k // 2, k % 2)
 
-    @pl.when(core[0] != 0)
+    @pl.when(lax.axis_index("core") != 0)
     def _():
         for k in range(4):
             pieces[k] = quadrant(k % 2, k // 2)
 
-    turned(core[2], pieces, outs)
+    turned(place_of(1), pieces, outs)
 
 
 def grad_image_body(dproj, head, out):
@@ -304,11 +314,6 @@
 
 
 def on_device(images, texts, head, scale, bias):
-    core = lax.axis_index("core")
-    across, along = lax.axis_index("x"), lax.axis_index(("yh", "yl"))
-    here = jnp.stack(
-        [core, jnp.where(core == 0, across, along), jnp.where(core == 0, along, across)]
-    ).astype(jnp.int32)
     ahead, back, swap = chip_pairs(1), chip_pairs(-1), core_pairs()
     count, width = images.shape
     half = width // 2
@@ -316,10 +321,10 @@
     tie = lax.optimization_barrier
 
     part_of = ((count // 2, width), BF)
-    info, par, ta, tb, ia, ib, both, unit_img, pnorm = call(
+    par, ta, tb, ia, ib, both, unit_img, pnorm = call(
         start_body,
-        [((3,), jnp.int32), ((2,), F32)] + [part_of] * 4 + [((3 * count, width), BF), (big, F32), ((count, 1), F32)],
-        images, texts, head, scalars=(here, scale, bias), small=2, space=pltpu.HBM, limit=16,
+        [((2,), F32)] + [part_of] * 4 + [((3 * count, width), BF), (big, F32), ((count, 1), F32)],
+        images, texts, head, scalars=(scale, bias), small=1, space=pltpu.HBM, limit=16,
         scratch=[
             pltpu.VMEM(big, BF), pltpu.VMEM(big, BF), pltpu.VMEM(head.shape, BF),
             pltpu.SemaphoreType.DMA((1 + len(CUTS),)),
@@ -329,55 +334,56 @@
     i1 = [moved(ia, back), moved(ib, back)]
     both_s = moved(both, swap)
     dimg, dtxt = call(home_body, [(big, F32)] * 2, both, scalars=(par,))
+    t1[0], dimg, dtxt = tie((t1[0], dimg, dtxt))
+    ordered, ordered2 = call(order_body, [(big, BF)] * 2, both, both_s)
     t2 = [moved(t, ahead) for t in t1]
     i2 = [moved(i, back) for i in i1]
     dimg, dtxt, dimg_s, dtxt_s = call(
-        near_body, [(big, F32)] * 4, *t1, *i1, both, both_s, dimg, dtxt, scalars=(par, info)
-    )
-    ordered, ordered2 = call(order_body, [(big, BF)] * 2, both, both_s)
-    *t2, i2[0], i2[1], dimg, dtxt, dimg_s, dtxt_s, ordered, ordered2 = tie(
-        (*t2, *i2, dimg, dtxt, dimg_s, dtxt_s, ordered, ordered2)
+        near_body, [(big, F32)] * 4, *t1, *i1, both, both_s, dimg, dtxt, scalars=(par,)
+    )
+    t2[0], i2[0], t2[1], dimg, dtxt, dimg_s, dtxt_s, ordered, ordered2 = tie(
+        (t2[0], i2[0], t2[1], dimg, dtxt, dimg_s, dtxt_s, ordered, ordered2)
     )
 
     (give,) = call(
         functools.partial(give_body, 1, image_of), [(big, BF)], *t2, both_s, dimg_s,
-        scalars=(par, info),
-    )
+        scalars=(par,),
+    )
+    i2[1], give = tie((i2[1], give))
     given = moved(give, swap)
     (dimg,) = call(
         functools.partial(far_body, image_of), [(big, F32)], *t2, both, dimg, scalars=(par,)
     )
     dproj, keep, send = call(
         image_end_body, [(big, BF), ((count, half), BF), ((count, half), BF)],
-        dimg, given, unit_img, pnorm, scalars=(par, info),
+        dimg, given, unit_img, pnorm, scalars=(par,),
     )
     other = moved(send, swap)
     quarter = ((half // 4, width), BF)
     parts = call(
-        head_body, [quarter] * 4, keep, other, ordered, ordered2, scalars=(info,),
+        head_body, [quarter] * 4, keep, other, ordered, ordered2,
         scratch=[pltpu.VMEM((4, half // 4, width), BF)],
     )
     parts = list(parts)
-    *i2, parts[0] = tie((*i2, parts[0]))
     parts = parts[:1] + [moved(p, ring_pairs(t, 0)) for p, t in zip(parts[1:], TURNS[1:])]
     (grad_image,) = call(grad_image_body, [(big, F32)], dproj, head)
     (give,) = call(
         functools.partial(give_body, 0, text_of), [(big, BF)], *i2, both_s, dtxt_s,
-        scalars=(par, info),
+        scalars=(par,),
     )
     (dtxt,) = call(
         functools.partial(far_body, text_of), [(big, F32)], *i2, both, dtxt, scalars=(par,)
     )
-    *parts, grad_image, give, dtxt = tie((*parts, grad_image, give, dtxt))
+    given_txt = moved(give, swap)
+    *parts, grad_image, given_txt, dtxt = tie((*parts, grad_image, given_txt, dtxt))
     small = ((half // 8, half), BF)
     parts = call(
-        quarter_body, [small] * 4, *parts, scalars=(info,),
+        quarter_body, [small] * 4, *parts,
         scratch=[pltpu.VMEM((4, half // 8, half), BF)],
     )
     parts = list(parts)
-    given = moved(give, swap)
     parts = parts[:1] + [moved(p, ring_pairs(t, 1)) for p, t in zip(parts[1:], TURNS[1:])]
-    (grad_text,) = call(text_end_body, [(big, F32)], dtxt, given, texts, scalars=(par,))
+    (grad_text,) = call(text_end_body, [(big, F32)], dtxt, given_txt, texts, scalars=(par,))
     *parts, grad_text = tie((*parts, grad_text))
     own = width // INNER
     (part,) = call(split_body, [((SIZES[3], half // 8, own), BF)], *parts)

time: 109 us -> 101 us (0.927)
  waiting for transfers between devices: 24.2 us -> 8.64 us
  starting transfers between devices: 26.9 us -> 33.6 us
  blocking collectives: 31.1 us -> 33 us
  Pallas kernels: 24.8 us -> 23.1 us
    ppermute x18, waiting for transfers between devices: 24.2 us -> 8.64 us  [moved(): return lax.ppermute(value, AXES, pairs)]
    ppermute x18, starting transfers between devices: 26.9 us -> 33.6 us  [moved(): return lax.ppermute(value, AXES, pairs)]
    all_to_all x1, blocking collectives: 14.9 us -> 17.1 us  [on_device(): part = lax.all_to_all(part, ('yh', 'x', 'core'), 0, 0)]
    pallas_call x16, Pallas kernels: 24.8 us -> 23.1 us  [call(): pl.pallas_call(body, out_shape=shapes, in_specs=in_specs, out_specs=[pl.B...]
  transfers between devices with their start and end apart: 18 -> 18, of which waited for: 7 -> 8; matrix products, arithmetic and copies ran while one was open for 0% -> 0% of each run, Pallas kernels for 14% -> 17%
where the time goes in v5:
time: 101 us
  starting transfers between devices  33.6 us (33%)
  blocking collectives  33 us (33%)
  Pallas kernels  23.1 us (23%)
  waiting for transfers between devices  8.64 us (9%)
  between operations  2.05 us (2%)
    ppermute x18, starting transfers between devices, moved(): return lax.ppermute(value, AXES, pairs)  33.6 us
    pallas_call x16, Pallas kernels, call(): pl.pallas_call(body, out_shape=shapes, in_specs=in_specs, out_specs=[pl.B...  23.1 us
    all_to_all x1, blocking collectives, on_device(): part = lax.all_to_all(part, ('yh', 'x', 'core'), 0, 0)  17.1 us
    all_to_all x1, blocking collectives, on_device(): part = lax.all_to_all(part, 'z', 0, 0)  16 us
    ppermute x18, waiting for transfers between devices, moved(): return lax.ppermute(value, AXES, pairs)  8.64 us
  transfers between devices with their start and end apart: 18, of which 8 were waited for; matrix products, arithmetic and copies ran while one was open for 0% of the time, Pallas kernels for 17%

profile of v5, /device:TPU:1, one launch (start us, length us, event | category | flops | bytes accessed | tf_op | source)
XLA Modules:
  0.0 100.7 jit_solution(9819011619794855887)
XLA Ops:
  1.9 3.2 %shard_map.76 = (f32[2]{0:T(128)S(1)}, bf16[128,1152]{1,0:T(8,128)(2,1)S(1)}, bf16[128,1152]{1,0:T(8,128)(2,1)S(1)}, bf16[128,1152]{1,0:T(8,128)(2,1)S(1)}, bf16...) custom-call(f32[1]{0:T(128)S(6)} %copy.8.scale, ...), custom_call_target="tpu_custom_call" | custom-call | bytes 7963656 | tf_op jit(solution)/shard_map/pallas_call | solution.py:48
  5.2 3.3 %collective-permute-start.7 = (bf16[768,1152]{1,0:T(8,128)(2,1)S(1)}, bf16[768,1152]{1,0:T(8,128)(2,1)S(1)}, u32[]{:S(2)}, u32[]{:S(2)}) collective-permute-start(bf16[768,1152]{1,0:T(8,128)(2,1)S(1)} %get-tuple-element.58.both), channel_id=1, source_target_pairs={{0,16},{1,17},{2,18},{3,19},{4,20},{5,21},{6,22},{7,23},{8,24},{9,... | collective-permute-start | bytes 5308424 | tf_op jit(solution)/shard_map/ppermute | solution.py:35
  8.5 5.1 %collective-permute-start.2 = (bf16[128,1152]{1,0:T(8,128)(2,1)S(1)}, bf16[128,1152]{1,0:T(8,128)(2,1)S(1)}, u32[]{:S(2)}, u32[]{:S(2)}) collective-permute-start(bf16[128,1152]{1,0:T(8,128)(2,1)S(1)} %get-tuple-element.62), channel_id=1, source_target_pairs={{0,224},{1,225},{2,226},{3,227},{4,228},{5,229},{6,230},{7,231},{8... | collective-permute-start | bytes 884744 | tf_op jit(solution)/shard_map/ppermute | solution.py:35
  13.6 5.1 %collective-permute-start.6 = (bf16[128,1152]{1,0:T(8,128)(2,1)S(1)}, bf16[128,1152]{1,0:T(8,128)(2,1)S(1)}, u32[]{:S(2)}, u32[]{:S(2)}) collective-permute-start(bf16[128,1152]{1,0:T(8,128)(2,1)S(1)} %get-tuple-element.64), channel_id=1, source_target_pairs={{0,224},{1,225},{2,226},{3,227},{4,228},{5,229},{6,230},{7,231},{8... | collective-permute-start | bytes 884744 | tf_op jit(solution)/shard_map/ppermute | solution.py:35
  18.7 1.7 %shard_map.77 = (f32[256,1152]{1,0:T(8,128)S(1)}, f32[256,1152]{1,0:T(8,128)S(1)}) custom-call(f32[2]{0:T(128)S(1)} %get-tuple-element.56.par, bf16[768,1152]{1,0:T(8,128)(2,1)S(1)} %get-tuple-element.58.both), custom_call_target="tpu_custom_call" | custom-call | bytes 4128768 | tf_op jit(solution)/shard_map/pallas_call | solution.py:48
  20.7 5.1 %collective-permute-start.3 = (bf16[128,1152]{1,0:T(8,128)(2,1)S(1)}, bf16[128,1152]{1,0:T(8,128)(2,1)S(1)}, u32[]{:S(2)}, u32[]{:S(2)}) collective-permute-start(bf16[128,1152]{1,0:T(8,128)(2,1)S(1)} %collective-permute-done.2.i1a), channel_id=1, source_target_pairs={{0,224},{1,225},{2,226},{3,227},{4,228},{5,229},{6,230},{7,231},{8... | collective-permute-start | bytes 884744 | tf_op jit(solution)/shard_map/ppermute | solution.py:35
  25.7 1.2 %collective-permute-done.4.t1b = bf16[128,1152]{1,0:T(8,128)(2,1)S(1)} collective-permute-done((bf16[128,1152]{1,0:T(8,128)(2,1)S(1)}, bf16[128,1152]{1,0:T(8,128)(2,1)S(1)}, u32[]{:S(2)}, u32[]{:S(2)}) %collective-permute-start.4) | collective-permute-done | bytes 294944 | tf_op jit(solution)/shard_map/ppermute | solution.py:35
  27.0 5.1 %collective-permute-start.8 = (bf16[128,1152]{1,0:T(8,128)(2,1)S(1)}, bf16[128,1152]{1,0:T(8,128)(2,1)S(1)}, u32[]{:S(2)}, u32[]{:S(2)}) collective-permute-start(bf16[128,1152]{1,0:T(8,128)(2,1)S(1)} %collective-permute-done.6.i1b), channel_id=1, source_target_pairs={{0,224},{1,225},{2,226},{3,227},{4,228},{5,229},{6,230},{7,231},{8... | collective-permute-start | bytes 884744 | tf_op jit(solution)/shard_map/ppermute | solution.py:35
  33.1 4.0 %shard_map.78 = (f32[256,1152]{1,0:T(8,128)S(1)}, f32[256,1152]{1,0:T(8,128)S(1)}, f32[256,1152]{1,0:T(8,128)S(1)}, f32[256,1152]{1,0:T(8,128)S(1)}) custom-call(f32[2]{0:T(128)S(1)} %get-tuple-element.56.par, bf16[128,1152]{1,0:T(8,128)(2,1)S(1)} %collective-permute-done.t1a, bf16[128,1152]{1,0:T(8,128)(2,1)S(1)} %collective-permute-done.4.t1b, ...), custom_call_target="tpu_custom_call" | custom-call | bytes 11796480 | tf_op jit(solution)/shard_map/pallas_call | solution.py:48
  37.1 1.6 %collective-permute-done.5.second = bf16[128,1152]{1,0:T(8,128)(2,1)S(1)} collective-permute-done((bf16[128,1152]{1,0:T(8,128)(2,1)S(1)}, bf16[128,1152]{1,0:T(8,128)(2,1)S(1)}, u32[]{:S(2)}, u32[]{:S(2)}) %collective-permute-start.5) | collective-permute-done | bytes 294944 | tf_op jit(solution)/shard_map/ppermute | solution.py:35
  38.8 1.5 %shard_map.81 = bf16[256,1152]{1,0:T(8,128)(2,1)S(1)} custom-call(f32[2]{0:T(128)S(1)} %get-tuple-element.56.par, bf16[128,1152]{1,0:T(8,128)(2,1)S(1)} %collective-permute-done.1.first, bf16[128,1152]{1,0:T(8,128)(2,1)S(1)} %collective-permute-done.5.second, bf16[768,1152]{1,0:T(8,128)(2,1)S(1)} %collective-permute-done.7.both_s, ...), custom_call_target="tpu_custom_call" | custom-call | bytes 4128768 | tf_op jit(solution)/shard_map/pallas_call | solution.py:48
  41.2 1.5 %shard_map.80.old = f32[256,1152]{1,0:T(8,128)S(1)} custom-call(f32[2]{0:T(128)S(1)} %get-tuple-element.56.par, bf16[128,1152]{1,0:T(8,128)(2,1)S(1)} %collective-permute-done.1.first, bf16[128,1152]{1,0:T(8,128)(2,1)S(1)} %collective-permute-done.5.second, bf16[768,1152]{1,0:T(8,128)(2,1)S(1)} %get-tuple-element.58.both, f32[256,1152]{1,0:T(8,128)S(1)} %get-tuple-element.75.old), custom_call_target="tpu_custom_call" | custom-call | bytes 4718592 | tf_op jit(solution)/shard_map/pallas_call | solution.py:48
  42.8 1.1 %shard_map.82 = (bf16[256,1152]{1,0:T(8,128)(2,1)S(1)}, bf16[256,576]{1,0:T(8,128)(2,1)S(1)}, bf16[256,576]{1,0:T(8,128)(2,1)S(1)}) custom-call(f32[2]{0:T(128)S(1)} %get-tuple-element.56.par, f32[256,1152]{1,0:T(8,128)S(1)} %shard_map.80.old, bf16[256,1152]{1,0:T(8,128)(2,1)S(1)} %collective-permute-done.9.given, f32[256,1152]{1,0:T(8,128)S(1)} %get-tuple-element.78.unit, ...), custom_call_target="tpu_custom_call" | custom-call | bytes 4129792 | tf_op jit(solution)/shard_map/pallas_call | solution.py:48
  45.1 1.1 %collective-permute-start.14 = (bf16[256,1152]{1,0:T(8,128)(2,1)S(1)}, bf16[256,1152]{1,0:T(8,128)(2,1)S(1)}, u32[]{:S(2)}, u32[]{:S(2)}) collective-permute-start(bf16[256,1152]{1,0:T(8,128)(2,1)S(1)} %shard_map.85), channel_id=1, source_target_pairs={{0,16},{1,17},{2,18},{3,19},{4,20},{5,21},{6,22},{7,23},{8,24},{9,... | collective-permute-start | bytes 1769480 | tf_op jit(solution)/shard_map/ppermute | solution.py:35
  46.2 1.3 %shard_map.83 = (bf16[144,1152]{1,0:T(8,128)(2,1)S(1)}, bf16[144,1152]{1,0:T(8,128)(2,1)S(1)}, bf16[144,1152]{1,0:T(8,128)(2,1)S(1)}, bf16[144,1152]{1,0:T(8,128)(2,1)S(1)}) custom-call(bf16[256,576]{1,0:T(8,128)(2,1)S(1)} %get-tuple-element.80.keep, bf16[256,576]{1,0:T(8,128)(2,1)S(1)} %collective-permute-done.10.other, ...), custom_call_target="tpu_custom_call" | custom-call | bytes 3096576 | tf_op jit(solution)/shard_map/pallas_call | solution.py:48
  47.5 1.3 %collective-permute-start.11 = (bf16[144,1152]{1,0:T(8,128)(2,1)S(1)}, bf16[144,1152]{1,0:T(8,128)(2,1)S(1)}, u32[]{:S(2)}, u32[]{:S(2)}) collective-permute-start(bf16[144,1152]{1,0:T(8,128)(2,1)S(1)} %get-tuple-element.85), channel_id=1, source_target_pairs={{0,64},{1,65},{2,66},{3,67},{4,68},{5,69},{6,70},{7,71},{8,72},{9,... | collective-permute-start | bytes 995336 | tf_op jit(solution)/shard_map/ppermute | solution.py:35
  49.2 2.3 %collective-permute-start.13 = (bf16[144,1152]{1,0:T(8,128)(2,1)S(1)}, bf16[144,1152]{1,0:T(8,128)(2,1)S(1)}, u32[]{:S(2)}, u32[]{:S(2)}) collective-permute-start(bf16[144,1152]{1,0:T(8,128)(2,1)S(1)} %get-tuple-element.87), channel_id=1, source_target_pairs={{0,96},{1,97},{2,98},{3,99},{4,100},{5,101},{6,102},{7,103},{8,104... | collective-permute-start | bytes 995336 | tf_op jit(solution)/shard_map/ppermute | solution.py:35
  51.4 1.5 %shard_map.86.old = f32[256,1152]{1,0:T(8,128)S(1)} custom-call(f32[2]{0:T(128)S(1)} %get-tuple-element.56.par, bf16[128,1152]{1,0:T(8,128)(2,1)S(1)} %collective-permute-done.3.first, bf16[128,1152]{1,0:T(8,128)(2,1)S(1)} %collective-permute-done.8.second, bf16[768,1152]{1,0:T(8,128)(2,1)S(1)} %get-tuple-element.58.both, f32[256,1152]{1,0:T(8,128)S(1)} %get-tuple-element.92.old), custom_call_target="tpu_custom_call" | custom-call | bytes 4718592 | tf_op jit(solution)/shard_map/pallas_call | solution.py:48
  53.2 2.0 %shard_map.84 = f32[256,1152]{1,0:T(8,128)} custom-call(bf16[256,1152]{1,0:T(8,128)(2,1)S(1)} %get-tuple-element.88.dproj, bf16[1152,1152]{1,0:T(8,128)(2,1)S(1)} %copy-done), custom_call_target="tpu_custom_call" | custom-call | bytes 4423680 | tf_op jit(solution)/shard_map/pallas_call | solution.py:48
  55.4 3.5 %collective-permute-done.12.c = bf16[144,1152]{1,0:T(8,128)(2,1)S(1)} collective-permute-done((bf16[144,1152]{1,0:T(8,128)(2,1)S(1)}, bf16[144,1152]{1,0:T(8,128)(2,1)S(1)}, u32[]{:S(2)}, u32[]{:S(2)}) %collective-permute-start.12) | collective-permute-done | bytes 331808 | tf_op jit(solution)/shard_map/ppermute | solution.py:35
  59.4 3.4 %collective-permute-start.16 = (bf16[72,576]{1,0:T(8,128)(2,1)S(1)}, bf16[72,576]{1,0:T(8,128)(2,1)S(1)}, u32[]{:S(2)}, u32[]{:S(2)}) collective-permute-start(bf16[72,576]{1,0:T(8,128)(2,1)S(1)} %get-tuple-element.100), channel_id=1, source_target_pairs={{0,1},{1,128},{2,3},{3,130},{4,5},{5,132},{6,7},{7,134},{8,9},{9,1... | collective-permute-start | bytes 248840 | tf_op jit(solution)/shard_map/ppermute | solution.py:35
  62.9 2.1 %shard_map.88 = f32[256,1152]{1,0:T(8,128)} custom-call(f32[2]{0:T(128)S(1)} %get-tuple-element.56.par, f32[256,1152]{1,0:T(8,128)S(1)} %shard_map.86.old, bf16[256,1152]{1,0:T(8,128)(2,1)S(1)} %collective-permute-done.14.given, bf16[256,1152]{1,0:T(8,128)(2,1)S(1)} %copy-done.1), custom_call_target="tpu_custom_call" | custom-call | bytes 3538944 | tf_op jit(solution)/shard_map/pallas_call | solution.py:48
  66.7 16.0 %all_to_all.10.parts = bf16[8,72,72]{2,1,0:T(8,128)(2,1)S(1)} all-to-all(bf16[8,72,72]{2,1,0:T(8,128)(2,1)S(1)} %shard_map.89), channel_id=1, replica_groups=mesh['yh'=2,'x'=4,'core'=2,'z'=8,'yl'=2] {'z'}, dimensions={0} | all-to-all | bytes 165888 | tf_op jit(solution)/shard_map/all_to_all | solution.py:390
  82.7 17.1 %all_to_all.11.parts = bf16[16,72,72]{2,1,0:T(8,128)(2,1)S(1)} all-to-all(bf16[16,72,72]{2,1,0:T(8,128)(2,1)S(1)} %shard_map.90), channel_id=1, replica_groups=mesh['yh'=2,'x'=4,'core'=2,'z'=8,'yl'=2] {'yh','x','core'}, dimensions={0} | all-to-all | bytes 331776 | tf_op jit(solution)/shard_map/all_to_all | solution.py:392
  (34 shorter events, 7.6 us)
Async XLA Ops:
  5.2 26.9 %collective-permute-start.7 = (bf16[768,1152]{1,0:T(8,128)(2,1)S(1)}, bf16[768,1152]{1,0:T(8,128)(2,1)S(1)}, u32[]{:S(2)}, u32[]{:S(2)}) collective-permute-start(bf16[768,1152]{1,0:T(8,128)(2,1)S(1)} %get-tuple-element.58.both), channel_id=1, source_target_pairs={{0,16},{1,17},{2,18},{3,19},{4,20},{5,21},{6,22},{7,23},{8,24},{9,... | collective-permute-start | bytes 5308424 | tf_op jit(solution)/shard_map/ppermute | solution.py:35
  8.5 12.2 %collective-permute-start = (bf16[128,1152]{1,0:T(8,128)(2,1)S(1)}, bf16[128,1152]{1,0:T(8,128)(2,1)S(1)}, u32[]{:S(2)}, u32[]{:S(2)}) collective-permute-start(bf16[128,1152]{1,0:T(8,128)(2,1)S(1)} %get-tuple-element.57), channel_id=1, source_target_pairs={{0,32},{1,33},{2,34},{3,35},{4,36},{5,37},{6,38},{7,39},{8,40},{9,... | collective-permute-start | bytes 884744 | tf_op jit(solution)/shard_map/ppermute | solution.py:35
  8.5 12.2 %collective-permute-start.2 = (bf16[128,1152]{1,0:T(8,128)(2,1)S(1)}, bf16[128,1152]{1,0:T(8,128)(2,1)S(1)}, u32[]{:S(2)}, u32[]{:S(2)}) collective-permute-start(bf16[128,1152]{1,0:T(8,128)(2,1)S(1)} %get-tuple-element.62), channel_id=1, source_target_pairs={{0,224},{1,225},{2,226},{3,227},{4,228},{5,229},{6,230},{7,231},{8... | collective-permute-start | bytes 884744 | tf_op jit(solution)/shard_map/ppermute | solution.py:35
  13.6 13.4 %collective-permute-start.4 = (bf16[128,1152]{1,0:T(8,128)(2,1)S(1)}, bf16[128,1152]{1,0:T(8,128)(2,1)S(1)}, u32[]{:S(2)}, u32[]{:S(2)}) collective-permute-start(bf16[128,1152]{1,0:T(8,128)(2,1)S(1)} %get-tuple-element.63), channel_id=1, source_target_pairs={{0,32},{1,33},{2,34},{3,35},{4,36},{5,37},{6,38},{7,39},{8,40},{9,... | collective-permute-start | bytes 884744 | tf_op jit(solution)/shard_map/ppermute | solution.py:35
  13.6 13.4 %collective-permute-start.6 = (bf16[128,1152]{1,0:T(8,128)(2,1)S(1)}, bf16[128,1152]{1,0:T(8,128)(2,1)S(1)}, u32[]{:S(2)}, u32[]{:S(2)}) collective-permute-start(bf16[128,1152]{1,0:T(8,128)(2,1)S(1)} %get-tuple-element.64), channel_id=1, source_target_pairs={{0,224},{1,225},{2,226},{3,227},{4,228},{5,229},{6,230},{7,231},{8... | collective-permute-start | bytes 884744 | tf_op jit(solution)/shard_map/ppermute | solution.py:35
  20.7 16.4 %collective-permute-start.1 = (bf16[128,1152]{1,0:T(8,128)(2,1)S(1)}, bf16[128,1152]{1,0:T(8,128)(2,1)S(1)}, u32[]{:S(2)}, u32[]{:S(2)}) collective-permute-start(bf16[128,1152]{1,0:T(8,128)(2,1)S(1)} %collective-permute-done.t1a), channel_id=1, source_target_pairs={{0,32},{1,33},{2,34},{3,35},{4,36},{5,37},{6,38},{7,39},{8,40},{9,... | collective-permute-start | bytes 884744 | tf_op jit(solution)/shard_map/ppermute | solution.py:35
  20.7 16.4 %collective-permute-start.3 = (bf16[128,1152]{1,0:T(8,128)(2,1)S(1)}, bf16[128,1152]{1,0:T(8,128)(2,1)S(1)}, u32[]{:S(2)}, u32[]{:S(2)}) collective-permute-start(bf16[128,1152]{1,0:T(8,128)(2,1)S(1)} %collective-permute-done.2.i1a), channel_id=1, source_target_pairs={{0,224},{1,225},{2,226},{3,227},{4,228},{5,229},{6,230},{7,231},{8... | collective-permute-start | bytes 884744 | tf_op jit(solution)/shard_map/ppermute | solution.py:35
  27.0 11.8 %collective-permute-start.5 = (bf16[128,1152]{1,0:T(8,128)(2,1)S(1)}, bf16[128,1152]{1,0:T(8,128)(2,1)S(1)}, u32[]{:S(2)}, u32[]{:S(2)}) collective-permute-start(bf16[128,1152]{1,0:T(8,128)(2,1)S(1)} %collective-permute-done.4.t1b), channel_id=1, source_target_pairs={{0,32},{1,33},{2,34},{3,35},{4,36},{5,37},{6,38},{7,39},{8,40},{9,... | collective-permute-start | bytes 884744 | tf_op jit(solution)/shard_map/ppermute | solution.py:35
  27.0 13.3 %collective-permute-start.8 = (bf16[128,1152]{1,0:T(8,128)(2,1)S(1)}, bf16[128,1152]{1,0:T(8,128)(2,1)S(1)}, u32[]{:S(2)}, u32[]{:S(2)}) collective-permute-start(bf16[128,1152]{1,0:T(8,128)(2,1)S(1)} %collective-permute-done.6.i1b), channel_id=1, source_target_pairs={{0,224},{1,225},{2,226},{3,227},{4,228},{5,229},{6,230},{7,231},{8... | collective-permute-start | bytes 884744 | tf_op jit(solution)/shard_map/ppermute | solution.py:35
  40.3 2.6 %collective-permute-start.9 = (bf16[256,1152]{1,0:T(8,128)(2,1)S(1)}, bf16[256,1152]{1,0:T(8,128)(2,1)S(1)}, u32[]{:S(2)}, u32[]{:S(2)}) collective-permute-start(bf16[256,1152]{1,0:T(8,128)(2,1)S(1)} %shard_map.81), channel_id=1, source_target_pairs={{0,16},{1,17},{2,18},{3,19},{4,20},{5,21},{6,22},{7,23},{8,24},{9,... | collective-permute-start | bytes 1769480 | tf_op jit(solution)/shard_map/ppermute | solution.py:35
  44.0 2.2 %collective-permute-start.10 = (bf16[256,576]{1,0:T(8,128)(2,1)S(1)}, bf16[256,576]{1,0:T(8,128)(2,1)S(1)}, u32[]{:S(2)}, u32[]{:S(2)}) collective-permute-start(bf16[256,576]{1,0:T(8,128)(2,1)S(1)} %get-tuple-element.81), channel_id=1, source_target_pairs={{0,16},{1,17},{2,18},{3,19},{4,20},{5,21},{6,22},{7,23},{8,24},{9,... | collective-permute-start | bytes 884744 | tf_op jit(solution)/shard_map/ppermute | solution.py:35
  45.1 10.2 %collective-permute-start.14 = (bf16[256,1152]{1,0:T(8,128)(2,1)S(1)}, bf16[256,1152]{1,0:T(8,128)(2,1)S(1)}, u32[]{:S(2)}, u32[]{:S(2)}) collective-permute-start(bf16[256,1152]{1,0:T(8,128)(2,1)S(1)} %shard_map.85), channel_id=1, source_target_pairs={{0,16},{1,17},{2,18},{3,19},{4,20},{5,21},{6,22},{7,23},{8,24},{9,... | collective-permute-start | bytes 1769480 | tf_op jit(solution)/shard_map/ppermute | solution.py:35
  47.5 7.9 %collective-permute-start.11 = (bf16[144,1152]{1,0:T(8,128)(2,1)S(1)}, bf16[144,1152]{1,0:T(8,128)(2,1)S(1)}, u32[]{:S(2)}, u32[]{:S(2)}) collective-permute-start(bf16[144,1152]{1,0:T(8,128)(2,1)S(1)} %get-tuple-element.85), channel_id=1, source_target_pairs={{0,64},{1,65},{2,66},{3,67},{4,68},{5,69},{6,70},{7,71},{8,72},{9,... | collective-permute-start | bytes 995336 | tf_op jit(solution)/shard_map/ppermute | solution.py:35
  48.8 10.1 %collective-permute-start.12 = (bf16[144,1152]{1,0:T(8,128)(2,1)S(1)}, bf16[144,1152]{1,0:T(8,128)(2,1)S(1)}, u32[]{:S(2)}, u32[]{:S(2)}) collective-permute-start(bf16[144,1152]{1,0:T(8,128)(2,1)S(1)} %get-tuple-element.86), channel_id=1, source_target_pairs={{0,32},{1,33},{2,34},{3,35},{4,36},{5,37},{6,38},{7,39},{8,40},{9,... | collective-permute-start | bytes 995336 | tf_op jit(solution)/shard_map/ppermute | solution.py:35
  49.2 9.7 %collective-permute-start.13 = (bf16[144,1152]{1,0:T(8,128)(2,1)S(1)}, bf16[144,1152]{1,0:T(8,128)(2,1)S(1)}, u32[]{:S(2)}, u32[]{:S(2)}) collective-permute-start(bf16[144,1152]{1,0:T(8,128)(2,1)S(1)} %get-tuple-element.87), channel_id=1, source_target_pairs={{0,96},{1,97},{2,98},{3,99},{4,100},{5,101},{6,102},{7,103},{8,104... | collective-permute-start | bytes 995336 | tf_op jit(solution)/shard_map/ppermute | solution.py:35
  51.4 1.7 %copy-start = (bf16[1152,1152]{1,0:T(8,128)(2,1)S(1)}, bf16[1152,1152]{1,0:T(8,128)(2,1)}, u32[]{:S(2)}) copy-start(bf16[1152,1152]{1,0:T(8,128)(2,1)} %head.3) | copy-start | bytes 7962628
  55.2 7.6 %copy-start.1 = (bf16[256,1152]{1,0:T(8,128)(2,1)S(1)}, bf16[256,1152]{1,0:T(8,128)(2,1)}, u32[]{:S(2)}) copy-start(bf16[256,1152]{1,0:T(8,128)(2,1)} %texts.3) | copy-start | bytes 1769476
  59.3 5.6 %collective-permute-start.15 = (bf16[72,576]{1,0:T(8,128)(2,1)S(1)}, bf16[72,576]{1,0:T(8,128)(2,1)S(1)}, u32[]{:S(2)}, u32[]{:S(2)}) collective-permute-start(bf16[72,576]{1,0:T(8,128)(2,1)S(1)} %get-tuple-element.99), channel_id=1, source_target_pairs={{0,128},{1,129},{2,130},{3,131},{4,132},{5,133},{6,134},{7,135},{8... | collective-permute-start | bytes 248840 | tf_op jit(solution)/shard_map/ppermute | solution.py:35
  59.4 6.2 %collective-permute-start.16 = (bf16[72,576]{1,0:T(8,128)(2,1)S(1)}, bf16[72,576]{1,0:T(8,128)(2,1)S(1)}, u32[]{:S(2)}, u32[]{:S(2)}) collective-permute-start(bf16[72,576]{1,0:T(8,128)(2,1)S(1)} %get-tuple-element.100), channel_id=1, source_target_pairs={{0,1},{1,128},{2,3},{3,130},{4,5},{5,132},{6,7},{7,134},{8,9},{9,1... | collective-permute-start | bytes 248840 | tf_op jit(solution)/shard_map/ppermute | solution.py:35
  62.9 3.7 %collective-permute-start.17 = (bf16[72,576]{1,0:T(8,128)(2,1)S(1)}, bf16[72,576]{1,0:T(8,128)(2,1)S(1)}, u32[]{:S(2)}, u32[]{:S(2)}) collective-permute-start(bf16[72,576]{1,0:T(8,128)(2,1)S(1)} %get-tuple-element.101), channel_id=1, source_target_pairs={{0,129},{1,0},{2,131},{3,2},{4,133},{5,4},{6,135},{7,6},{8,137},{9... | collective-permute-start | bytes 248840 | tf_op jit(solution)/shard_map/ppermute | solution.py:35

commit v6 on v5

--- a/solution.py
+++ b/solution.py
@@ -21,6 +21,11 @@
 def chip_pairs(steps):
     shift = steps * SIZES[2] * INNER
     return [(source, (source + shift) % COUNT) for source in range(COUNT)]
+
+
+def mixed_pairs(kind):
+    ahead, back = chip_pairs(1), chip_pairs(-1)
+    return [(ahead if (k // INNER) % 2 == kind else back)[k] for k in range(COUNT)]
 
 
 def core_pairs(only=None):
@@ -65,8 +70,12 @@
     return 1.0 / (1.0 + jnp.exp(-x))
 
 
+def logits(par, rows, cols):
+    return par[0:1, 0:1] * mm(rows, cols, (1, 1)) + par[1:2, 0:1]
+
+
 def applied(par, rows, cols):
-    logit = par[0] * mm(rows, cols, (1, 1)) + par[1]
+    logit = logits(par, rows, cols)
     return mm(sigmoid(logit).astype(BF), cols, (1, 0))
 
 
@@ -88,7 +97,7 @@
 
 def start_body(
     scale, bias, images, texts, head, par,
-    ta, tb, ia, ib, both, unit, norm, t_in, i_in, h_in, sems,
+    p1a, p1b, p2a, p2b, both, unit, norm, t_in, i_in, h_in, sems,
 ):
     copies = [
         pltpu.make_async_copy(texts, t_in, sems.at[0]),
@@ -99,13 +108,13 @@
         copies.append(pltpu.make_async_copy(head.at[rows], h_in.at[rows], sems.at[2 + k]))
     for copy in copies:
         copy.start()
-    par[0] = scale[0]
-    par[1] = bias[0]
+    par[0:1] = jnp.full((1, par.shape[1]), scale[0], F32)
+    par[1:2] = jnp.full((1, par.shape[1]), bias[0], F32)
     copies[0].wait()
     count = t_in.shape[0]
     low = text_unit(t_in[...])[0].astype(BF)
-    halved(low, ta, tb)
     both[:count] = low
+    low_txt = low
     copies[1].wait()
     both[2 * count :] = i_in[...]
     proj = None
@@ -119,8 +128,17 @@
     unit[...] = value
     norm[...] = inverse
     low = value.astype(BF)
-    halved(low, ia, ib)
     both[count : 2 * count] = low
+
+    @pl.when(lax.axis_index("core") == 0)
+    def _():
+        halved(low_txt, p1a, p1b)
+        halved(low, p2a, p2b)
+
+    @pl.when(lax.axis_index("core") != 0)
+    def _():
+        halved(low, p1a, p1b)
+        halved(low_txt, p2a, p2b)
 
 
 def text_of(both):
@@ -144,7 +162,7 @@
 
 def home_body(par, both, dimg, dtxt):
     img_b, txt_b = image_of(both), text_of(both)
-    logit = par[0] * mm(img_b, txt_b, (1, 1)) + par[1]
+    logit = logits(par, img_b, txt_b)
     eye = lax.broadcasted_iota(jnp.int32, logit.shape, 0) == lax.broadcasted_iota(
         jnp.int32, logit.shape, 1
     )
@@ -153,12 +171,13 @@
     dtxt[...] = mm(grad, img_b, (0, 0))
 
 
-def joined(first, second):
-    return jnp.concatenate([first[...], second[...]], 0)
-
-
-def near_body(par, t1a, t1b, i1a, i1b, both, both_s, dimg, dtxt, dimg_o, dtxt_o, dimg_s, dtxt_s):
-    t1, i1 = joined(t1a, t1b), joined(i1a, i1b)
+def joined(one, two, kind):
+    here = lax.axis_index("core") == kind
+    return jnp.concatenate([jnp.where(here, a[...], b[...]) for a, b in zip(one, two)], 0)
+
+
+def near_body(par, p1a, p1b, p2a, p2b, both, both_s, dimg, dtxt, dimg_o, dtxt_o, dimg_s, dtxt_s):
+    t1, i1 = (joined((p1a, p1b), (p2a, p2b), kind) for kind in range(2))
     dimg_o[...] = dimg[...] + applied(par, image_of(both), t1)
     dtxt_o[...] = dtxt[...] + applied(par, text_of(both), i1)
     dimg_s[...] = applied(par, image_of(both_s), t1)
@@ -173,22 +192,22 @@
         dimg_o[...] += applied(par, image_of(both), text_of(both_s))
 
 
-def give_body(giver, rows_of, par, first, second, both_s, old, out):
+def give_body(giver, kind, rows_of, par, p1a, p1b, p2a, p2b, both_s, old, out):
     @pl.when(lax.axis_index("core") == giver)
     def _():
-        out[...] = (old[...] + applied(par, rows_of(both_s), joined(first, second))).astype(BF)
+        out[...] = (old[...] + applied(par, rows_of(both_s), joined((p1a, p1b), (p2a, p2b), kind))).astype(BF)
 
     @pl.when(lax.axis_index("core") != giver)
     def _():
         out[...] = old[...].astype(BF)
 
 
-def far_body(rows_of, par, first, second, both, old, out):
-    out[...] = old[...] + applied(par, rows_of(both), joined(first, second))
+def far_body(kind, rows_of, par, p1a, p1b, p2a, p2b, both, old, out):
+    out[...] = old[...] + applied(par, rows_of(both), joined((p1a, p1b), (p2a, p2b), kind))
 
 
 def image_end_body(par, old, given, unit, norm, whole, keep, send):
-    dimg = par[0] * (old[...] + given[...].astype(F32))
+    dimg = par[0:1, 0:1] * (old[...] + given[...].astype(F32))
     value = unit[...]
     dproj = ((dimg - value * jnp.sum(value * dimg, -1, keepdims=True)) * norm[...]).astype(BF)
     whole[...] = dproj
@@ -206,7 +225,7 @@
 
 
 def text_end_body(par, old, given, texts, out):
-    dtxt = par[0] * (old[...] + given[...].astype(F32))
+    dtxt = par[0:1, 0:1] * (old[...] + given[...].astype(F32))
     value, inverse = text_unit(texts[...])
     out[...] = (dtxt - value * jnp.sum(value * dtxt, -1, keepdims=True)) * inverse
 
@@ -314,49 +333,47 @@
 
 
 def on_device(images, texts, head, scale, bias):
-    ahead, back, swap = chip_pairs(1), chip_pairs(-1), core_pairs()
+    swap = core_pairs()
     count, width = images.shape
     half = width // 2
     big = (count, width)
     tie = lax.optimization_barrier
 
     part_of = ((count // 2, width), BF)
-    par, ta, tb, ia, ib, both, unit_img, pnorm = call(
+    par, p1a, p1b, p2a, p2b, both, unit_img, pnorm = call(
         start_body,
-        [((2,), F32)] + [part_of] * 4 + [((3 * count, width), BF), (big, F32), ((count, 1), F32)],
-        images, texts, head, scalars=(scale, bias), small=1, space=pltpu.HBM, limit=16,
+        [((2, 128), F32)] + [part_of] * 4 + [((3 * count, width), BF), (big, F32), ((count, 1), F32)],
+        images, texts, head, scalars=(scale, bias), space=pltpu.HBM, limit=16,
         scratch=[
             pltpu.VMEM(big, BF), pltpu.VMEM(big, BF), pltpu.VMEM(head.shape, BF),
             pltpu.SemaphoreType.DMA((1 + len(CUTS),)),
         ],
     )
-    t1 = [moved(ta, ahead), moved(tb, ahead)]
-    i1 = [moved(ia, back), moved(ib, back)]
+    ways = (mixed_pairs(0), mixed_pairs(1))
+    near = [moved(p1a, ways[0]), moved(p2a, ways[1]), moved(p1b, ways[0]), moved(p2b, ways[1])]
     both_s = moved(both, swap)
-    dimg, dtxt = call(home_body, [(big, F32)] * 2, both, scalars=(par,))
-    t1[0], dimg, dtxt = tie((t1[0], dimg, dtxt))
+    dimg, dtxt = call(home_body, [(big, F32)] * 2, par, both)
+    near[0], dimg, dtxt = tie((near[0], dimg, dtxt))
     ordered, ordered2 = call(order_body, [(big, BF)] * 2, both, both_s)
-    t2 = [moved(t, ahead) for t in t1]
-    i2 = [moved(i, back) for i in i1]
+    far = [moved(p, ways[k % 2]) for k, p in enumerate(near)]
     dimg, dtxt, dimg_s, dtxt_s = call(
-        near_body, [(big, F32)] * 4, *t1, *i1, both, both_s, dimg, dtxt, scalars=(par,)
-    )
-    t2[0], i2[0], t2[1], dimg, dtxt, dimg_s, dtxt_s, ordered, ordered2 = tie(
-        (t2[0], i2[0], t2[1], dimg, dtxt, dimg_s, dtxt_s, ordered, ordered2)
-    )
+        near_body, [(big, F32)] * 4, par, near[0], near[2], near[1], near[3], both, both_s, dimg, dtxt
+    )
+    *far, dimg, dtxt, dimg_s, dtxt_s, ordered, ordered2 = tie(
+        (*far, dimg, dtxt, dimg_s, dtxt_s, ordered, ordered2)
+    )
+    far = [far[0], far[2], far[1], far[3]]
 
     (give,) = call(
-        functools.partial(give_body, 1, image_of), [(big, BF)], *t2, both_s, dimg_s,
-        scalars=(par,),
-    )
-    i2[1], give = tie((i2[1], give))
+        functools.partial(give_body, 1, 0, image_of), [(big, BF)], par, *far, both_s, dimg_s
+    )
     given = moved(give, swap)
     (dimg,) = call(
-        functools.partial(far_body, image_of), [(big, F32)], *t2, both, dimg, scalars=(par,)
+        functools.partial(far_body, 0, image_of), [(big, F32)], par, *far, both, dimg
     )
     dproj, keep, send = call(
         image_end_body, [(big, BF), ((count, half), BF), ((count, half), BF)],
-        dimg, given, unit_img, pnorm, scalars=(par,),
+        par, dimg, given, unit_img, pnorm,
     )
     other = moved(send, swap)
     quarter = ((half // 4, width), BF)
@@ -368,11 +385,10 @@
     parts = parts[:1] + [moved(p, ring_pairs(t, 0)) for p, t in zip(parts[1:], TURNS[1:])]
     (grad_image,) = call(grad_image_body, [(big, F32)], dproj, head)
     (give,) = call(
-        functools.partial(give_body, 0, text_of), [(big, BF)], *i2, both_s, dtxt_s,
-        scalars=(par,),
+        functools.partial(give_body, 0, 1, text_of), [(big, BF)], par, *far, both_s, dtxt_s
     )
     (dtxt,) = call(
-        functools.partial(far_body, text_of), [(big, F32)], *i2, both, dtxt, scalars=(par,)
+        functools.partial(far_body, 1, text_of), [(big, F32)], par, *far, both, dtxt
     )
     given_txt = moved(give, swap)
     *parts, grad_image, given_txt, dtxt = tie((*parts, grad_image, given_txt, dtxt))
@@ -383,7 +399,7 @@
     )
     parts = list(parts)
     parts = parts[:1] + [moved(p, ring_pairs(t, 1)) for p, t in zip(parts[1:], TURNS[1:])]
-    (grad_text,) = call(text_end_body, [(big, F32)], dtxt, given_txt, texts, scalars=(par,))
+    (grad_text,) = call(text_end_body, [(big, F32)], par, dtxt, given_txt, texts)
     *parts, grad_text = tie((*parts, grad_text))
     own = width // INNER
     (part,) = call(split_body, [((SIZES[3], half // 8, own), BF)], *parts)

time: 101 us -> 99.2 us (0.982)
  waiting for transfers between devices: 8.64 us -> 13.2 us
  Pallas kernels: 23.1 us -> 19 us
  starting transfers between devices: 33.6 us -> 31.2 us
    ppermute x18, waiting for transfers between devices: 8.64 us -> 13.2 us  [moved(): return lax.ppermute(value, AXES, pairs)]
    pallas_call x16, Pallas kernels: 23.1 us -> 19 us  [call(): pl.pallas_call(body, out_shape=shapes, in_specs=in_specs, out_specs=[pl.B...]
    ppermute x18, starting transfers between devices: 33.6 us -> 31.2 us  [moved(): return lax.ppermute(value, AXES, pairs)]
  transfers between devices with their start and end apart: 18 -> 18, of which waited for: 8 -> 8; matrix products, arithmetic and copies ran while one was open for 0% -> 0% of each run, Pallas kernels for 17% -> 13%
where the time goes in v6:
time: 99.2 us; the launch traced here: 98.5 us
  blocking collectives  32.4 us (33%)
  starting transfers between devices  31.2 us (31%)
  Pallas kernels  19 us (19%)
  waiting for transfers between devices  13.2 us (13%)
  between operations  2.06 us (2%)
    ppermute x18, starting transfers between devices, moved(): return lax.ppermute(value, AXES, pairs)  31.2 us
    pallas_call x16, Pallas kernels, call(): pl.pallas_call(body, out_shape=shapes, in_specs=in_specs, out_specs=[pl.B...  19 us
    all_to_all x1, blocking collectives, on_device(): part = lax.all_to_all(part, ('yh', 'x', 'core'), 0, 0)  16.5 us
    all_to_all x1, blocking collectives, on_device(): part = lax.all_to_all(part, 'z', 0, 0)  15.9 us
    ppermute x18, waiting for transfers between devices, moved(): return lax.ppermute(value, AXES, pairs)  13.2 us
  transfers between devices with their start and end apart: 18, of which 8 were waited for; matrix products, arithmetic and copies ran while one was open for 0% of the time, Pallas kernels for 13%

profile of v6, /device:TPU:1, one launch (start us, length us, event | category | flops | bytes accessed | tf_op | source)
XLA Modules:
  0.0 98.5 jit_solution(2710566205002183020)
XLA Ops:
  1.9 3.3 %shard_map.76 = (f32[2,128]{1,0:T(2,128)S(1)}, bf16[128,1152]{1,0:T(8,128)(2,1)S(1)}, bf16[128,1152]{1,0:T(8,128)(2,1)S(1)}, bf16[128,1152]{1,0:T(8,128)(2,1)S(1...) custom-call(f32[1]{0:T(128)S(6)} %copy.8.scale, ...), custom_call_target="tpu_custom_call" | custom-call | bytes 7964672 | tf_op jit(solution)/shard_map/pallas_call | solution.py:53
  5.2 3.3 %collective-permute-start.8 = (bf16[768,1152]{1,0:T(8,128)(2,1)S(1)}, bf16[768,1152]{1,0:T(8,128)(2,1)S(1)}, u32[]{:S(2)}, u32[]{:S(2)}) collective-permute-start(bf16[768,1152]{1,0:T(8,128)(2,1)S(1)} %get-tuple-element.57.both), channel_id=1, source_target_pairs={{0,16},{1,17},{2,18},{3,19},{4,20},{5,21},{6,22},{7,23},{8,24},{9,... | collective-permute-start | bytes 5308424 | tf_op jit(solution)/shard_map/ppermute | solution.py:40
  8.6 3.4 %collective-permute-start = (bf16[128,1152]{1,0:T(8,128)(2,1)S(1)}, bf16[128,1152]{1,0:T(8,128)(2,1)S(1)}, u32[]{:S(2)}, u32[]{:S(2)}) collective-permute-start(bf16[128,1152]{1,0:T(8,128)(2,1)S(1)} %get-tuple-element.56), channel_id=1, source_target_pairs={{0,32},{1,33},{2,34},{3,35},{4,36},{5,37},{6,38},{7,39},{8,40},{9,... | collective-permute-start | bytes 884744 | tf_op jit(solution)/shard_map/ppermute | solution.py:40
  11.9 5.1 %collective-permute-start.4 = (bf16[128,1152]{1,0:T(8,128)(2,1)S(1)}, bf16[128,1152]{1,0:T(8,128)(2,1)S(1)}, u32[]{:S(2)}, u32[]{:S(2)}) collective-permute-start(bf16[128,1152]{1,0:T(8,128)(2,1)S(1)} %get-tuple-element.62), channel_id=1, source_target_pairs={{0,32},{1,33},{2,34},{3,35},{4,36},{5,37},{6,38},{7,39},{8,40},{9,... | collective-permute-start | bytes 884744 | tf_op jit(solution)/shard_map/ppermute | solution.py:40
  17.0 1.1 %shard_map.77 = (f32[256,1152]{1,0:T(8,128)S(1)}, f32[256,1152]{1,0:T(8,128)S(1)}) custom-call(f32[2,128]{1,0:T(2,128)S(1)} %get-tuple-element.55.par, bf16[768,1152]{1,0:T(8,128)(2,1)S(1)} %get-tuple-element.57.both), custom_call_target="tpu_custom_call" | custom-call | bytes 4129792 | tf_op jit(solution)/shard_map/pallas_call | solution.py:53
  18.2 5.2 %collective-permute-start.1 = (bf16[128,1152]{1,0:T(8,128)(2,1)S(1)}, bf16[128,1152]{1,0:T(8,128)(2,1)S(1)}, u32[]{:S(2)}, u32[]{:S(2)}) collective-permute-start(bf16[128,1152]{1,0:T(8,128)(2,1)S(1)} %collective-permute-done.p1a), channel_id=1, source_target_pairs={{0,32},{1,33},{2,34},{3,35},{4,36},{5,37},{6,38},{7,39},{8,40},{9,... | collective-permute-start | bytes 884744 | tf_op jit(solution)/shard_map/ppermute | solution.py:40
  23.3 5.6 %collective-permute-start.5 = (bf16[128,1152]{1,0:T(8,128)(2,1)S(1)}, bf16[128,1152]{1,0:T(8,128)(2,1)S(1)}, u32[]{:S(2)}, u32[]{:S(2)}) collective-permute-start(bf16[128,1152]{1,0:T(8,128)(2,1)S(1)} %collective-permute-done.4.p1b), channel_id=1, source_target_pairs={{0,32},{1,33},{2,34},{3,35},{4,36},{5,37},{6,38},{7,39},{8,40},{9,... | collective-permute-start | bytes 884744 | tf_op jit(solution)/shard_map/ppermute | solution.py:40
  29.0 1.0 %shard_map.79 = (bf16[256,1152]{1,0:T(8,128)(2,1)S(1)}, bf16[256,1152]{1,0:T(8,128)(2,1)S(1)}) custom-call(bf16[768,1152]{1,0:T(8,128)(2,1)S(1)} %get-tuple-element.57.both, bf16[768,1152]{1,0:T(8,128)(2,1)S(1)} %collective-permute-done.8.both_s), custom_call_target="tpu_custom_call" | custom-call | bytes 4718592 | tf_op jit(solution)/shard_map/pallas_call | solution.py:53
  30.0 3.5 %shard_map.78 = (f32[256,1152]{1,0:T(8,128)S(1)}, f32[256,1152]{1,0:T(8,128)S(1)}, f32[256,1152]{1,0:T(8,128)S(1)}, f32[256,1152]{1,0:T(8,128)S(1)}) custom-call(f32[2,128]{1,0:T(2,128)S(1)} %get-tuple-element.55.par, bf16[128,1152]{1,0:T(8,128)(2,1)S(1)} %collective-permute-done.p1a, bf16[128,1152]{1,0:T(8,128)(2,1)S(1)} %collective-permute-done.4.p1b, ...), custom_call_target="tpu_custom_call" | custom-call | bytes 11797504 | tf_op jit(solution)/shard_map/pallas_call | solution.py:53
  33.5 1.6 %collective-permute-done.3.p2a = bf16[128,1152]{1,0:T(8,128)(2,1)S(1)} collective-permute-done((bf16[128,1152]{1,0:T(8,128)(2,1)S(1)}, bf16[128,1152]{1,0:T(8,128)(2,1)S(1)}, u32[]{:S(2)}, u32[]{:S(2)}) %collective-permute-start.3) | collective-permute-done | bytes 294944 | tf_op jit(solution)/shard_map/ppermute | solution.py:40
  36.0 4.5 %collective-permute-done.7.p2b = bf16[128,1152]{1,0:T(8,128)(2,1)S(1)} collective-permute-done((bf16[128,1152]{1,0:T(8,128)(2,1)S(1)}, bf16[128,1152]{1,0:T(8,128)(2,1)S(1)}, u32[]{:S(2)}, u32[]{:S(2)}) %collective-permute-start.7) | collective-permute-done | bytes 294944 | tf_op jit(solution)/shard_map/ppermute | solution.py:40
  41.5 0.9 shard_map.80.old
  42.4 1.0 %collective-permute-done.9.given = bf16[256,1152]{1,0:T(8,128)(2,1)S(1)} collective-permute-done((bf16[256,1152]{1,0:T(8,128)(2,1)S(1)}, bf16[256,1152]{1,0:T(8,128)(2,1)S(1)}, u32[]{:S(2)}, u32[]{:S(2)}) %collective-permute-start.9) | collective-permute-done | bytes 589856 | tf_op jit(solution)/shard_map/ppermute | solution.py:40
  44.4 1.4 %collective-permute-start.14 = (bf16[256,1152]{1,0:T(8,128)(2,1)S(1)}, bf16[256,1152]{1,0:T(8,128)(2,1)S(1)}, u32[]{:S(2)}, u32[]{:S(2)}) collective-permute-start(bf16[256,1152]{1,0:T(8,128)(2,1)S(1)} %shard_map.85), channel_id=1, source_target_pairs={{0,16},{1,17},{2,18},{3,19},{4,20},{5,21},{6,22},{7,23},{8,24},{9,... | collective-permute-start | bytes 1769480 | tf_op jit(solution)/shard_map/ppermute | solution.py:40
  45.8 1.3 %shard_map.83 = (bf16[144,1152]{1,0:T(8,128)(2,1)S(1)}, bf16[144,1152]{1,0:T(8,128)(2,1)S(1)}, bf16[144,1152]{1,0:T(8,128)(2,1)S(1)}, bf16[144,1152]{1,0:T(8,128)(2,1)S(1)}) custom-call(bf16[256,576]{1,0:T(8,128)(2,1)S(1)} %get-tuple-element.80.keep, bf16[256,576]{1,0:T(8,128)(2,1)S(1)} %collective-permute-done.10.other, ...), custom_call_target="tpu_custom_call" | custom-call | bytes 3096576 | tf_op jit(solution)/shard_map/pallas_call | solution.py:53
  47.2 1.4 %collective-permute-start.11 = (bf16[144,1152]{1,0:T(8,128)(2,1)S(1)}, bf16[144,1152]{1,0:T(8,128)(2,1)S(1)}, u32[]{:S(2)}, u32[]{:S(2)}) collective-permute-start(bf16[144,1152]{1,0:T(8,128)(2,1)S(1)} %get-tuple-element.85), channel_id=1, source_target_pairs={{0,64},{1,65},{2,66},{3,67},{4,68},{5,69},{6,70},{7,71},{8,72},{9,... | collective-permute-start | bytes 995336 | tf_op jit(solution)/shard_map/ppermute | solution.py:40
  48.8 2.4 %collective-permute-start.13 = (bf16[144,1152]{1,0:T(8,128)(2,1)S(1)}, bf16[144,1152]{1,0:T(8,128)(2,1)S(1)}, u32[]{:S(2)}, u32[]{:S(2)}) collective-permute-start(bf16[144,1152]{1,0:T(8,128)(2,1)S(1)} %get-tuple-element.87), channel_id=1, source_target_pairs={{0,96},{1,97},{2,98},{3,99},{4,100},{5,101},{6,102},{7,103},{8,104... | collective-permute-start | bytes 995336 | tf_op jit(solution)/shard_map/ppermute | solution.py:40
  53.0 2.0 %shard_map.84 = f32[256,1152]{1,0:T(8,128)} custom-call(bf16[256,1152]{1,0:T(8,128)(2,1)S(1)} %get-tuple-element.88.dproj, bf16[1152,1152]{1,0:T(8,128)(2,1)S(1)} %copy-done), custom_call_target="tpu_custom_call" | custom-call | bytes 4423680 | tf_op jit(solution)/shard_map/pallas_call | solution.py:53
  55.1 3.5 %collective-permute-done.12.c = bf16[144,1152]{1,0:T(8,128)(2,1)S(1)} collective-permute-done((bf16[144,1152]{1,0:T(8,128)(2,1)S(1)}, bf16[144,1152]{1,0:T(8,128)(2,1)S(1)}, u32[]{:S(2)}, u32[]{:S(2)}) %collective-permute-start.12) | collective-permute-done | bytes 331808 | tf_op jit(solution)/shard_map/ppermute | solution.py:40
  60.0 1.8 %collective-permute-start.17 = (bf16[72,576]{1,0:T(8,128)(2,1)S(1)}, bf16[72,576]{1,0:T(8,128)(2,1)S(1)}, u32[]{:S(2)}, u32[]{:S(2)}) collective-permute-start(bf16[72,576]{1,0:T(8,128)(2,1)S(1)} %get-tuple-element.99), channel_id=1, source_target_pairs={{0,129},{1,0},{2,131},{3,2},{4,133},{5,4},{6,135},{7,6},{8,137},{9... | collective-permute-start | bytes 248840 | tf_op jit(solution)/shard_map/ppermute | solution.py:40
  61.9 1.6 %shard_map.88 = f32[256,1152]{1,0:T(8,128)} custom-call(f32[2,128]{1,0:T(2,128)S(1)} %get-tuple-element.55.par, f32[256,1152]{1,0:T(8,128)S(1)} %shard_map.86.old, bf16[256,1152]{1,0:T(8,128)(2,1)S(1)} %collective-permute-done.14.given, bf16[256,1152]{1,0:T(8,128)(2,1)S(1)} %copy-done.1), custom_call_target="tpu_custom_call" | custom-call | bytes 3539968 | tf_op jit(solution)/shard_map/pallas_call | solution.py:53
  64.1 1.0 collective-permute-done.16.c
  65.2 15.9 %all_to_all.10.parts = bf16[8,72,72]{2,1,0:T(8,128)(2,1)S(1)} all-to-all(bf16[8,72,72]{2,1,0:T(8,128)(2,1)S(1)} %shard_map.89), channel_id=1, replica_groups=mesh['yh'=2,'x'=4,'core'=2,'z'=8,'yl'=2] {'z'}, dimensions={0} | all-to-all | bytes 165888 | tf_op jit(solution)/shard_map/all_to_all | solution.py:406
  81.1 16.5 %all_to_all.11.parts = bf16[16,72,72]{2,1,0:T(8,128)(2,1)S(1)} all-to-all(bf16[16,72,72]{2,1,0:T(8,128)(2,1)S(1)} %shard_map.90), channel_id=1, replica_groups=mesh['yh'=2,'x'=4,'core'=2,'z'=8,'yl'=2] {'yh','x','core'}, dimensions={0} | all-to-all | bytes 331776 | tf_op jit(solution)/shard_map/all_to_all | solution.py:408
  (34 shorter events, 8.1 us)
Async XLA Ops:
  5.2 23.7 %collective-permute-start.8 = (bf16[768,1152]{1,0:T(8,128)(2,1)S(1)}, bf16[768,1152]{1,0:T(8,128)(2,1)S(1)}, u32[]{:S(2)}, u32[]{:S(2)}) collective-permute-start(bf16[768,1152]{1,0:T(8,128)(2,1)S(1)} %get-tuple-element.57.both), channel_id=1, source_target_pairs={{0,16},{1,17},{2,18},{3,19},{4,20},{5,21},{6,22},{7,23},{8,24},{9,... | collective-permute-start | bytes 5308424 | tf_op jit(solution)/shard_map/ppermute | solution.py:40
  8.6 9.6 %collective-permute-start = (bf16[128,1152]{1,0:T(8,128)(2,1)S(1)}, bf16[128,1152]{1,0:T(8,128)(2,1)S(1)}, u32[]{:S(2)}, u32[]{:S(2)}) collective-permute-start(bf16[128,1152]{1,0:T(8,128)(2,1)S(1)} %get-tuple-element.56), channel_id=1, source_target_pairs={{0,32},{1,33},{2,34},{3,35},{4,36},{5,37},{6,38},{7,39},{8,40},{9,... | collective-permute-start | bytes 884744 | tf_op jit(solution)/shard_map/ppermute | solution.py:40
  11.9 11.4 %collective-permute-start.2 = (bf16[128,1152]{1,0:T(8,128)(2,1)S(1)}, bf16[128,1152]{1,0:T(8,128)(2,1)S(1)}, u32[]{:S(2)}, u32[]{:S(2)}) collective-permute-start(bf16[128,1152]{1,0:T(8,128)(2,1)S(1)} %get-tuple-element.61), channel_id=1, source_target_pairs={{0,224},{1,225},{2,226},{3,227},{4,228},{5,229},{6,230},{7,231},{8... | collective-permute-start | bytes 884744 | tf_op jit(solution)/shard_map/ppermute | solution.py:40
  11.9 11.4 %collective-permute-start.4 = (bf16[128,1152]{1,0:T(8,128)(2,1)S(1)}, bf16[128,1152]{1,0:T(8,128)(2,1)S(1)}, u32[]{:S(2)}, u32[]{:S(2)}) collective-permute-start(bf16[128,1152]{1,0:T(8,128)(2,1)S(1)} %get-tuple-element.62), channel_id=1, source_target_pairs={{0,32},{1,33},{2,34},{3,35},{4,36},{5,37},{6,38},{7,39},{8,40},{9,... | collective-permute-start | bytes 884744 | tf_op jit(solution)/shard_map/ppermute | solution.py:40
  17.0 12.0 %collective-permute-start.6 = (bf16[128,1152]{1,0:T(8,128)(2,1)S(1)}, bf16[128,1152]{1,0:T(8,128)(2,1)S(1)}, u32[]{:S(2)}, u32[]{:S(2)}) collective-permute-start(bf16[128,1152]{1,0:T(8,128)(2,1)S(1)} %get-tuple-element.63), channel_id=1, source_target_pairs={{0,224},{1,225},{2,226},{3,227},{4,228},{5,229},{6,230},{7,231},{8... | collective-permute-start | bytes 884744 | tf_op jit(solution)/shard_map/ppermute | solution.py:40
  18.2 15.4 %collective-permute-start.1 = (bf16[128,1152]{1,0:T(8,128)(2,1)S(1)}, bf16[128,1152]{1,0:T(8,128)(2,1)S(1)}, u32[]{:S(2)}, u32[]{:S(2)}) collective-permute-start(bf16[128,1152]{1,0:T(8,128)(2,1)S(1)} %collective-permute-done.p1a), channel_id=1, source_target_pairs={{0,32},{1,33},{2,34},{3,35},{4,36},{5,37},{6,38},{7,39},{8,40},{9,... | collective-permute-start | bytes 884744 | tf_op jit(solution)/shard_map/ppermute | solution.py:40
  23.3 11.8 %collective-permute-start.3 = (bf16[128,1152]{1,0:T(8,128)(2,1)S(1)}, bf16[128,1152]{1,0:T(8,128)(2,1)S(1)}, u32[]{:S(2)}, u32[]{:S(2)}) collective-permute-start(bf16[128,1152]{1,0:T(8,128)(2,1)S(1)} %collective-permute-done.2.p2a), channel_id=1, source_target_pairs={{0,224},{1,225},{2,226},{3,227},{4,228},{5,229},{6,230},{7,231},{8... | collective-permute-start | bytes 884744 | tf_op jit(solution)/shard_map/ppermute | solution.py:40
  23.3 12.6 %collective-permute-start.5 = (bf16[128,1152]{1,0:T(8,128)(2,1)S(1)}, bf16[128,1152]{1,0:T(8,128)(2,1)S(1)}, u32[]{:S(2)}, u32[]{:S(2)}) collective-permute-start(bf16[128,1152]{1,0:T(8,128)(2,1)S(1)} %collective-permute-done.4.p1b), channel_id=1, source_target_pairs={{0,32},{1,33},{2,34},{3,35},{4,36},{5,37},{6,38},{7,39},{8,40},{9,... | collective-permute-start | bytes 884744 | tf_op jit(solution)/shard_map/ppermute | solution.py:40
  29.0 11.4 %collective-permute-start.7 = (bf16[128,1152]{1,0:T(8,128)(2,1)S(1)}, bf16[128,1152]{1,0:T(8,128)(2,1)S(1)}, u32[]{:S(2)}, u32[]{:S(2)}) collective-permute-start(bf16[128,1152]{1,0:T(8,128)(2,1)S(1)} %collective-permute-done.6.p2b), channel_id=1, source_target_pairs={{0,224},{1,225},{2,226},{3,227},{4,228},{5,229},{6,230},{7,231},{8... | collective-permute-start | bytes 884744 | tf_op jit(solution)/shard_map/ppermute | solution.py:40
  41.4 2.1 %collective-permute-start.9 = (bf16[256,1152]{1,0:T(8,128)(2,1)S(1)}, bf16[256,1152]{1,0:T(8,128)(2,1)S(1)}, u32[]{:S(2)}, u32[]{:S(2)}) collective-permute-start(bf16[256,1152]{1,0:T(8,128)(2,1)S(1)} %shard_map.81), channel_id=1, source_target_pairs={{0,16},{1,17},{2,18},{3,19},{4,20},{5,21},{6,22},{7,23},{8,24},{9,... | collective-permute-start | bytes 1769480 | tf_op jit(solution)/shard_map/ppermute | solution.py:40
  44.1 1.7 %collective-permute-start.10 = (bf16[256,576]{1,0:T(8,128)(2,1)S(1)}, bf16[256,576]{1,0:T(8,128)(2,1)S(1)}, u32[]{:S(2)}, u32[]{:S(2)}) collective-permute-start(bf16[256,576]{1,0:T(8,128)(2,1)S(1)} %get-tuple-element.81), channel_id=1, source_target_pairs={{0,16},{1,17},{2,18},{3,19},{4,20},{5,21},{6,22},{7,23},{8,24},{9,... | collective-permute-start | bytes 884744 | tf_op jit(solution)/shard_map/ppermute | solution.py:40
  44.4 10.7 %collective-permute-start.14 = (bf16[256,1152]{1,0:T(8,128)(2,1)S(1)}, bf16[256,1152]{1,0:T(8,128)(2,1)S(1)}, u32[]{:S(2)}, u32[]{:S(2)}) collective-permute-start(bf16[256,1152]{1,0:T(8,128)(2,1)S(1)} %shard_map.85), channel_id=1, source_target_pairs={{0,16},{1,17},{2,18},{3,19},{4,20},{5,21},{6,22},{7,23},{8,24},{9,... | collective-permute-start | bytes 1769480 | tf_op jit(solution)/shard_map/ppermute | solution.py:40
  47.2 7.9 %collective-permute-start.11 = (bf16[144,1152]{1,0:T(8,128)(2,1)S(1)}, bf16[144,1152]{1,0:T(8,128)(2,1)S(1)}, u32[]{:S(2)}, u32[]{:S(2)}) collective-permute-start(bf16[144,1152]{1,0:T(8,128)(2,1)S(1)} %get-tuple-element.85), channel_id=1, source_target_pairs={{0,64},{1,65},{2,66},{3,67},{4,68},{5,69},{6,70},{7,71},{8,72},{9,... | collective-permute-start | bytes 995336 | tf_op jit(solution)/shard_map/ppermute | solution.py:40
  48.6 10.0 %collective-permute-start.12 = (bf16[144,1152]{1,0:T(8,128)(2,1)S(1)}, bf16[144,1152]{1,0:T(8,128)(2,1)S(1)}, u32[]{:S(2)}, u32[]{:S(2)}) collective-permute-start(bf16[144,1152]{1,0:T(8,128)(2,1)S(1)} %get-tuple-element.86), channel_id=1, source_target_pairs={{0,32},{1,33},{2,34},{3,35},{4,36},{5,37},{6,38},{7,39},{8,40},{9,... | collective-permute-start | bytes 995336 | tf_op jit(solution)/shard_map/ppermute | solution.py:40
  48.8 9.7 %collective-permute-start.13 = (bf16[144,1152]{1,0:T(8,128)(2,1)S(1)}, bf16[144,1152]{1,0:T(8,128)(2,1)S(1)}, u32[]{:S(2)}, u32[]{:S(2)}) collective-permute-start(bf16[144,1152]{1,0:T(8,128)(2,1)S(1)} %get-tuple-element.87), channel_id=1, source_target_pairs={{0,96},{1,97},{2,98},{3,99},{4,100},{5,101},{6,102},{7,103},{8,104... | collective-permute-start | bytes 995336 | tf_op jit(solution)/shard_map/ppermute | solution.py:40
  51.3 1.7 %copy-start = (bf16[1152,1152]{1,0:T(8,128)(2,1)S(1)}, bf16[1152,1152]{1,0:T(8,128)(2,1)}, u32[]{:S(2)}) copy-start(bf16[1152,1152]{1,0:T(8,128)(2,1)} %head.3) | copy-start | bytes 7962628
  55.0 6.8 %copy-start.1 = (bf16[256,1152]{1,0:T(8,128)(2,1)S(1)}, bf16[256,1152]{1,0:T(8,128)(2,1)}, u32[]{:S(2)}) copy-start(bf16[256,1152]{1,0:T(8,128)(2,1)} %texts.3) | copy-start | bytes 1769476
  59.0 5.1 %collective-permute-start.15 = (bf16[72,576]{1,0:T(8,128)(2,1)S(1)}, bf16[72,576]{1,0:T(8,128)(2,1)S(1)}, u32[]{:S(2)}, u32[]{:S(2)}) collective-permute-start(bf16[72,576]{1,0:T(8,128)(2,1)S(1)} %get-tuple-element.97), channel_id=1, source_target_pairs={{0,128},{1,129},{2,130},{3,131},{4,132},{5,133},{6,134},{7,135},{8... | collective-permute-start | bytes 248840 | tf_op jit(solution)/shard_map/ppermute | solution.py:40
  59.1 6.0 %collective-permute-start.16 = (bf16[72,576]{1,0:T(8,128)(2,1)S(1)}, bf16[72,576]{1,0:T(8,128)(2,1)S(1)}, u32[]{:S(2)}, u32[]{:S(2)}) collective-permute-start(bf16[72,576]{1,0:T(8,128)(2,1)S(1)} %get-tuple-element.98), channel_id=1, source_target_pairs={{0,1},{1,128},{2,3},{3,130},{4,5},{5,132},{6,7},{7,134},{8,9},{9,1... | collective-permute-start | bytes 248840 | tf_op jit(solution)/shard_map/ppermute | solution.py:40
  60.0 5.0 %collective-permute-start.17 = (bf16[72,576]{1,0:T(8,128)(2,1)S(1)}, bf16[72,576]{1,0:T(8,128)(2,1)S(1)}, u32[]{:S(2)}, u32[]{:S(2)}) collective-permute-start(bf16[72,576]{1,0:T(8,128)(2,1)S(1)} %get-tuple-element.99), channel_id=1, source_target_pairs={{0,129},{1,0},{2,131},{3,2},{4,133},{5,4},{6,135},{7,6},{8,137},{9... | collective-permute-start | bytes 248840 | tf_op jit(solution)/shard_map/ppermute | solution.py:40

commit v7 on v6

--- a/solution.py
+++ b/solution.py
@@ -296,11 +296,24 @@
     out[...] = mm(dproj[...], head[...], (1, 1))
 
 
+FOLD = 3
+
+
+def folded(piece):
+    rows = piece.shape[0] // FOLD
+    return jnp.concatenate([piece[k * rows : (k + 1) * rows] for k in range(FOLD)], 1)
+
+
+def unfolded(piece):
+    width = piece.shape[1] // FOLD
+    return jnp.concatenate([piece[:, k * width : (k + 1) * width] for k in range(FOLD)], 0)
+
+
 def split_body(a, b, c, d, out):
     total = a[...].astype(F32) + b[...].astype(F32) + c[...].astype(F32) + d[...].astype(F32)
-    own = out.shape[2]
+    own = out.shape[2] // FOLD
     for k in range(out.shape[0]):
-        out[k] = total[:, k * own : (k + 1) * own].astype(BF)
+        out[k] = folded(total[:, k * own : (k + 1) * own]).astype(BF)
 
 
 def spread_body(parts, out):
@@ -316,7 +329,7 @@
     yhs, xs, cores = SIZES[:3]
     order = [(yh * xs + x) * cores for x in range(xs) for yh in range(yhs)]
     order += [(yh * xs + x) * cores + 1 for yh in range(yhs) for x in range(xs)]
-    out[...] = jnp.concatenate([parts[k].astype(F32) for k in order], 0).T * factor
+    out[...] = jnp.concatenate([unfolded(parts[k].astype(F32)) for k in order], 0).T * factor
 
 
 def ring_pairs(turn, first):
@@ -402,9 +415,9 @@
     (grad_text,) = call(text_end_body, [(big, F32)], par, dtxt, given_txt, texts)
     *parts, grad_text = tie((*parts, grad_text))
     own = width // INNER
-    (part,) = call(split_body, [((SIZES[3], half // 8, own), BF)], *parts)
+    (part,) = call(split_body, [((SIZES[3], half // 8 // FOLD, own * FOLD), BF)], *parts)
     part = lax.all_to_all(part, "z", 0, 0)
-    (part,) = call(spread_body, [((BLKS, half // 8, own), BF)], part)
+    (part,) = call(spread_body, [((BLKS, half // 8 // FOLD, own * FOLD), BF)], part)
     part = lax.all_to_all(part, ("yh", "x", "core"), 0, 0)
     factor = 1.0 / float(count * COUNT) ** 0.5
     (head_grad,) = call(functools.partial(join_body, factor), [((own, width), F32)], part)

time: 99.2 us -> 97.8 us (0.986)
  blocking collectives: 32.4 us -> 31.1 us
where the time goes in v7:
time: 97.8 us; the launch traced here: 97.3 us
  starting transfers between devices  31.2 us (32%)
  blocking collectives  31.1 us (32%)
  Pallas kernels  19 us (19%)
  waiting for transfers between devices  13.2 us (13%)
  between operations  2.06 us (2%)
    ppermute x18, starting transfers between devices, moved(): return lax.ppermute(value, AXES, pairs)  31.2 us
    pallas_call x16, Pallas kernels, call(): pl.pallas_call(body, out_shape=shapes, in_specs=in_specs, out_specs=[pl.B...  19 us
    all_to_all x1, blocking collectives, on_device(): part = lax.all_to_all(part, ('yh', 'x', 'core'), 0, 0)  15.9 us
    all_to_all x1, blocking collectives, on_device(): part = lax.all_to_all(part, 'z', 0, 0)  15.2 us
    ppermute x18, waiting for transfers between devices, moved(): return lax.ppermute(value, AXES, pairs)  13.2 us
  transfers between devices with their start and end apart: 18, of which 8 were waited for; matrix products, arithmetic and copies ran while one was open for 0% of the time, Pallas kernels for 13%

profile of v7, /device:TPU:1, one launch (start us, length us, event | category | flops | bytes accessed | tf_op | source)
XLA Modules:
  0.0 97.3 jit_solution(10549919521652511639)
XLA Ops:
  1.9 3.3 %shard_map.76 = (f32[2,128]{1,0:T(2,128)S(1)}, bf16[128,1152]{1,0:T(8,128)(2,1)S(1)}, bf16[128,1152]{1,0:T(8,128)(2,1)S(1)}, bf16[128,1152]{1,0:T(8,128)(2,1)S(1...) custom-call(f32[1]{0:T(128)S(6)} %copy.8.scale, ...), custom_call_target="tpu_custom_call" | custom-call | bytes 7964672 | tf_op jit(solution)/shard_map/pallas_call | solution.py:53
  5.2 3.3 %collective-permute-start.8 = (bf16[768,1152]{1,0:T(8,128)(2,1)S(1)}, bf16[768,1152]{1,0:T(8,128)(2,1)S(1)}, u32[]{:S(2)}, u32[]{:S(2)}) collective-permute-start(bf16[768,1152]{1,0:T(8,128)(2,1)S(1)} %get-tuple-element.57.both), channel_id=1, source_target_pairs={{0,16},{1,17},{2,18},{3,19},{4,20},{5,21},{6,22},{7,23},{8,24},{9,... | collective-permute-start | bytes 5308424 | tf_op jit(solution)/shard_map/ppermute | solution.py:40
  8.6 3.4 %collective-permute-start = (bf16[128,1152]{1,0:T(8,128)(2,1)S(1)}, bf16[128,1152]{1,0:T(8,128)(2,1)S(1)}, u32[]{:S(2)}, u32[]{:S(2)}) collective-permute-start(bf16[128,1152]{1,0:T(8,128)(2,1)S(1)} %get-tuple-element.56), channel_id=1, source_target_pairs={{0,32},{1,33},{2,34},{3,35},{4,36},{5,37},{6,38},{7,39},{8,40},{9,... | collective-permute-start | bytes 884744 | tf_op jit(solution)/shard_map/ppermute | solution.py:40
  11.9 5.1 %collective-permute-start.4 = (bf16[128,1152]{1,0:T(8,128)(2,1)S(1)}, bf16[128,1152]{1,0:T(8,128)(2,1)S(1)}, u32[]{:S(2)}, u32[]{:S(2)}) collective-permute-start(bf16[128,1152]{1,0:T(8,128)(2,1)S(1)} %get-tuple-element.62), channel_id=1, source_target_pairs={{0,32},{1,33},{2,34},{3,35},{4,36},{5,37},{6,38},{7,39},{8,40},{9,... | collective-permute-start | bytes 884744 | tf_op jit(solution)/shard_map/ppermute | solution.py:40
  17.0 1.1 %shard_map.77 = (f32[256,1152]{1,0:T(8,128)S(1)}, f32[256,1152]{1,0:T(8,128)S(1)}) custom-call(f32[2,128]{1,0:T(2,128)S(1)} %get-tuple-element.55.par, bf16[768,1152]{1,0:T(8,128)(2,1)S(1)} %get-tuple-element.57.both), custom_call_target="tpu_custom_call" | custom-call | bytes 4129792 | tf_op jit(solution)/shard_map/pallas_call | solution.py:53
  18.2 5.2 %collective-permute-start.1 = (bf16[128,1152]{1,0:T(8,128)(2,1)S(1)}, bf16[128,1152]{1,0:T(8,128)(2,1)S(1)}, u32[]{:S(2)}, u32[]{:S(2)}) collective-permute-start(bf16[128,1152]{1,0:T(8,128)(2,1)S(1)} %collective-permute-done.p1a), channel_id=1, source_target_pairs={{0,32},{1,33},{2,34},{3,35},{4,36},{5,37},{6,38},{7,39},{8,40},{9,... | collective-permute-start | bytes 884744 | tf_op jit(solution)/shard_map/ppermute | solution.py:40
  23.3 5.6 %collective-permute-start.5 = (bf16[128,1152]{1,0:T(8,128)(2,1)S(1)}, bf16[128,1152]{1,0:T(8,128)(2,1)S(1)}, u32[]{:S(2)}, u32[]{:S(2)}) collective-permute-start(bf16[128,1152]{1,0:T(8,128)(2,1)S(1)} %collective-permute-done.4.p1b), channel_id=1, source_target_pairs={{0,32},{1,33},{2,34},{3,35},{4,36},{5,37},{6,38},{7,39},{8,40},{9,... | collective-permute-start | bytes 884744 | tf_op jit(solution)/shard_map/ppermute | solution.py:40
  29.0 1.0 %shard_map.79 = (bf16[256,1152]{1,0:T(8,128)(2,1)S(1)}, bf16[256,1152]{1,0:T(8,128)(2,1)S(1)}) custom-call(bf16[768,1152]{1,0:T(8,128)(2,1)S(1)} %get-tuple-element.57.both, bf16[768,1152]{1,0:T(8,128)(2,1)S(1)} %collective-permute-done.8.both_s), custom_call_target="tpu_custom_call" | custom-call | bytes 4718592 | tf_op jit(solution)/shard_map/pallas_call | solution.py:53
  30.0 3.5 %shard_map.78 = (f32[256,1152]{1,0:T(8,128)S(1)}, f32[256,1152]{1,0:T(8,128)S(1)}, f32[256,1152]{1,0:T(8,128)S(1)}, f32[256,1152]{1,0:T(8,128)S(1)}) custom-call(f32[2,128]{1,0:T(2,128)S(1)} %get-tuple-element.55.par, bf16[128,1152]{1,0:T(8,128)(2,1)S(1)} %collective-permute-done.p1a, bf16[128,1152]{1,0:T(8,128)(2,1)S(1)} %collective-permute-done.4.p1b, ...), custom_call_target="tpu_custom_call" | custom-call | bytes 11797504 | tf_op jit(solution)/shard_map/pallas_call | solution.py:53
  33.5 1.6 %collective-permute-done.3.p2a = bf16[128,1152]{1,0:T(8,128)(2,1)S(1)} collective-permute-done((bf16[128,1152]{1,0:T(8,128)(2,1)S(1)}, bf16[128,1152]{1,0:T(8,128)(2,1)S(1)}, u32[]{:S(2)}, u32[]{:S(2)}) %collective-permute-start.3) | collective-permute-done | bytes 294944 | tf_op jit(solution)/shard_map/ppermute | solution.py:40
  36.0 4.5 %collective-permute-done.7.p2b = bf16[128,1152]{1,0:T(8,128)(2,1)S(1)} collective-permute-done((bf16[128,1152]{1,0:T(8,128)(2,1)S(1)}, bf16[128,1152]{1,0:T(8,128)(2,1)S(1)}, u32[]{:S(2)}, u32[]{:S(2)}) %collective-permute-start.7) | collective-permute-done | bytes 294944 | tf_op jit(solution)/shard_map/ppermute | solution.py:40
  42.4 1.0 %collective-permute-done.9.given = bf16[256,1152]{1,0:T(8,128)(2,1)S(1)} collective-permute-done((bf16[256,1152]{1,0:T(8,128)(2,1)S(1)}, bf16[256,1152]{1,0:T(8,128)(2,1)S(1)}, u32[]{:S(2)}, u32[]{:S(2)}) %collective-permute-start.9) | collective-permute-done | bytes 589856 | tf_op jit(solution)/shard_map/ppermute | solution.py:40
  44.4 1.4 %collective-permute-start.14 = (bf16[256,1152]{1,0:T(8,128)(2,1)S(1)}, bf16[256,1152]{1,0:T(8,128)(2,1)S(1)}, u32[]{:S(2)}, u32[]{:S(2)}) collective-permute-start(bf16[256,1152]{1,0:T(8,128)(2,1)S(1)} %shard_map.85), channel_id=1, source_target_pairs={{0,16},{1,17},{2,18},{3,19},{4,20},{5,21},{6,22},{7,23},{8,24},{9,... | collective-permute-start | bytes 1769480 | tf_op jit(solution)/shard_map/ppermute | solution.py:40
  45.8 1.3 %shard_map.83 = (bf16[144,1152]{1,0:T(8,128)(2,1)S(1)}, bf16[144,1152]{1,0:T(8,128)(2,1)S(1)}, bf16[144,1152]{1,0:T(8,128)(2,1)S(1)}, bf16[144,1152]{1,0:T(8,128)(2,1)S(1)}) custom-call(bf16[256,576]{1,0:T(8,128)(2,1)S(1)} %get-tuple-element.80.keep, bf16[256,576]{1,0:T(8,128)(2,1)S(1)} %collective-permute-done.10.other, ...), custom_call_target="tpu_custom_call" | custom-call | bytes 3096576 | tf_op jit(solution)/shard_map/pallas_call | solution.py:53
  47.2 1.4 %collective-permute-start.11 = (bf16[144,1152]{1,0:T(8,128)(2,1)S(1)}, bf16[144,1152]{1,0:T(8,128)(2,1)S(1)}, u32[]{:S(2)}, u32[]{:S(2)}) collective-permute-start(bf16[144,1152]{1,0:T(8,128)(2,1)S(1)} %get-tuple-element.85), channel_id=1, source_target_pairs={{0,64},{1,65},{2,66},{3,67},{4,68},{5,69},{6,70},{7,71},{8,72},{9,... | collective-permute-start | bytes 995336 | tf_op jit(solution)/shard_map/ppermute | solution.py:40
  48.8 2.4 %collective-permute-start.13 = (bf16[144,1152]{1,0:T(8,128)(2,1)S(1)}, bf16[144,1152]{1,0:T(8,128)(2,1)S(1)}, u32[]{:S(2)}, u32[]{:S(2)}) collective-permute-start(bf16[144,1152]{1,0:T(8,128)(2,1)S(1)} %get-tuple-element.87), channel_id=1, source_target_pairs={{0,96},{1,97},{2,98},{3,99},{4,100},{5,101},{6,102},{7,103},{8,104... | collective-permute-start | bytes 995336 | tf_op jit(solution)/shard_map/ppermute | solution.py:40
  53.0 2.0 %shard_map.84 = f32[256,1152]{1,0:T(8,128)} custom-call(bf16[256,1152]{1,0:T(8,128)(2,1)S(1)} %get-tuple-element.88.dproj, bf16[1152,1152]{1,0:T(8,128)(2,1)S(1)} %copy-done), custom_call_target="tpu_custom_call" | custom-call | bytes 4423680 | tf_op jit(solution)/shard_map/pallas_call | solution.py:53
  55.1 3.5 %collective-permute-done.12.c = bf16[144,1152]{1,0:T(8,128)(2,1)S(1)} collective-permute-done((bf16[144,1152]{1,0:T(8,128)(2,1)S(1)}, bf16[144,1152]{1,0:T(8,128)(2,1)S(1)}, u32[]{:S(2)}, u32[]{:S(2)}) %collective-permute-start.12) | collective-permute-done | bytes 331808 | tf_op jit(solution)/shard_map/ppermute | solution.py:40
  60.0 1.8 %collective-permute-start.17 = (bf16[72,576]{1,0:T(8,128)(2,1)S(1)}, bf16[72,576]{1,0:T(8,128)(2,1)S(1)}, u32[]{:S(2)}, u32[]{:S(2)}) collective-permute-start(bf16[72,576]{1,0:T(8,128)(2,1)S(1)} %get-tuple-element.99), channel_id=1, source_target_pairs={{0,129},{1,0},{2,131},{3,2},{4,133},{5,4},{6,135},{7,6},{8,137},{9... | collective-permute-start | bytes 248840 | tf_op jit(solution)/shard_map/ppermute | solution.py:40
  61.9 1.6 %shard_map.88 = f32[256,1152]{1,0:T(8,128)} custom-call(f32[2,128]{1,0:T(2,128)S(1)} %get-tuple-element.55.par, f32[256,1152]{1,0:T(8,128)S(1)} %shard_map.86.old, bf16[256,1152]{1,0:T(8,128)(2,1)S(1)} %collective-permute-done.14.given, bf16[256,1152]{1,0:T(8,128)(2,1)S(1)} %copy-done.1), custom_call_target="tpu_custom_call" | custom-call | bytes 3539968 | tf_op jit(solution)/shard_map/pallas_call | solution.py:53
  64.1 1.0 %collective-permute-done.16.c = bf16[72,576]{1,0:T(8,128)(2,1)S(1)} collective-permute-done((bf16[72,576]{1,0:T(8,128)(2,1)S(1)}, bf16[72,576]{1,0:T(8,128)(2,1)S(1)}, u32[]{:S(2)}, u32[]{:S(2)}) %collective-permute-start.16) | collective-permute-done | bytes 82976 | tf_op jit(solution)/shard_map/ppermute | solution.py:40
  65.2 15.2 %all_to_all.10.parts = bf16[8,24,216]{2,1,0:T(8,128)(2,1)S(1)} all-to-all(bf16[8,24,216]{2,1,0:T(8,128)(2,1)S(1)} %shard_map.89), channel_id=1, replica_groups=mesh['yh'=2,'x'=4,'core'=2,'z'=8,'yl'=2] {'z'}, dimensions={0} | all-to-all | bytes 165888 | tf_op jit(solution)/shard_map/all_to_all | solution.py:419
  80.5 15.9 %all_to_all.11.parts = bf16[16,24,216]{2,1,0:T(8,128)(2,1)S(1)} all-to-all(bf16[16,24,216]{2,1,0:T(8,128)(2,1)S(1)} %shard_map.90), channel_id=1, replica_groups=mesh['yh'=2,'x'=4,'core'=2,'z'=8,'yl'=2] {'yh','x','core'}, dimensions={0} | all-to-all | bytes 331776 | tf_op jit(solution)/shard_map/all_to_all | solution.py:421
  96.3 1.0 shard_map.91
  (34 shorter events, 8.1 us)
Async XLA Ops:
  5.2 23.7 %collective-permute-start.8 = (bf16[768,1152]{1,0:T(8,128)(2,1)S(1)}, bf16[768,1152]{1,0:T(8,128)(2,1)S(1)}, u32[]{:S(2)}, u32[]{:S(2)}) collective-permute-start(bf16[768,1152]{1,0:T(8,128)(2,1)S(1)} %get-tuple-element.57.both), channel_id=1, source_target_pairs={{0,16},{1,17},{2,18},{3,19},{4,20},{5,21},{6,22},{7,23},{8,24},{9,... | collective-permute-start | bytes 5308424 | tf_op jit(solution)/shard_map/ppermute | solution.py:40
  8.6 9.6 %collective-permute-start = (bf16[128,1152]{1,0:T(8,128)(2,1)S(1)}, bf16[128,1152]{1,0:T(8,128)(2,1)S(1)}, u32[]{:S(2)}, u32[]{:S(2)}) collective-permute-start(bf16[128,1152]{1,0:T(8,128)(2,1)S(1)} %get-tuple-element.56), channel_id=1, source_target_pairs={{0,32},{1,33},{2,34},{3,35},{4,36},{5,37},{6,38},{7,39},{8,40},{9,... | collective-permute-start | bytes 884744 | tf_op jit(solution)/shard_map/ppermute | solution.py:40
  11.9 11.4 %collective-permute-start.2 = (bf16[128,1152]{1,0:T(8,128)(2,1)S(1)}, bf16[128,1152]{1,0:T(8,128)(2,1)S(1)}, u32[]{:S(2)}, u32[]{:S(2)}) collective-permute-start(bf16[128,1152]{1,0:T(8,128)(2,1)S(1)} %get-tuple-element.61), channel_id=1, source_target_pairs={{0,224},{1,225},{2,226},{3,227},{4,228},{5,229},{6,230},{7,231},{8... | collective-permute-start | bytes 884744 | tf_op jit(solution)/shard_map/ppermute | solution.py:40
  11.9 11.4 %collective-permute-start.4 = (bf16[128,1152]{1,0:T(8,128)(2,1)S(1)}, bf16[128,1152]{1,0:T(8,128)(2,1)S(1)}, u32[]{:S(2)}, u32[]{:S(2)}) collective-permute-start(bf16[128,1152]{1,0:T(8,128)(2,1)S(1)} %get-tuple-element.62), channel_id=1, source_target_pairs={{0,32},{1,33},{2,34},{3,35},{4,36},{5,37},{6,38},{7,39},{8,40},{9,... | collective-permute-start | bytes 884744 | tf_op jit(solution)/shard_map/ppermute | solution.py:40
  17.0 12.0 %collective-permute-start.6 = (bf16[128,1152]{1,0:T(8,128)(2,1)S(1)}, bf16[128,1152]{1,0:T(8,128)(2,1)S(1)}, u32[]{:S(2)}, u32[]{:S(2)}) collective-permute-start(bf16[128,1152]{1,0:T(8,128)(2,1)S(1)} %get-tuple-element.63), channel_id=1, source_target_pairs={{0,224},{1,225},{2,226},{3,227},{4,228},{5,229},{6,230},{7,231},{8... | collective-permute-start | bytes 884744 | tf_op jit(solution)/shard_map/ppermute | solution.py:40
  18.2 15.4 %collective-permute-start.1 = (bf16[128,1152]{1,0:T(8,128)(2,1)S(1)}, bf16[128,1152]{1,0:T(8,128)(2,1)S(1)}, u32[]{:S(2)}, u32[]{:S(2)}) collective-permute-start(bf16[128,1152]{1,0:T(8,128)(2,1)S(1)} %collective-permute-done.p1a), channel_id=1, source_target_pairs={{0,32},{1,33},{2,34},{3,35},{4,36},{5,37},{6,38},{7,39},{8,40},{9,... | collective-permute-start | bytes 884744 | tf_op jit(solution)/shard_map/ppermute | solution.py:40
  23.3 11.8 %collective-permute-start.3 = (bf16[128,1152]{1,0:T(8,128)(2,1)S(1)}, bf16[128,1152]{1,0:T(8,128)(2,1)S(1)}, u32[]{:S(2)}, u32[]{:S(2)}) collective-permute-start(bf16[128,1152]{1,0:T(8,128)(2,1)S(1)} %collective-permute-done.2.p2a), channel_id=1, source_target_pairs={{0,224},{1,225},{2,226},{3,227},{4,228},{5,229},{6,230},{7,231},{8... | collective-permute-start | bytes 884744 | tf_op jit(solution)/shard_map/ppermute | solution.py:40
  23.3 12.6 %collective-permute-start.5 = (bf16[128,1152]{1,0:T(8,128)(2,1)S(1)}, bf16[128,1152]{1,0:T(8,128)(2,1)S(1)}, u32[]{:S(2)}, u32[]{:S(2)}) collective-permute-start(bf16[128,1152]{1,0:T(8,128)(2,1)S(1)} %collective-permute-done.4.p1b), channel_id=1, source_target_pairs={{0,32},{1,33},{2,34},{3,35},{4,36},{5,37},{6,38},{7,39},{8,40},{9,... | collective-permute-start | bytes 884744 | tf_op jit(solution)/shard_map/ppermute | solution.py:40
  29.0 11.4 %collective-permute-start.7 = (bf16[128,1152]{1,0:T(8,128)(2,1)S(1)}, bf16[128,1152]{1,0:T(8,128)(2,1)S(1)}, u32[]{:S(2)}, u32[]{:S(2)}) collective-permute-start(bf16[128,1152]{1,0:T(8,128)(2,1)S(1)} %collective-permute-done.6.p2b), channel_id=1, source_target_pairs={{0,224},{1,225},{2,226},{3,227},{4,228},{5,229},{6,230},{7,231},{8... | collective-permute-start | bytes 884744 | tf_op jit(solution)/shard_map/ppermute | solution.py:40
  41.4 2.1 %collective-permute-start.9 = (bf16[256,1152]{1,0:T(8,128)(2,1)S(1)}, bf16[256,1152]{1,0:T(8,128)(2,1)S(1)}, u32[]{:S(2)}, u32[]{:S(2)}) collective-permute-start(bf16[256,1152]{1,0:T(8,128)(2,1)S(1)} %shard_map.81), channel_id=1, source_target_pairs={{0,16},{1,17},{2,18},{3,19},{4,20},{5,21},{6,22},{7,23},{8,24},{9,... | collective-permute-start | bytes 1769480 | tf_op jit(solution)/shard_map/ppermute | solution.py:40
  44.1 1.7 %collective-permute-start.10 = (bf16[256,576]{1,0:T(8,128)(2,1)S(1)}, bf16[256,576]{1,0:T(8,128)(2,1)S(1)}, u32[]{:S(2)}, u32[]{:S(2)}) collective-permute-start(bf16[256,576]{1,0:T(8,128)(2,1)S(1)} %get-tuple-element.81), channel_id=1, source_target_pairs={{0,16},{1,17},{2,18},{3,19},{4,20},{5,21},{6,22},{7,23},{8,24},{9,... | collective-permute-start | bytes 884744 | tf_op jit(solution)/shard_map/ppermute | solution.py:40
  44.4 10.7 %collective-permute-start.14 = (bf16[256,1152]{1,0:T(8,128)(2,1)S(1)}, bf16[256,1152]{1,0:T(8,128)(2,1)S(1)}, u32[]{:S(2)}, u32[]{:S(2)}) collective-permute-start(bf16[256,1152]{1,0:T(8,128)(2,1)S(1)} %shard_map.85), channel_id=1, source_target_pairs={{0,16},{1,17},{2,18},{3,19},{4,20},{5,21},{6,22},{7,23},{8,24},{9,... | collective-permute-start | bytes 1769480 | tf_op jit(solution)/shard_map/ppermute | solution.py:40
  47.2 7.9 %collective-permute-start.11 = (bf16[144,1152]{1,0:T(8,128)(2,1)S(1)}, bf16[144,1152]{1,0:T(8,128)(2,1)S(1)}, u32[]{:S(2)}, u32[]{:S(2)}) collective-permute-start(bf16[144,1152]{1,0:T(8,128)(2,1)S(1)} %get-tuple-element.85), channel_id=1, source_target_pairs={{0,64},{1,65},{2,66},{3,67},{4,68},{5,69},{6,70},{7,71},{8,72},{9,... | collective-permute-start | bytes 995336 | tf_op jit(solution)/shard_map/ppermute | solution.py:40
  48.6 10.0 %collective-permute-start.12 = (bf16[144,1152]{1,0:T(8,128)(2,1)S(1)}, bf16[144,1152]{1,0:T(8,128)(2,1)S(1)}, u32[]{:S(2)}, u32[]{:S(2)}) collective-permute-start(bf16[144,1152]{1,0:T(8,128)(2,1)S(1)} %get-tuple-element.86), channel_id=1, source_target_pairs={{0,32},{1,33},{2,34},{3,35},{4,36},{5,37},{6,38},{7,39},{8,40},{9,... | collective-permute-start | bytes 995336 | tf_op jit(solution)/shard_map/ppermute | solution.py:40
  48.8 9.7 %collective-permute-start.13 = (bf16[144,1152]{1,0:T(8,128)(2,1)S(1)}, bf16[144,1152]{1,0:T(8,128)(2,1)S(1)}, u32[]{:S(2)}, u32[]{:S(2)}) collective-permute-start(bf16[144,1152]{1,0:T(8,128)(2,1)S(1)} %get-tuple-element.87), channel_id=1, source_target_pairs={{0,96},{1,97},{2,98},{3,99},{4,100},{5,101},{6,102},{7,103},{8,104... | collective-permute-start | bytes 995336 | tf_op jit(solution)/shard_map/ppermute | solution.py:40
  51.3 1.7 %copy-start = (bf16[1152,1152]{1,0:T(8,128)(2,1)S(1)}, bf16[1152,1152]{1,0:T(8,128)(2,1)}, u32[]{:S(2)}) copy-start(bf16[1152,1152]{1,0:T(8,128)(2,1)} %head.3) | copy-start | bytes 7962628
  55.0 6.8 %copy-start.1 = (bf16[256,1152]{1,0:T(8,128)(2,1)S(1)}, bf16[256,1152]{1,0:T(8,128)(2,1)}, u32[]{:S(2)}) copy-start(bf16[256,1152]{1,0:T(8,128)(2,1)} %texts.3) | copy-start | bytes 1769476
  59.0 5.1 %collective-permute-start.15 = (bf16[72,576]{1,0:T(8,128)(2,1)S(1)}, bf16[72,576]{1,0:T(8,128)(2,1)S(1)}, u32[]{:S(2)}, u32[]{:S(2)}) collective-permute-start(bf16[72,576]{1,0:T(8,128)(2,1)S(1)} %get-tuple-element.97), channel_id=1, source_target_pairs={{0,128},{1,129},{2,130},{3,131},{4,132},{5,133},{6,134},{7,135},{8... | collective-permute-start | bytes 248840 | tf_op jit(solution)/shard_map/ppermute | solution.py:40
  59.1 6.0 %collective-permute-start.16 = (bf16[72,576]{1,0:T(8,128)(2,1)S(1)}, bf16[72,576]{1,0:T(8,128)(2,1)S(1)}, u32[]{:S(2)}, u32[]{:S(2)}) collective-permute-start(bf16[72,576]{1,0:T(8,128)(2,1)S(1)} %get-tuple-element.98), channel_id=1, source_target_pairs={{0,1},{1,128},{2,3},{3,130},{4,5},{5,132},{6,7},{7,134},{8,9},{9,1... | collective-permute-start | bytes 248840 | tf_op jit(solution)/shard_map/ppermute | solution.py:40
  60.0 5.0 %collective-permute-start.17 = (bf16[72,576]{1,0:T(8,128)(2,1)S(1)}, bf16[72,576]{1,0:T(8,128)(2,1)S(1)}, u32[]{:S(2)}, u32[]{:S(2)}) collective-permute-start(bf16[72,576]{1,0:T(8,128)(2,1)S(1)} %get-tuple-element.99), channel_id=1, source_target_pairs={{0,129},{1,0},{2,131},{3,2},{4,133},{5,4},{6,135},{7,6},{8,137},{9... | collective-permute-start | bytes 248840 | tf_op jit(solution)/shard_map/ppermute | solution.py:40

commit v8 on v7

--- a/solution.py
+++ b/solution.py
@@ -171,6 +171,32 @@
     dtxt[...] = mm(grad, img_b, (0, 0))
 
 
+def half_of(one, two, kind):
+    return jnp.where(lax.axis_index("core") == kind, one[...], two[...])
+
+
+def give_first_body(par, one, two, both_s, old, out):
+    out[...] = old[...]
+
+    @pl.when(lax.axis_index("core") == 1)
+    def _():
+        out[...] += applied(par, image_of(both_s), half_of(one, two, 0))
+
+
+def give_last_body(par, one, two, both_s, old, out):
+    @pl.when(lax.axis_index("core") == 1)
+    def _():
+        out[...] = (old[...] + applied(par, image_of(both_s), half_of(one, two, 0))).astype(BF)
+
+    @pl.when(lax.axis_index("core") != 1)
+    def _():
+        out[...] = old[...].astype(BF)
+
+
+def far_half_body(par, one, two, both, old, out):
+    out[...] = old[...] + applied(par, image_of(both), half_of(one, two, 0))
+
+
 def joined(one, two, kind):
     here = lax.axis_index("core") == kind
     return jnp.concatenate([jnp.where(here, a[...], b[...]) for a, b in zip(one, two)], 0)
@@ -250,9 +276,13 @@
         out[...] = pieces[lax.rem(place + turn, 4)]
 
 
-def head_body(keep, other, images, images2, *rest):
+def head_own_body(keep, images, out):
+    out[...] = mm(keep[...], images[...], (0, 0))
+
+
+def head_body(base, other, images2, *rest):
     outs, pieces = rest[:4], rest[4]
-    total = mm(keep[...], images[...], (0, 0)) + mm(other[...], images2[...], (0, 0))
+    total = base[...] + mm(other[...], images2[...], (0, 0))
     rows, half = pieces.shape[1], total.shape[1] // 2
 
     @pl.when(lax.axis_index("core") == 0)
@@ -372,26 +402,25 @@
     dimg, dtxt, dimg_s, dtxt_s = call(
         near_body, [(big, F32)] * 4, par, near[0], near[2], near[1], near[3], both, both_s, dimg, dtxt
     )
-    *far, dimg, dtxt, dimg_s, dtxt_s, ordered, ordered2 = tie(
-        (*far, dimg, dtxt, dimg_s, dtxt_s, ordered, ordered2)
-    )
+    far[0], far[1], dimg, dtxt, dimg_s, dtxt_s, ordered, ordered2 = tie(
+        (far[0], far[1], dimg, dtxt, dimg_s, dtxt_s, ordered, ordered2)
+    )
+    (dimg_s,) = call(give_first_body, [(big, F32)], par, far[0], far[1], both_s, dimg_s)
+    (dimg,) = call(far_half_body, [(big, F32)], par, far[0], far[1], both, dimg)
+    far[2], far[3], dimg, dimg_s = tie((far[2], far[3], dimg, dimg_s))
+    (give,) = call(give_last_body, [(big, BF)], par, far[2], far[3], both_s, dimg_s)
+    given = moved(give, swap)
+    (dimg,) = call(far_half_body, [(big, F32)], par, far[2], far[3], both, dimg)
     far = [far[0], far[2], far[1], far[3]]
-
-    (give,) = call(
-        functools.partial(give_body, 1, 0, image_of), [(big, BF)], par, *far, both_s, dimg_s
-    )
-    given = moved(give, swap)
-    (dimg,) = call(
-        functools.partial(far_body, 0, image_of), [(big, F32)], par, *far, both, dimg
-    )
     dproj, keep, send = call(
         image_end_body, [(big, BF), ((count, half), BF), ((count, half), BF)],
         par, dimg, given, unit_img, pnorm,
     )
     other = moved(send, swap)
+    (base,) = call(head_own_body, [((half, width), F32)], keep, ordered)
     quarter = ((half // 4, width), BF)
     parts = call(
-        head_body, [quarter] * 4, keep, other, ordered, ordered2,
+        head_body, [quarter] * 4, base, other, ordered2,
         scratch=[pltpu.VMEM((4, half // 4, width), BF)],
     )
     parts = list(parts)

time: 97.8 us -> 97.7 us (level)
  waiting for transfers between devices: 13.2 us -> 11.6 us
  Pallas kernels: 19 us -> 20.5 us
    ppermute x18, waiting for transfers between devices: 13.2 us -> 11.6 us  [moved(): return lax.ppermute(value, AXES, pairs)]
    pallas_call x16 -> x19, Pallas kernels: 19 us -> 20.5 us  [call(): pl.pallas_call(body, out_shape=shapes, in_specs=in_specs, out_specs=[pl.B...]
  transfers between devices with their start and end apart: 18 -> 18, of which waited for: 8 -> 6; matrix products, arithmetic and copies ran while one was open for 0% -> 0% of each run, Pallas kernels for 13% -> 15%
where the time goes in v8:
time: 97.7 us; the launch traced here: 97.3 us
  starting transfers between devices  31.4 us (32%)
  blocking collectives  30.9 us (32%)
  Pallas kernels  20.5 us (21%)
  waiting for transfers between devices  11.6 us (12%)
  between operations  2.09 us (2%)
    ppermute x18, starting transfers between devices, moved(): return lax.ppermute(value, AXES, pairs)  31.4 us
    pallas_call x19, Pallas kernels, call(): pl.pallas_call(body, out_shape=shapes, in_specs=in_specs, out_specs=[pl.B...  20.5 us
    all_to_all x1, blocking collectives, on_device(): part = lax.all_to_all(part, ('yh', 'x', 'core'), 0, 0)  15.7 us
    all_to_all x1, blocking collectives, on_device(): part = lax.all_to_all(part, 'z', 0, 0)  15.2 us
    ppermute x18, waiting for transfers between devices, moved(): return lax.ppermute(value, AXES, pairs)  11.6 us
  transfers between devices with their start and end apart: 18, of which 6 were waited for; matrix products, arithmetic and copies ran while one was open for 0% of the time, Pallas kernels for 15%

profile of v8, /device:TPU:1, one launch (start us, length us, event | category | flops | bytes accessed | tf_op | source)
XLA Modules:
  0.0 97.3 jit_solution(14953587301961404222)
XLA Ops:
  1.9 3.3 %shard_map.76 = (f32[2,128]{1,0:T(2,128)S(1)}, bf16[128,1152]{1,0:T(8,128)(2,1)S(1)}, bf16[128,1152]{1,0:T(8,128)(2,1)S(1)}, bf16[128,1152]{1,0:T(8,128)(2,1)S(1...) custom-call(f32[1]{0:T(128)S(6)} %copy.8.scale, ...), custom_call_target="tpu_custom_call" | custom-call | bytes 7964672 | tf_op jit(solution)/shard_map/pallas_call | solution.py:53
  5.2 3.3 %collective-permute-start.8 = (bf16[768,1152]{1,0:T(8,128)(2,1)S(1)}, bf16[768,1152]{1,0:T(8,128)(2,1)S(1)}, u32[]{:S(2)}, u32[]{:S(2)}) collective-permute-start(bf16[768,1152]{1,0:T(8,128)(2,1)S(1)} %get-tuple-element.61.both), channel_id=1, source_target_pairs={{0,16},{1,17},{2,18},{3,19},{4,20},{5,21},{6,22},{7,23},{8,24},{9,... | collective-permute-start | bytes 5308424 | tf_op jit(solution)/shard_map/ppermute | solution.py:40
  8.6 3.4 %collective-permute-start.4 = (bf16[128,1152]{1,0:T(8,128)(2,1)S(1)}, bf16[128,1152]{1,0:T(8,128)(2,1)S(1)}, u32[]{:S(2)}, u32[]{:S(2)}) collective-permute-start(bf16[128,1152]{1,0:T(8,128)(2,1)S(1)} %get-tuple-element.60), channel_id=1, source_target_pairs={{0,32},{1,33},{2,34},{3,35},{4,36},{5,37},{6,38},{7,39},{8,40},{9,... | collective-permute-start | bytes 884744 | tf_op jit(solution)/shard_map/ppermute | solution.py:40
  11.9 5.1 %collective-permute-start = (bf16[128,1152]{1,0:T(8,128)(2,1)S(1)}, bf16[128,1152]{1,0:T(8,128)(2,1)S(1)}, u32[]{:S(2)}, u32[]{:S(2)}) collective-permute-start(bf16[128,1152]{1,0:T(8,128)(2,1)S(1)} %get-tuple-element.58), channel_id=1, source_target_pairs={{0,32},{1,33},{2,34},{3,35},{4,36},{5,37},{6,38},{7,39},{8,40},{9,... | collective-permute-start | bytes 884744 | tf_op jit(solution)/shard_map/ppermute | solution.py:40
  17.0 1.1 %shard_map.77 = (f32[256,1152]{1,0:T(8,128)S(1)}, f32[256,1152]{1,0:T(8,128)S(1)}) custom-call(f32[2,128]{1,0:T(2,128)S(1)} %get-tuple-element.57.par, bf16[768,1152]{1,0:T(8,128)(2,1)S(1)} %get-tuple-element.61.both), custom_call_target="tpu_custom_call" | custom-call | bytes 4129792 | tf_op jit(solution)/shard_map/pallas_call | solution.py:53
  18.2 5.2 %collective-permute-start.5 = (bf16[128,1152]{1,0:T(8,128)(2,1)S(1)}, bf16[128,1152]{1,0:T(8,128)(2,1)S(1)}, u32[]{:S(2)}, u32[]{:S(2)}) collective-permute-start(bf16[128,1152]{1,0:T(8,128)(2,1)S(1)} %collective-permute-done.4.p1a), channel_id=1, source_target_pairs={{0,32},{1,33},{2,34},{3,35},{4,36},{5,37},{6,38},{7,39},{8,40},{9,... | collective-permute-start | bytes 884744 | tf_op jit(solution)/shard_map/ppermute | solution.py:40
  23.3 5.6 %collective-permute-start.1 = (bf16[128,1152]{1,0:T(8,128)(2,1)S(1)}, bf16[128,1152]{1,0:T(8,128)(2,1)S(1)}, u32[]{:S(2)}, u32[]{:S(2)}) collective-permute-start(bf16[128,1152]{1,0:T(8,128)(2,1)S(1)} %collective-permute-done.p1b), channel_id=1, source_target_pairs={{0,32},{1,33},{2,34},{3,35},{4,36},{5,37},{6,38},{7,39},{8,40},{9,... | collective-permute-start | bytes 884744 | tf_op jit(solution)/shard_map/ppermute | solution.py:40
  29.0 1.0 %shard_map.79 = (bf16[256,1152]{1,0:T(8,128)(2,1)S(1)}, bf16[256,1152]{1,0:T(8,128)(2,1)S(1)}) custom-call(bf16[768,1152]{1,0:T(8,128)(2,1)S(1)} %get-tuple-element.61.both, bf16[768,1152]{1,0:T(8,128)(2,1)S(1)} %collective-permute-done.8.both_s), custom_call_target="tpu_custom_call" | custom-call | bytes 4718592 | tf_op jit(solution)/shard_map/pallas_call | solution.py:53
  30.0 3.5 %shard_map.78 = (f32[256,1152]{1,0:T(8,128)S(1)}, f32[256,1152]{1,0:T(8,128)S(1)}, f32[256,1152]{1,0:T(8,128)S(1)}, f32[256,1152]{1,0:T(8,128)S(1)}) custom-call(f32[2,128]{1,0:T(2,128)S(1)} %get-tuple-element.57.par, bf16[128,1152]{1,0:T(8,128)(2,1)S(1)} %collective-permute-done.4.p1a, bf16[128,1152]{1,0:T(8,128)(2,1)S(1)} %collective-permute-done.p1b, ...), custom_call_target="tpu_custom_call" | custom-call | bytes 11797504 | tf_op jit(solution)/shard_map/pallas_call | solution.py:53
  33.5 1.6 %collective-permute-done.7.two.p2a = bf16[128,1152]{1,0:T(8,128)(2,1)S(1)} collective-permute-done((bf16[128,1152]{1,0:T(8,128)(2,1)S(1)}, bf16[128,1152]{1,0:T(8,128)(2,1)S(1)}, u32[]{:S(2)}, u32[]{:S(2)}) %collective-permute-start.7) | collective-permute-done | bytes 294944 | tf_op jit(solution)/shard_map/ppermute | solution.py:40
  36.8 3.7 %collective-permute-done.3.two.p2b = bf16[128,1152]{1,0:T(8,128)(2,1)S(1)} collective-permute-done((bf16[128,1152]{1,0:T(8,128)(2,1)S(1)}, bf16[128,1152]{1,0:T(8,128)(2,1)S(1)}, u32[]{:S(2)}, u32[]{:S(2)}) %collective-permute-start.3) | collective-permute-done | bytes 294944 | tf_op jit(solution)/shard_map/ppermute | solution.py:40
  42.1 1.2 %collective-permute-done.9.given = bf16[256,1152]{1,0:T(8,128)(2,1)S(1)} collective-permute-done((bf16[256,1152]{1,0:T(8,128)(2,1)S(1)}, bf16[256,1152]{1,0:T(8,128)(2,1)S(1)}, u32[]{:S(2)}, u32[]{:S(2)}) %collective-permute-start.9) | collective-permute-done | bytes 589856 | tf_op jit(solution)/shard_map/ppermute | solution.py:40
  44.2 1.4 %collective-permute-start.14 = (bf16[256,1152]{1,0:T(8,128)(2,1)S(1)}, bf16[256,1152]{1,0:T(8,128)(2,1)S(1)}, u32[]{:S(2)}, u32[]{:S(2)}) collective-permute-start(bf16[256,1152]{1,0:T(8,128)(2,1)S(1)} %shard_map.88), channel_id=1, source_target_pairs={{0,16},{1,17},{2,18},{3,19},{4,20},{5,21},{6,22},{7,23},{8,24},{9,... | collective-permute-start | bytes 1769480 | tf_op jit(solution)/shard_map/ppermute | solution.py:40
  46.2 1.0 shard_map.86
  47.1 1.4 %collective-permute-start.11 = (bf16[144,1152]{1,0:T(8,128)(2,1)S(1)}, bf16[144,1152]{1,0:T(8,128)(2,1)S(1)}, u32[]{:S(2)}, u32[]{:S(2)}) collective-permute-start(bf16[144,1152]{1,0:T(8,128)(2,1)S(1)} %get-tuple-element.89), channel_id=1, source_target_pairs={{0,64},{1,65},{2,66},{3,67},{4,68},{5,69},{6,70},{7,71},{8,72},{9,... | collective-permute-start | bytes 995336 | tf_op jit(solution)/shard_map/ppermute | solution.py:40
  48.8 2.4 %collective-permute-start.13 = (bf16[144,1152]{1,0:T(8,128)(2,1)S(1)}, bf16[144,1152]{1,0:T(8,128)(2,1)S(1)}, u32[]{:S(2)}, u32[]{:S(2)}) collective-permute-start(bf16[144,1152]{1,0:T(8,128)(2,1)S(1)} %get-tuple-element.91), channel_id=1, source_target_pairs={{0,96},{1,97},{2,98},{3,99},{4,100},{5,101},{6,102},{7,103},{8,104... | collective-permute-start | bytes 995336 | tf_op jit(solution)/shard_map/ppermute | solution.py:40
  53.0 2.0 %shard_map.87 = f32[256,1152]{1,0:T(8,128)} custom-call(bf16[256,1152]{1,0:T(8,128)(2,1)S(1)} %get-tuple-element.92.dproj, bf16[1152,1152]{1,0:T(8,128)(2,1)S(1)} %copy-done), custom_call_target="tpu_custom_call" | custom-call | bytes 4423680 | tf_op jit(solution)/shard_map/pallas_call | solution.py:53
  55.0 3.5 %collective-permute-done.12.c = bf16[144,1152]{1,0:T(8,128)(2,1)S(1)} collective-permute-done((bf16[144,1152]{1,0:T(8,128)(2,1)S(1)}, bf16[144,1152]{1,0:T(8,128)(2,1)S(1)}, u32[]{:S(2)}, u32[]{:S(2)}) %collective-permute-start.12) | collective-permute-done | bytes 331808 | tf_op jit(solution)/shard_map/ppermute | solution.py:40
  59.3 1.1 %collective-permute-start.16 = (bf16[72,576]{1,0:T(8,128)(2,1)S(1)}, bf16[72,576]{1,0:T(8,128)(2,1)S(1)}, u32[]{:S(2)}, u32[]{:S(2)}) collective-permute-start(bf16[72,576]{1,0:T(8,128)(2,1)S(1)} %get-tuple-element.102), channel_id=1, source_target_pairs={{0,1},{1,128},{2,3},{3,130},{4,5},{5,132},{6,7},{7,134},{8,9},{9,1... | collective-permute-start | bytes 248840 | tf_op jit(solution)/shard_map/ppermute | solution.py:40
  60.4 1.7 %collective-permute-start.17 = (bf16[72,576]{1,0:T(8,128)(2,1)S(1)}, bf16[72,576]{1,0:T(8,128)(2,1)S(1)}, u32[]{:S(2)}, u32[]{:S(2)}) collective-permute-start(bf16[72,576]{1,0:T(8,128)(2,1)S(1)} %get-tuple-element.103), channel_id=1, source_target_pairs={{0,129},{1,0},{2,131},{3,2},{4,133},{5,4},{6,135},{7,6},{8,137},{9... | collective-permute-start | bytes 248840 | tf_op jit(solution)/shard_map/ppermute | solution.py:40
  62.0 1.6 %shard_map.91 = f32[256,1152]{1,0:T(8,128)} custom-call(f32[2,128]{1,0:T(2,128)S(1)} %get-tuple-element.57.par, f32[256,1152]{1,0:T(8,128)S(1)} %shard_map.89.old, bf16[256,1152]{1,0:T(8,128)(2,1)S(1)} %collective-permute-done.14.given, bf16[256,1152]{1,0:T(8,128)(2,1)S(1)} %copy-done.1), custom_call_target="tpu_custom_call" | custom-call | bytes 3539968 | tf_op jit(solution)/shard_map/pallas_call | solution.py:53
  65.4 15.2 %all_to_all.10.parts = bf16[8,24,216]{2,1,0:T(8,128)(2,1)S(1)} all-to-all(bf16[8,24,216]{2,1,0:T(8,128)(2,1)S(1)} %shard_map.92), channel_id=1, replica_groups=mesh['yh'=2,'x'=4,'core'=2,'z'=8,'yl'=2] {'z'}, dimensions={0} | all-to-all | bytes 165888 | tf_op jit(solution)/shard_map/all_to_all | solution.py:448
  80.7 15.7 %all_to_all.11.parts = bf16[16,24,216]{2,1,0:T(8,128)(2,1)S(1)} all-to-all(bf16[16,24,216]{2,1,0:T(8,128)(2,1)S(1)} %shard_map.93), channel_id=1, replica_groups=mesh['yh'=2,'x'=4,'core'=2,'z'=8,'yl'=2] {'yh','x','core'}, dimensions={0} | all-to-all | bytes 331776 | tf_op jit(solution)/shard_map/all_to_all | solution.py:450
  96.3 1.0 shard_map.94
  (37 shorter events, 9.3 us)
Async XLA Ops:
  5.2 23.7 %collective-permute-start.8 = (bf16[768,1152]{1,0:T(8,128)(2,1)S(1)}, bf16[768,1152]{1,0:T(8,128)(2,1)S(1)}, u32[]{:S(2)}, u32[]{:S(2)}) collective-permute-start(bf16[768,1152]{1,0:T(8,128)(2,1)S(1)} %get-tuple-element.61.both), channel_id=1, source_target_pairs={{0,16},{1,17},{2,18},{3,19},{4,20},{5,21},{6,22},{7,23},{8,24},{9,... | collective-permute-start | bytes 5308424 | tf_op jit(solution)/shard_map/ppermute | solution.py:40
  8.6 9.6 %collective-permute-start.4 = (bf16[128,1152]{1,0:T(8,128)(2,1)S(1)}, bf16[128,1152]{1,0:T(8,128)(2,1)S(1)}, u32[]{:S(2)}, u32[]{:S(2)}) collective-permute-start(bf16[128,1152]{1,0:T(8,128)(2,1)S(1)} %get-tuple-element.60), channel_id=1, source_target_pairs={{0,32},{1,33},{2,34},{3,35},{4,36},{5,37},{6,38},{7,39},{8,40},{9,... | collective-permute-start | bytes 884744 | tf_op jit(solution)/shard_map/ppermute | solution.py:40
  11.9 11.4 %collective-permute-start.6 = (bf16[128,1152]{1,0:T(8,128)(2,1)S(1)}, bf16[128,1152]{1,0:T(8,128)(2,1)S(1)}, u32[]{:S(2)}, u32[]{:S(2)}) collective-permute-start(bf16[128,1152]{1,0:T(8,128)(2,1)S(1)} %get-tuple-element.65), channel_id=1, source_target_pairs={{0,224},{1,225},{2,226},{3,227},{4,228},{5,229},{6,230},{7,231},{8... | collective-permute-start | bytes 884744 | tf_op jit(solution)/shard_map/ppermute | solution.py:40
  11.9 11.4 %collective-permute-start = (bf16[128,1152]{1,0:T(8,128)(2,1)S(1)}, bf16[128,1152]{1,0:T(8,128)(2,1)S(1)}, u32[]{:S(2)}, u32[]{:S(2)}) collective-permute-start(bf16[128,1152]{1,0:T(8,128)(2,1)S(1)} %get-tuple-element.58), channel_id=1, source_target_pairs={{0,32},{1,33},{2,34},{3,35},{4,36},{5,37},{6,38},{7,39},{8,40},{9,... | collective-permute-start | bytes 884744 | tf_op jit(solution)/shard_map/ppermute | solution.py:40
  17.0 12.0 %collective-permute-start.2 = (bf16[128,1152]{1,0:T(8,128)(2,1)S(1)}, bf16[128,1152]{1,0:T(8,128)(2,1)S(1)}, u32[]{:S(2)}, u32[]{:S(2)}) collective-permute-start(bf16[128,1152]{1,0:T(8,128)(2,1)S(1)} %get-tuple-element.59), channel_id=1, source_target_pairs={{0,224},{1,225},{2,226},{3,227},{4,228},{5,229},{6,230},{7,231},{8... | collective-permute-start | bytes 884744 | tf_op jit(solution)/shard_map/ppermute | solution.py:40
  18.2 15.4 %collective-permute-start.5 = (bf16[128,1152]{1,0:T(8,128)(2,1)S(1)}, bf16[128,1152]{1,0:T(8,128)(2,1)S(1)}, u32[]{:S(2)}, u32[]{:S(2)}) collective-permute-start(bf16[128,1152]{1,0:T(8,128)(2,1)S(1)} %collective-permute-done.4.p1a), channel_id=1, source_target_pairs={{0,32},{1,33},{2,34},{3,35},{4,36},{5,37},{6,38},{7,39},{8,40},{9,... | collective-permute-start | bytes 884744 | tf_op jit(solution)/shard_map/ppermute | solution.py:40
  23.3 11.8 %collective-permute-start.7 = (bf16[128,1152]{1,0:T(8,128)(2,1)S(1)}, bf16[128,1152]{1,0:T(8,128)(2,1)S(1)}, u32[]{:S(2)}, u32[]{:S(2)}) collective-permute-start(bf16[128,1152]{1,0:T(8,128)(2,1)S(1)} %collective-permute-done.6.p2a), channel_id=1, source_target_pairs={{0,224},{1,225},{2,226},{3,227},{4,228},{5,229},{6,230},{7,231},{8... | collective-permute-start | bytes 884744 | tf_op jit(solution)/shard_map/ppermute | solution.py:40
  23.3 13.4 %collective-permute-start.1 = (bf16[128,1152]{1,0:T(8,128)(2,1)S(1)}, bf16[128,1152]{1,0:T(8,128)(2,1)S(1)}, u32[]{:S(2)}, u32[]{:S(2)}) collective-permute-start(bf16[128,1152]{1,0:T(8,128)(2,1)S(1)} %collective-permute-done.p1b), channel_id=1, source_target_pairs={{0,32},{1,33},{2,34},{3,35},{4,36},{5,37},{6,38},{7,39},{8,40},{9,... | collective-permute-start | bytes 884744 | tf_op jit(solution)/shard_map/ppermute | solution.py:40
  29.0 11.4 %collective-permute-start.3 = (bf16[128,1152]{1,0:T(8,128)(2,1)S(1)}, bf16[128,1152]{1,0:T(8,128)(2,1)S(1)}, u32[]{:S(2)}, u32[]{:S(2)}) collective-permute-start(bf16[128,1152]{1,0:T(8,128)(2,1)S(1)} %collective-permute-done.2.p2b), channel_id=1, source_target_pairs={{0,224},{1,225},{2,226},{3,227},{4,228},{5,229},{6,230},{7,231},{8... | collective-permute-start | bytes 884744 | tf_op jit(solution)/shard_map/ppermute | solution.py:40
  41.2 2.1 %collective-permute-start.9 = (bf16[256,1152]{1,0:T(8,128)(2,1)S(1)}, bf16[256,1152]{1,0:T(8,128)(2,1)S(1)}, u32[]{:S(2)}, u32[]{:S(2)}) collective-permute-start(bf16[256,1152]{1,0:T(8,128)(2,1)S(1)} %shard_map.83), channel_id=1, source_target_pairs={{0,16},{1,17},{2,18},{3,19},{4,20},{5,21},{6,22},{7,23},{8,24},{9,... | collective-permute-start | bytes 1769480 | tf_op jit(solution)/shard_map/ppermute | solution.py:40
  43.9 2.2 %collective-permute-start.10 = (bf16[256,576]{1,0:T(8,128)(2,1)S(1)}, bf16[256,576]{1,0:T(8,128)(2,1)S(1)}, u32[]{:S(2)}, u32[]{:S(2)}) collective-permute-start(bf16[256,576]{1,0:T(8,128)(2,1)S(1)} %get-tuple-element.86), channel_id=1, source_target_pairs={{0,16},{1,17},{2,18},{3,19},{4,20},{5,21},{6,22},{7,23},{8,24},{9,... | collective-permute-start | bytes 884744 | tf_op jit(solution)/shard_map/ppermute | solution.py:40
  44.2 10.8 %collective-permute-start.14 = (bf16[256,1152]{1,0:T(8,128)(2,1)S(1)}, bf16[256,1152]{1,0:T(8,128)(2,1)S(1)}, u32[]{:S(2)}, u32[]{:S(2)}) collective-permute-start(bf16[256,1152]{1,0:T(8,128)(2,1)S(1)} %shard_map.88), channel_id=1, source_target_pairs={{0,16},{1,17},{2,18},{3,19},{4,20},{5,21},{6,22},{7,23},{8,24},{9,... | collective-permute-start | bytes 1769480 | tf_op jit(solution)/shard_map/ppermute | solution.py:40
  47.1 7.9 %collective-permute-start.11 = (bf16[144,1152]{1,0:T(8,128)(2,1)S(1)}, bf16[144,1152]{1,0:T(8,128)(2,1)S(1)}, u32[]{:S(2)}, u32[]{:S(2)}) collective-permute-start(bf16[144,1152]{1,0:T(8,128)(2,1)S(1)} %get-tuple-element.89), channel_id=1, source_target_pairs={{0,64},{1,65},{2,66},{3,67},{4,68},{5,69},{6,70},{7,71},{8,72},{9,... | collective-permute-start | bytes 995336 | tf_op jit(solution)/shard_map/ppermute | solution.py:40
  48.5 10.0 %collective-permute-start.12 = (bf16[144,1152]{1,0:T(8,128)(2,1)S(1)}, bf16[144,1152]{1,0:T(8,128)(2,1)S(1)}, u32[]{:S(2)}, u32[]{:S(2)}) collective-permute-start(bf16[144,1152]{1,0:T(8,128)(2,1)S(1)} %get-tuple-element.90), channel_id=1, source_target_pairs={{0,32},{1,33},{2,34},{3,35},{4,36},{5,37},{6,38},{7,39},{8,40},{9,... | collective-permute-start | bytes 995336 | tf_op jit(solution)/shard_map/ppermute | solution.py:40
  48.8 9.7 %collective-permute-start.13 = (bf16[144,1152]{1,0:T(8,128)(2,1)S(1)}, bf16[144,1152]{1,0:T(8,128)(2,1)S(1)}, u32[]{:S(2)}, u32[]{:S(2)}) collective-permute-start(bf16[144,1152]{1,0:T(8,128)(2,1)S(1)} %get-tuple-element.91), channel_id=1, source_target_pairs={{0,96},{1,97},{2,98},{3,99},{4,100},{5,101},{6,102},{7,103},{8,104... | collective-permute-start | bytes 995336 | tf_op jit(solution)/shard_map/ppermute | solution.py:40
  51.2 1.7 %copy-start = (bf16[1152,1152]{1,0:T(8,128)(2,1)S(1)}, bf16[1152,1152]{1,0:T(8,128)(2,1)}, u32[]{:S(2)}) copy-start(bf16[1152,1152]{1,0:T(8,128)(2,1)} %head.3) | copy-start | bytes 7962628
  55.0 7.0 %copy-start.1 = (bf16[256,1152]{1,0:T(8,128)(2,1)S(1)}, bf16[256,1152]{1,0:T(8,128)(2,1)}, u32[]{:S(2)}) copy-start(bf16[256,1152]{1,0:T(8,128)(2,1)} %texts.3) | copy-start | bytes 1769476
  59.0 5.6 %collective-permute-start.15 = (bf16[72,576]{1,0:T(8,128)(2,1)S(1)}, bf16[72,576]{1,0:T(8,128)(2,1)S(1)}, u32[]{:S(2)}, u32[]{:S(2)}) collective-permute-start(bf16[72,576]{1,0:T(8,128)(2,1)S(1)} %get-tuple-element.101), channel_id=1, source_target_pairs={{0,128},{1,129},{2,130},{3,131},{4,132},{5,133},{6,134},{7,135},{8... | collective-permute-start | bytes 248840 | tf_op jit(solution)/shard_map/ppermute | solution.py:40
  59.3 6.0 %collective-permute-start.16 = (bf16[72,576]{1,0:T(8,128)(2,1)S(1)}, bf16[72,576]{1,0:T(8,128)(2,1)S(1)}, u32[]{:S(2)}, u32[]{:S(2)}) collective-permute-start(bf16[72,576]{1,0:T(8,128)(2,1)S(1)} %get-tuple-element.102), channel_id=1, source_target_pairs={{0,1},{1,128},{2,3},{3,130},{4,5},{5,132},{6,7},{7,134},{8,9},{9,1... | collective-permute-start | bytes 248840 | tf_op jit(solution)/shard_map/ppermute | solution.py:40
  60.4 4.9 %collective-permute-start.17 = (bf16[72,576]{1,0:T(8,128)(2,1)S(1)}, bf16[72,576]{1,0:T(8,128)(2,1)S(1)}, u32[]{:S(2)}, u32[]{:S(2)}) collective-permute-start(bf16[72,576]{1,0:T(8,128)(2,1)S(1)} %get-tuple-element.103), channel_id=1, source_target_pairs={{0,129},{1,0},{2,131},{3,2},{4,133},{5,4},{6,135},{7,6},{8,137},{9... | collective-permute-start | bytes 248840 | tf_op jit(solution)/shard_map/ppermute | solution.py:40

commit v9 on v7

--- a/solution.py
+++ b/solution.py
@@ -86,37 +86,26 @@
     return tfloat * inverse, inverse
 
 
-def halved(value, first, second):
-    rows = value.shape[0] // 2
-    first[...] = value[:rows]
-    second[...] = value[rows:]
-
-
 CUTS = (0, 256, 512, 768, 1152)
 
 
 def start_body(
-    scale, bias, images, texts, head, par,
-    p1a, p1b, p2a, p2b, both, unit, norm, t_in, i_in, h_in, sems,
+    scale, bias, images, texts, head, par, own, rows, unit, norm, t_in, i_in, h_in, sems
 ):
     copies = [
         pltpu.make_async_copy(texts, t_in, sems.at[0]),
         pltpu.make_async_copy(images, i_in, sems.at[1]),
     ]
     for k in range(len(CUTS) - 1):
-        rows = pl.ds(CUTS[k], CUTS[k + 1] - CUTS[k])
-        copies.append(pltpu.make_async_copy(head.at[rows], h_in.at[rows], sems.at[2 + k]))
+        part = pl.ds(CUTS[k], CUTS[k + 1] - CUTS[k])
+        copies.append(pltpu.make_async_copy(head.at[part], h_in.at[part], sems.at[2 + k]))
     for copy in copies:
         copy.start()
     par[0:1] = jnp.full((1, par.shape[1]), scale[0], F32)
     par[1:2] = jnp.full((1, par.shape[1]), bias[0], F32)
     copies[0].wait()
-    count = t_in.shape[0]
-    low = text_unit(t_in[...])[0].astype(BF)
-    both[:count] = low
-    low_txt = low
+    low_txt = text_unit(t_in[...])[0].astype(BF)
     copies[1].wait()
-    both[2 * count :] = i_in[...]
     proj = None
     for k in range(len(CUTS) - 1):
         copies[2 + k].wait()
@@ -128,86 +117,49 @@
     unit[...] = value
     norm[...] = inverse
     low = value.astype(BF)
-    both[count : 2 * count] = low
-
-    @pl.when(lax.axis_index("core") == 0)
-    def _():
-        halved(low_txt, p1a, p1b)
-        halved(low, p2a, p2b)
-
-    @pl.when(lax.axis_index("core") != 0)
-    def _():
-        halved(low, p1a, p1b)
-        halved(low_txt, p2a, p2b)
-
-
-def text_of(both):
-    return both[: both.shape[0] // 3]
-
-
-def image_of(both):
-    count = both.shape[0] // 3
-    return both[count : 2 * count]
-
-
-def order_body(both, both_s, out, out2):
-    own = both.shape[1] // INNER
-    count = both.shape[0] // 3
+    first = lax.axis_index("core") == 0
+    own[...] = jnp.where(first, low_txt, low)
+    rows[...] = jnp.where(first, low, low_txt)
+
+
+def order_body(images, images_s, out, out_s):
+    own = images.shape[1] // INNER
     for z in range(SIZES[3]):
         for yl in range(SIZES[4]):
             source, target = (z * SIZES[4] + yl) * own, (yl * SIZES[3] + z) * own
-            out[:, target : target + own] = both[2 * count :, source : source + own]
-            out2[:, target : target + own] = both_s[2 * count :, source : source + own]
-
-
-def home_body(par, both, dimg, dtxt):
-    img_b, txt_b = image_of(both), text_of(both)
-    logit = logits(par, img_b, txt_b)
+            out[:, target : target + own] = images[:, source : source + own]
+            out_s[:, target : target + own] = images_s[:, source : source + own]
+
+
+def home_body(par, own, rows, to_rows, to_own):
+    logit = logits(par, rows[...], own[...])
     eye = lax.broadcasted_iota(jnp.int32, logit.shape, 0) == lax.broadcasted_iota(
         jnp.int32, logit.shape, 1
     )
     grad = jnp.where(eye, -sigmoid(-logit), sigmoid(logit)).astype(BF)
-    dimg[...] = mm(grad, txt_b, (1, 0))
-    dtxt[...] = mm(grad, img_b, (0, 0))
-
-
-def joined(one, two, kind):
-    here = lax.axis_index("core") == kind
-    return jnp.concatenate([jnp.where(here, a[...], b[...]) for a, b in zip(one, two)], 0)
-
-
-def near_body(par, p1a, p1b, p2a, p2b, both, both_s, dimg, dtxt, dimg_o, dtxt_o, dimg_s, dtxt_s):
-    t1, i1 = (joined((p1a, p1b), (p2a, p2b), kind) for kind in range(2))
-    dimg_o[...] = dimg[...] + applied(par, image_of(both), t1)
-    dtxt_o[...] = dtxt[...] + applied(par, text_of(both), i1)
-    dimg_s[...] = applied(par, image_of(both_s), t1)
-    dtxt_s[...] = applied(par, text_of(both_s), i1)
-
-    @pl.when(lax.axis_index("core") == 0)
-    def _():
-        dtxt_o[...] += applied(par, text_of(both), image_of(both_s))
-
-    @pl.when(lax.axis_index("core") != 0)
-    def _():
-        dimg_o[...] += applied(par, image_of(both), text_of(both_s))
-
-
-def give_body(giver, kind, rows_of, par, p1a, p1b, p2a, p2b, both_s, old, out):
-    @pl.when(lax.axis_index("core") == giver)
-    def _():
-        out[...] = (old[...] + applied(par, rows_of(both_s), joined((p1a, p1b), (p2a, p2b), kind))).astype(BF)
-
-    @pl.when(lax.axis_index("core") != giver)
-    def _():
-        out[...] = old[...].astype(BF)
-
-
-def far_body(kind, rows_of, par, p1a, p1b, p2a, p2b, both, old, out):
-    out[...] = old[...] + applied(par, rows_of(both), joined((p1a, p1b), (p2a, p2b), kind))
-
-
-def image_end_body(par, old, given, unit, norm, whole, keep, send):
-    dimg = par[0:1, 0:1] * (old[...] + given[...].astype(F32))
+    to_rows[...] = mm(grad, own[...], (1, 0))
+    to_own[...] = mm(grad, rows[...], (0, 0))
+
+
+def near_body(par, block, own, rows, rows_s, to_rows, to_own, out_rows, out_own, out_s):
+    out_rows[...] = to_rows[...] + applied(par, rows[...], block[...])
+    out_own[...] = to_own[...] + applied(par, own[...], rows_s[...])
+    out_s[...] = applied(par, rows_s[...], block[...])
+
+
+def next_body(par, block, rows, rows_s, to_rows, to_s, out_rows, out_s):
+    out_rows[...] = to_rows[...] + applied(par, rows[...], block[...])
+    out_s[...] = to_s[...] + applied(par, rows_s[...], block[...])
+
+
+def far_body(par, block, rows, old, out):
+    out[...] = (old[...] + applied(par, rows[...], block[...])).astype(out.dtype)
+
+
+def image_end_body(par, to_rows, to_own, given, unit, norm, whole, keep, send):
+    whole_own = to_own[...] + given[...].astype(F32)
+    first = lax.axis_index("core") == 0
+    dimg = par[0:1, 0:1] * jnp.where(first, to_rows[...], whole_own)
     value = unit[...]
     dproj = ((dimg - value * jnp.sum(value * dimg, -1, keepdims=True)) * norm[...]).astype(BF)
     whole[...] = dproj
@@ -224,13 +176,15 @@
         send[...] = dproj[:, :half]
 
 
-def text_end_body(par, old, given, texts, out):
-    dtxt = par[0:1, 0:1] * (old[...] + given[...].astype(F32))
+def text_end_body(par, to_rows, to_own, given, texts, out):
+    whole_own = to_own[...] + given[...].astype(F32)
+    first = lax.axis_index("core") == 0
+    dtxt = par[0:1, 0:1] * jnp.where(first, whole_own, to_rows[...])
     value, inverse = text_unit(texts[...])
     out[...] = (dtxt - value * jnp.sum(value * dtxt, -1, keepdims=True)) * inverse
 
 
-TURNS = (0, 2, 1, 3)
+TURNS = ((0, 1, 2, 3), (0, 2, 1, 3))
 
 
 def across_place():
@@ -245,14 +199,19 @@
     return jnp.where(lax.axis_index("core") == first, across_place(), along_place())
 
 
-def turned(place, pieces, outs):
-    for turn, out in zip(TURNS, outs):
+def turned(stage, pieces, outs):
+    place = place_of(stage)
+    for turn, out in zip(TURNS[stage], outs):
         out[...] = pieces[lax.rem(place + turn, 4)]
 
 
-def head_body(keep, other, images, images2, *rest):
+def head_own_body(keep, images, out):
+    out[...] = mm(keep[...], images[...], (0, 0))
+
+
+def head_body(base, other, images2, *rest):
     outs, pieces = rest[:4], rest[4]
-    total = mm(keep[...], images[...], (0, 0)) + mm(other[...], images2[...], (0, 0))
+    total = base[...] + mm(other[...], images2[...], (0, 0))
     rows, half = pieces.shape[1], total.shape[1] // 2
 
     @pl.when(lax.axis_index("core") == 0)
@@ -268,7 +227,7 @@
             second = total[up + rows : up + 2 * rows, left : left + half]
             pieces[k] = jnp.concatenate([first, second], 1).astype(BF)
 
-    turned(place_of(0), pieces, outs)
+    turned(0, pieces, outs)
 
 
 def quarter_body(a, b, c, d, *rest):
@@ -289,7 +248,7 @@
         for k in range(4):
             pieces[k] = quadrant(k % 2, k // 2)
 
-    turned(place_of(1), pieces, outs)
+    turned(1, pieces, outs)
 
 
 def grad_image_body(dproj, head, out):
@@ -352,68 +311,61 @@
     big = (count, width)
     tie = lax.optimization_barrier
 
-    part_of = ((count // 2, width), BF)
-    par, p1a, p1b, p2a, p2b, both, unit_img, pnorm = call(
+    par, own, rows, unit_img, pnorm = call(
         start_body,
-        [((2, 128), F32)] + [part_of] * 4 + [((3 * count, width), BF), (big, F32), ((count, 1), F32)],
+        [((2, 128), F32), (big, BF), (big, BF), (big, F32), ((count, 1), F32)],
         images, texts, head, scalars=(scale, bias), space=pltpu.HBM, limit=16,
         scratch=[
             pltpu.VMEM(big, BF), pltpu.VMEM(big, BF), pltpu.VMEM(head.shape, BF),
             pltpu.SemaphoreType.DMA((1 + len(CUTS),)),
         ],
     )
-    ways = (mixed_pairs(0), mixed_pairs(1))
-    near = [moved(p1a, ways[0]), moved(p2a, ways[1]), moved(p1b, ways[0]), moved(p2b, ways[1])]
-    both_s = moved(both, swap)
-    dimg, dtxt = call(home_body, [(big, F32)] * 2, par, both)
-    near[0], dimg, dtxt = tie((near[0], dimg, dtxt))
-    ordered, ordered2 = call(order_body, [(big, BF)] * 2, both, both_s)
-    far = [moved(p, ways[k % 2]) for k, p in enumerate(near)]
-    dimg, dtxt, dimg_s, dtxt_s = call(
-        near_body, [(big, F32)] * 4, par, near[0], near[2], near[1], near[3], both, both_s, dimg, dtxt
-    )
-    *far, dimg, dtxt, dimg_s, dtxt_s, ordered, ordered2 = tie(
-        (*far, dimg, dtxt, dimg_s, dtxt_s, ordered, ordered2)
-    )
-    far = [far[0], far[2], far[1], far[3]]
-
-    (give,) = call(
-        functools.partial(give_body, 1, 0, image_of), [(big, BF)], par, *far, both_s, dimg_s
-    )
+    way = mixed_pairs(0)
+    near = moved(own, way)
+    near_s = moved(moved(rows, swap), way)
+    rows_s = moved(own, swap)
+    images_s = moved(images, swap)
+    to_rows, to_own = call(home_body, [(big, F32)] * 2, par, own, rows)
+    near, to_rows, to_own = tie((near, to_rows, to_own))
+    far = moved(near, way)
+    to_rows, to_own, to_s = call(
+        near_body, [(big, F32)] * 3, par, near, own, rows, rows_s, to_rows, to_own
+    )
+    near_s, to_rows, to_own, to_s = tie((near_s, to_rows, to_own, to_s))
+    far_s = moved(near_s, way)
+    to_rows, to_s = call(next_body, [(big, F32)] * 2, par, near_s, rows, rows_s, to_rows, to_s)
+    ordered, ordered2 = call(order_body, [(big, BF)] * 2, images, images_s)
+    far, to_rows, to_own, to_s, ordered, ordered2 = tie(
+        (far, to_rows, to_own, to_s, ordered, ordered2)
+    )
+    (to_rows,) = call(far_body, [(big, F32)], par, far, rows, to_rows)
+    far_s, to_rows = tie((far_s, to_rows))
+    (give,) = call(far_body, [(big, BF)], par, far_s, rows_s, to_s)
     given = moved(give, swap)
-    (dimg,) = call(
-        functools.partial(far_body, 0, image_of), [(big, F32)], par, *far, both, dimg
-    )
+    (to_rows,) = call(far_body, [(big, F32)], par, far_s, rows, to_rows)
     dproj, keep, send = call(
         image_end_body, [(big, BF), ((count, half), BF), ((count, half), BF)],
-        par, dimg, given, unit_img, pnorm,
+        par, to_rows, to_own, given, unit_img, pnorm,
     )
     other = moved(send, swap)
+    (base,) = call(head_own_body, [((half, width), F32)], keep, ordered)
     quarter = ((half // 4, width), BF)
     parts = call(
-        head_body, [quarter] * 4, keep, other, ordered, ordered2,
+        head_body, [quarter] * 4, base, other, ordered2,
         scratch=[pltpu.VMEM((4, half // 4, width), BF)],
     )
     parts = list(parts)
-    parts = parts[:1] + [moved(p, ring_pairs(t, 0)) for p, t in zip(parts[1:], TURNS[1:])]
+    parts = parts[:1] + [moved(p, ring_pairs(t, 0)) for p, t in zip(parts[1:], TURNS[0][1:])]
     (grad_image,) = call(grad_image_body, [(big, F32)], dproj, head)
-    (give,) = call(
-        functools.partial(give_body, 0, 1, text_of), [(big, BF)], par, *far, both_s, dtxt_s
-    )
-    (dtxt,) = call(
-        functools.partial(far_body, 1, text_of), [(big, F32)], par, *far, both, dtxt
-    )
-    given_txt = moved(give, swap)
-    *parts, grad_image, given_txt, dtxt = tie((*parts, grad_image, given_txt, dtxt))
+    (grad_text,) = call(text_end_body, [(big, F32)], par, to_rows, to_own, given, texts)
+    *parts, grad_image, grad_text = tie((*parts, grad_image, grad_text))
     small = ((half // 8, half), BF)
     parts = call(
         quarter_body, [small] * 4, *parts,
         scratch=[pltpu.VMEM((4, half // 8, half), BF)],
     )
     parts = list(parts)
-    parts = parts[:1] + [moved(p, ring_pairs(t, 1)) for p, t in zip(parts[1:], TURNS[1:])]
-    (grad_text,) = call(text_end_body, [(big, F32)], par, dtxt, given_txt, texts)
-    *parts, grad_text = tie((*parts, grad_text))
+    parts = parts[:1] + [moved(p, ring_pairs(t, 1)) for p, t in zip(parts[1:], TURNS[1][1:])]
     own = width // INNER
     (part,) = call(split_body, [((SIZES[3], half // 8 // FOLD, own * FOLD), BF)], *parts)
     part = lax.all_to_all(part, "z", 0, 0)

time: 97.8 us -> 97.7 us (level)
  waiting for transfers between devices: 13.2 us -> 16.7 us
  starting transfers between devices: 31.2 us -> 29.1 us
  blocking collectives: 31.1 us -> 30.1 us
    ppermute x18 -> x15, waiting for transfers between devices: 13.2 us -> 16.7 us  [moved(): return lax.ppermute(value, AXES, pairs)]
    ppermute x18 -> x15, starting transfers between devices: 31.2 us -> 29.1 us  [moved(): return lax.ppermute(value, AXES, pairs)]
    all_to_all x1, blocking collectives: 15.2 us -> 14.2 us  [on_device(): part = lax.all_to_all(part, 'z', 0, 0)]
    pallas_call x16 -> x17, Pallas kernels: 19 us -> 19.4 us  [call(): pl.pallas_call(body, out_shape=shapes, in_specs=in_specs, out_specs=[pl.B...]
  transfers between devices with their start and end apart: 18 -> 15, of which waited for: 8 -> 9; matrix products, arithmetic and copies ran while one was open for 0% -> 0% of each run, Pallas kernels for 13% -> 12%
where the time goes in v9:
time: 97.7 us; the launch traced here: 97.3 us
  blocking collectives  30.1 us (31%)
  starting transfers between devices  29.1 us (30%)
  Pallas kernels  19.4 us (20%)
  waiting for transfers between devices  16.7 us (17%)
  between operations  2.07 us (2%)
    ppermute x15, starting transfers between devices, moved(): return lax.ppermute(value, AXES, pairs)  29.1 us
    pallas_call x17, Pallas kernels, call(): pl.pallas_call(body, out_shape=shapes, in_specs=in_specs, out_specs=[pl.B...  19.4 us
    ppermute x15, waiting for transfers between devices, moved(): return lax.ppermute(value, AXES, pairs)  16.7 us
    all_to_all x1, blocking collectives, on_device(): part = lax.all_to_all(part, ('yh', 'x', 'core'), 0, 0)  15.8 us
    all_to_all x1, blocking collectives, on_device(): part = lax.all_to_all(part, 'z', 0, 0)  14.2 us
  transfers between devices with their start and end apart: 15, of which 9 were waited for; matrix products, arithmetic and copies ran while one was open for 0% of the time, Pallas kernels for 12%

profile of v9, /device:TPU:1, one launch (start us, length us, event | category | flops | bytes accessed | tf_op | source)
XLA Modules:
  0.0 97.3 jit_solution(6336389600252018197)
XLA Ops:
  1.9 3.3 %shard_map.76 = (f32[2,128]{1,0:T(2,128)S(1)}, bf16[256,1152]{1,0:T(8,128)(2,1)S(1)}, bf16[256,1152]{1,0:T(8,128)(2,1)S(1)}, f32[256,1152]{1,0:T(8,128)S(1)}, f32[256,1]{1,0:T(8,128)S(1)}) custom-call(f32[1]{0:T(128)S(6)} %copy.8.scale, f32[1]{0:T(128)S(6)} %copy.9.bias, bf16[256,1152]{1,0:T(8,128)(2,1)} %images.3, bf16[256,1152]{1,0:T(8,128)(2,1)} %texts.3, ...), custom_call_target="tpu_custom_call" | custom-call | bytes 6195200 | tf_op jit(solution)/shard_map/pallas_call | solution.py:53
  5.3 3.3 %collective-permute-start = (bf16[256,1152]{1,0:T(8,128)(2,1)S(1)}, bf16[256,1152]{1,0:T(8,128)(2,1)S(1)}, u32[]{:S(2)}, u32[]{:S(2)}) collective-permute-start(bf16[256,1152]{1,0:T(8,128)(2,1)S(1)} %get-tuple-element.50.rows), channel_id=1, source_target_pairs={{0,16},{1,17},{2,18},{3,19},{4,20},{5,21},{6,22},{7,23},{8,24},{9,... | collective-permute-start | bytes 1769480 | tf_op jit(solution)/shard_map/ppermute | solution.py:40
  8.6 3.4 %collective-permute-start.2 = (bf16[256,1152]{1,0:T(8,128)(2,1)S(1)}, bf16[256,1152]{1,0:T(8,128)(2,1)S(1)}, u32[]{:S(2)}, u32[]{:S(2)}) collective-permute-start(bf16[256,1152]{1,0:T(8,128)(2,1)S(1)} %get-tuple-element.51.own), channel_id=1, source_target_pairs={{0,32},{1,33},{2,34},{3,35},{4,36},{5,37},{6,38},{7,39},{8,40},{9,... | collective-permute-start | bytes 1769480 | tf_op jit(solution)/shard_map/ppermute | solution.py:40
  12.0 2.1 %collective-permute-start.1 = (bf16[256,1152]{1,0:T(8,128)(2,1)S(1)}, bf16[256,1152]{1,0:T(8,128)(2,1)S(1)}, u32[]{:S(2)}, u32[]{:S(2)}) collective-permute-start(bf16[256,1152]{1,0:T(8,128)(2,1)S(1)} %collective-permute-done), channel_id=1, source_target_pairs={{0,32},{1,33},{2,34},{3,35},{4,36},{5,37},{6,38},{7,39},{8,40},{9,... | collective-permute-start | bytes 1769480 | tf_op jit(solution)/shard_map/ppermute | solution.py:40
  14.0 1.2 %shard_map.77 = (f32[256,1152]{1,0:T(8,128)S(1)}, f32[256,1152]{1,0:T(8,128)S(1)}) custom-call(f32[2,128]{1,0:T(2,128)S(1)} %get-tuple-element.49.par, bf16[256,1152]{1,0:T(8,128)(2,1)S(1)} %get-tuple-element.51.own, bf16[256,1152]{1,0:T(8,128)(2,1)S(1)} %get-tuple-element.50.rows), custom_call_target="tpu_custom_call" | custom-call | bytes 3539968 | tf_op jit(solution)/shard_map/pallas_call | solution.py:53
  15.2 3.6 %collective-permute-done.2.block = bf16[256,1152]{1,0:T(8,128)(2,1)S(1)} collective-permute-done((bf16[256,1152]{1,0:T(8,128)(2,1)S(1)}, bf16[256,1152]{1,0:T(8,128)(2,1)S(1)}, u32[]{:S(2)}, u32[]{:S(2)}) %collective-permute-start.2) | collective-permute-done | bytes 589856 | tf_op jit(solution)/shard_map/ppermute | solution.py:40
  18.8 5.5 %collective-permute-start.5 = (bf16[256,1152]{1,0:T(8,128)(2,1)S(1)}, bf16[256,1152]{1,0:T(8,128)(2,1)S(1)}, u32[]{:S(2)}, u32[]{:S(2)}) collective-permute-start(bf16[256,1152]{1,0:T(8,128)(2,1)S(1)} %collective-permute-done.2.block), channel_id=1, source_target_pairs={{0,32},{1,33},{2,34},{3,35},{4,36},{5,37},{6,38},{7,39},{8,40},{9,... | collective-permute-start | bytes 1769480 | tf_op jit(solution)/shard_map/ppermute | solution.py:40
  24.3 2.0 %shard_map.78 = (f32[256,1152]{1,0:T(8,128)S(1)}, f32[256,1152]{1,0:T(8,128)S(1)}, f32[256,1152]{1,0:T(8,128)S(1)}) custom-call(f32[2,128]{1,0:T(2,128)S(1)} %get-tuple-element.49.par, bf16[256,1152]{1,0:T(8,128)(2,1)S(1)} %collective-permute-done.2.block, bf16[256,1152]{1,0:T(8,128)(2,1)S(1)} %get-tuple-element.51.own, ...), custom_call_target="tpu_custom_call" | custom-call | bytes 8258560 | tf_op jit(solution)/shard_map/pallas_call | solution.py:53
  26.4 4.3 %collective-permute-start.4 = (bf16[256,1152]{1,0:T(8,128)(2,1)S(1)}, bf16[256,1152]{1,0:T(8,128)(2,1)S(1)}, u32[]{:S(2)}, u32[]{:S(2)}) collective-permute-start(bf16[256,1152]{1,0:T(8,128)(2,1)S(1)} %collective-permute-done.1.block), channel_id=1, source_target_pairs={{0,32},{1,33},{2,34},{3,35},{4,36},{5,37},{6,38},{7,39},{8,40},{9,... | collective-permute-start | bytes 1769480 | tf_op jit(solution)/shard_map/ppermute | solution.py:40
  30.6 1.0 %shard_map.80 = (bf16[256,1152]{1,0:T(8,128)(2,1)S(1)}, bf16[256,1152]{1,0:T(8,128)(2,1)S(1)}) custom-call(bf16[256,1152]{1,0:T(8,128)(2,1)S(1)} %copy-done.2, bf16[256,1152]{1,0:T(8,128)(2,1)S(1)} %collective-permute-done.6.images_s), custom_call_target="tpu_custom_call" | custom-call | bytes 2359296 | tf_op jit(solution)/shard_map/pallas_call | solution.py:53
  31.6 1.7 %shard_map.79 = (f32[256,1152]{1,0:T(8,128)S(1)}, f32[256,1152]{1,0:T(8,128)S(1)}) custom-call(f32[2,128]{1,0:T(2,128)S(1)} %get-tuple-element.49.par, bf16[256,1152]{1,0:T(8,128)(2,1)S(1)} %collective-permute-done.1.block, bf16[256,1152]{1,0:T(8,128)(2,1)S(1)} %get-tuple-element.50.rows, bf16[256,1152]{1,0:T(8,128)(2,1)S(1)} %collective-permute-done.3.rows_s.rows, ...), custom_call_target="tpu_custom_call" | custom-call | bytes 6489088 | tf_op jit(solution)/shard_map/pallas_call | solution.py:53
  34.3 3.5 %collective-permute-done.4.block = bf16[256,1152]{1,0:T(8,128)(2,1)S(1)} collective-permute-done((bf16[256,1152]{1,0:T(8,128)(2,1)S(1)}, bf16[256,1152]{1,0:T(8,128)(2,1)S(1)}, u32[]{:S(2)}, u32[]{:S(2)}) %collective-permute-start.4) | collective-permute-done | bytes 589856 | tf_op jit(solution)/shard_map/ppermute | solution.py:40
  38.7 4.5 %collective-permute-start.7 = (bf16[256,1152]{1,0:T(8,128)(2,1)S(1)}, bf16[256,1152]{1,0:T(8,128)(2,1)S(1)}, u32[]{:S(2)}, u32[]{:S(2)}) collective-permute-start(bf16[256,1152]{1,0:T(8,128)(2,1)S(1)} %shard_map.83), channel_id=1, source_target_pairs={{0,16},{1,17},{2,18},{3,19},{4,20},{5,21},{6,22},{7,23},{8,24},{9,... | collective-permute-start | bytes 1769480 | tf_op jit(solution)/shard_map/ppermute | solution.py:40
  48.2 1.3 %collective-permute-start.10 = (bf16[144,1152]{1,0:T(8,128)(2,1)S(1)}, bf16[144,1152]{1,0:T(8,128)(2,1)S(1)}, u32[]{:S(2)}, u32[]{:S(2)}) collective-permute-start(bf16[144,1152]{1,0:T(8,128)(2,1)S(1)} %get-tuple-element.82), channel_id=1, source_target_pairs={{0,64},{1,65},{2,66},{3,67},{4,68},{5,69},{6,70},{7,71},{8,72},{9,... | collective-permute-start | bytes 995336 | tf_op jit(solution)/shard_map/ppermute | solution.py:40
  50.9 2.0 %shard_map.87 = f32[256,1152]{1,0:T(8,128)} custom-call(bf16[256,1152]{1,0:T(8,128)(2,1)S(1)} %get-tuple-element.84.dproj, bf16[1152,1152]{1,0:T(8,128)(2,1)S(1)} %copy-done), custom_call_target="tpu_custom_call" | custom-call | bytes 4423680 | tf_op jit(solution)/shard_map/pallas_call | solution.py:53
  53.0 1.6 %shard_map.88 = f32[256,1152]{1,0:T(8,128)} custom-call(f32[2,128]{1,0:T(2,128)S(1)} %get-tuple-element.49.par, f32[256,1152]{1,0:T(8,128)S(1)} %shard_map.82.to_rows, f32[256,1152]{1,0:T(8,128)S(1)} %get-tuple-element.72.to_own, bf16[256,1152]{1,0:T(8,128)(2,1)S(1)} %collective-permute-done.7.given, bf16[256,1152]{1,0:T(8,128)(2,1)S(1)} %copy-done.1), custom_call_target="tpu_custom_call" | custom-call | bytes 4719616 | tf_op jit(solution)/shard_map/pallas_call | solution.py:53
  54.6 1.5 %collective-permute-done.10.c = bf16[144,1152]{1,0:T(8,128)(2,1)S(1)} collective-permute-done((bf16[144,1152]{1,0:T(8,128)(2,1)S(1)}, bf16[144,1152]{1,0:T(8,128)(2,1)S(1)}, u32[]{:S(2)}, u32[]{:S(2)}) %collective-permute-start.10) | collective-permute-done | bytes 331808 | tf_op jit(solution)/shard_map/ppermute | solution.py:40
  56.1 2.2 %collective-permute-done.11.d = bf16[144,1152]{1,0:T(8,128)(2,1)S(1)} collective-permute-done((bf16[144,1152]{1,0:T(8,128)(2,1)S(1)}, bf16[144,1152]{1,0:T(8,128)(2,1)S(1)}, u32[]{:S(2)}, u32[]{:S(2)}) %collective-permute-start.11) | collective-permute-done | bytes 331808 | tf_op jit(solution)/shard_map/ppermute | solution.py:40
  58.2 1.4 %collective-permute-done.9.b = bf16[144,1152]{1,0:T(8,128)(2,1)S(1)} collective-permute-done((bf16[144,1152]{1,0:T(8,128)(2,1)S(1)}, bf16[144,1152]{1,0:T(8,128)(2,1)S(1)}, u32[]{:S(2)}, u32[]{:S(2)}) %collective-permute-start.9) | collective-permute-done | bytes 331808 | tf_op jit(solution)/shard_map/ppermute | solution.py:40
  60.2 2.7 %collective-permute-start.14 = (bf16[72,576]{1,0:T(8,128)(2,1)S(1)}, bf16[72,576]{1,0:T(8,128)(2,1)S(1)}, u32[]{:S(2)}, u32[]{:S(2)}) collective-permute-start(bf16[72,576]{1,0:T(8,128)(2,1)S(1)} %get-tuple-element.94), channel_id=1, source_target_pairs={{0,129},{1,0},{2,131},{3,2},{4,133},{5,4},{6,135},{7,6},{8,137},{9... | collective-permute-start | bytes 248840 | tf_op jit(solution)/shard_map/ppermute | solution.py:40
  62.9 2.2 %collective-permute-done.12.b = bf16[72,576]{1,0:T(8,128)(2,1)S(1)} collective-permute-done((bf16[72,576]{1,0:T(8,128)(2,1)S(1)}, bf16[72,576]{1,0:T(8,128)(2,1)S(1)}, u32[]{:S(2)}, u32[]{:S(2)}) %collective-permute-start.12) | collective-permute-done | bytes 82976 | tf_op jit(solution)/shard_map/ppermute | solution.py:40
  65.1 1.0 %collective-permute-done.13.c = bf16[72,576]{1,0:T(8,128)(2,1)S(1)} collective-permute-done((bf16[72,576]{1,0:T(8,128)(2,1)S(1)}, bf16[72,576]{1,0:T(8,128)(2,1)S(1)}, u32[]{:S(2)}, u32[]{:S(2)}) %collective-permute-start.13) | collective-permute-done | bytes 82976 | tf_op jit(solution)/shard_map/ppermute | solution.py:40
  66.2 14.2 %all_to_all.10.parts = bf16[8,24,216]{2,1,0:T(8,128)(2,1)S(1)} all-to-all(bf16[8,24,216]{2,1,0:T(8,128)(2,1)S(1)} %shard_map.90), channel_id=1, replica_groups=mesh['yh'=2,'x'=4,'core'=2,'z'=8,'yl'=2] {'z'}, dimensions={0} | all-to-all | bytes 165888 | tf_op jit(solution)/shard_map/all_to_all | solution.py:371
  80.5 15.8 %all_to_all.11.parts = bf16[16,24,216]{2,1,0:T(8,128)(2,1)S(1)} all-to-all(bf16[16,24,216]{2,1,0:T(8,128)(2,1)S(1)} %shard_map.91), channel_id=1, replica_groups=mesh['yh'=2,'x'=4,'core'=2,'z'=8,'yl'=2] {'yh','x','core'}, dimensions={0} | all-to-all | bytes 331776 | tf_op jit(solution)/shard_map/all_to_all | solution.py:373
  (31 shorter events, 10.0 us)
Async XLA Ops:
  1.9 12.1 %copy-start.2 = (bf16[256,1152]{1,0:T(8,128)(2,1)S(1)}, bf16[256,1152]{1,0:T(8,128)(2,1)}, u32[]{:S(2)}) copy-start(bf16[256,1152]{1,0:T(8,128)(2,1)} %images.3) | copy-start | bytes 1769476
  5.3 6.7 %collective-permute-start = (bf16[256,1152]{1,0:T(8,128)(2,1)S(1)}, bf16[256,1152]{1,0:T(8,128)(2,1)S(1)}, u32[]{:S(2)}, u32[]{:S(2)}) collective-permute-start(bf16[256,1152]{1,0:T(8,128)(2,1)S(1)} %get-tuple-element.50.rows), channel_id=1, source_target_pairs={{0,16},{1,17},{2,18},{3,19},{4,20},{5,21},{6,22},{7,23},{8,24},{9,... | collective-permute-start | bytes 1769480 | tf_op jit(solution)/shard_map/ppermute | solution.py:40
  8.6 10.2 %collective-permute-start.2 = (bf16[256,1152]{1,0:T(8,128)(2,1)S(1)}, bf16[256,1152]{1,0:T(8,128)(2,1)S(1)}, u32[]{:S(2)}, u32[]{:S(2)}) collective-permute-start(bf16[256,1152]{1,0:T(8,128)(2,1)S(1)} %get-tuple-element.51.own), channel_id=1, source_target_pairs={{0,32},{1,33},{2,34},{3,35},{4,36},{5,37},{6,38},{7,39},{8,40},{9,... | collective-permute-start | bytes 1769480 | tf_op jit(solution)/shard_map/ppermute | solution.py:40
  12.0 12.4 %collective-permute-start.3 = (bf16[256,1152]{1,0:T(8,128)(2,1)S(1)}, bf16[256,1152]{1,0:T(8,128)(2,1)S(1)}, u32[]{:S(2)}, u32[]{:S(2)}) collective-permute-start(bf16[256,1152]{1,0:T(8,128)(2,1)S(1)} %get-tuple-element.51.own), channel_id=1, source_target_pairs={{0,16},{1,17},{2,18},{3,19},{4,20},{5,21},{6,22},{7,23},{8,24},{9,... | collective-permute-start | bytes 1769480 | tf_op jit(solution)/shard_map/ppermute | solution.py:40
  12.0 14.4 %collective-permute-start.1 = (bf16[256,1152]{1,0:T(8,128)(2,1)S(1)}, bf16[256,1152]{1,0:T(8,128)(2,1)S(1)}, u32[]{:S(2)}, u32[]{:S(2)}) collective-permute-start(bf16[256,1152]{1,0:T(8,128)(2,1)S(1)} %collective-permute-done), channel_id=1, source_target_pairs={{0,32},{1,33},{2,34},{3,35},{4,36},{5,37},{6,38},{7,39},{8,40},{9,... | collective-permute-start | bytes 1769480 | tf_op jit(solution)/shard_map/ppermute | solution.py:40
  14.0 16.6 %collective-permute-start.6 = (bf16[256,1152]{1,0:T(8,128)(2,1)S(1)}, bf16[256,1152]{1,0:T(8,128)(2,1)S(1)}, u32[]{:S(2)}, u32[]{:S(2)}) collective-permute-start(bf16[256,1152]{1,0:T(8,128)(2,1)S(1)} %copy-done.2), channel_id=1, source_target_pairs={{0,16},{1,17},{2,18},{3,19},{4,20},{5,21},{6,22},{7,23},{8,24},{9,... | collective-permute-start | bytes 1769480 | tf_op jit(solution)/shard_map/ppermute | solution.py:40
  18.8 14.5 %collective-permute-start.5 = (bf16[256,1152]{1,0:T(8,128)(2,1)S(1)}, bf16[256,1152]{1,0:T(8,128)(2,1)S(1)}, u32[]{:S(2)}, u32[]{:S(2)}) collective-permute-start(bf16[256,1152]{1,0:T(8,128)(2,1)S(1)} %collective-permute-done.2.block), channel_id=1, source_target_pairs={{0,32},{1,33},{2,34},{3,35},{4,36},{5,37},{6,38},{7,39},{8,40},{9,... | collective-permute-start | bytes 1769480 | tf_op jit(solution)/shard_map/ppermute | solution.py:40
  26.4 11.4 %collective-permute-start.4 = (bf16[256,1152]{1,0:T(8,128)(2,1)S(1)}, bf16[256,1152]{1,0:T(8,128)(2,1)S(1)}, u32[]{:S(2)}, u32[]{:S(2)}) collective-permute-start(bf16[256,1152]{1,0:T(8,128)(2,1)S(1)} %collective-permute-done.1.block), channel_id=1, source_target_pairs={{0,32},{1,33},{2,34},{3,35},{4,36},{5,37},{6,38},{7,39},{8,40},{9,... | collective-permute-start | bytes 1769480 | tf_op jit(solution)/shard_map/ppermute | solution.py:40
  38.7 6.1 %collective-permute-start.7 = (bf16[256,1152]{1,0:T(8,128)(2,1)S(1)}, bf16[256,1152]{1,0:T(8,128)(2,1)S(1)}, u32[]{:S(2)}, u32[]{:S(2)}) collective-permute-start(bf16[256,1152]{1,0:T(8,128)(2,1)S(1)} %shard_map.83), channel_id=1, source_target_pairs={{0,16},{1,17},{2,18},{3,19},{4,20},{5,21},{6,22},{7,23},{8,24},{9,... | collective-permute-start | bytes 1769480 | tf_op jit(solution)/shard_map/ppermute | solution.py:40
  45.5 1.7 %collective-permute-start.8 = (bf16[256,576]{1,0:T(8,128)(2,1)S(1)}, bf16[256,576]{1,0:T(8,128)(2,1)S(1)}, u32[]{:S(2)}, u32[]{:S(2)}) collective-permute-start(bf16[256,576]{1,0:T(8,128)(2,1)S(1)} %get-tuple-element.78), channel_id=1, source_target_pairs={{0,16},{1,17},{2,18},{3,19},{4,20},{5,21},{6,22},{7,23},{8,24},{9,... | collective-permute-start | bytes 884744 | tf_op jit(solution)/shard_map/ppermute | solution.py:40
  46.5 4.4 %copy-start = (bf16[1152,1152]{1,0:T(8,128)(2,1)S(1)}, bf16[1152,1152]{1,0:T(8,128)(2,1)}, u32[]{:S(2)}) copy-start(bf16[1152,1152]{1,0:T(8,128)(2,1)} %head.3) | copy-start | bytes 7962628
  48.2 7.9 %collective-permute-start.10 = (bf16[144,1152]{1,0:T(8,128)(2,1)S(1)}, bf16[144,1152]{1,0:T(8,128)(2,1)S(1)}, u32[]{:S(2)}, u32[]{:S(2)}) collective-permute-start(bf16[144,1152]{1,0:T(8,128)(2,1)S(1)} %get-tuple-element.82), channel_id=1, source_target_pairs={{0,64},{1,65},{2,66},{3,67},{4,68},{5,69},{6,70},{7,71},{8,72},{9,... | collective-permute-start | bytes 995336 | tf_op jit(solution)/shard_map/ppermute | solution.py:40
  49.4 8.8 %collective-permute-start.11 = (bf16[144,1152]{1,0:T(8,128)(2,1)S(1)}, bf16[144,1152]{1,0:T(8,128)(2,1)S(1)}, u32[]{:S(2)}, u32[]{:S(2)}) collective-permute-start(bf16[144,1152]{1,0:T(8,128)(2,1)S(1)} %get-tuple-element.83), channel_id=1, source_target_pairs={{0,96},{1,97},{2,98},{3,99},{4,100},{5,101},{6,102},{7,103},{8,104... | collective-permute-start | bytes 995336 | tf_op jit(solution)/shard_map/ppermute | solution.py:40
  50.2 9.4 %collective-permute-start.9 = (bf16[144,1152]{1,0:T(8,128)(2,1)S(1)}, bf16[144,1152]{1,0:T(8,128)(2,1)S(1)}, u32[]{:S(2)}, u32[]{:S(2)}) collective-permute-start(bf16[144,1152]{1,0:T(8,128)(2,1)S(1)} %get-tuple-element.81), channel_id=1, source_target_pairs={{0,32},{1,33},{2,34},{3,35},{4,36},{5,37},{6,38},{7,39},{8,40},{9,... | collective-permute-start | bytes 995336 | tf_op jit(solution)/shard_map/ppermute | solution.py:40
  50.9 2.0 %copy-start.1 = (bf16[256,1152]{1,0:T(8,128)(2,1)S(1)}, bf16[256,1152]{1,0:T(8,128)(2,1)}, u32[]{:S(2)}) copy-start(bf16[256,1152]{1,0:T(8,128)(2,1)} %texts.3) | copy-start | bytes 1769476
  60.0 5.1 %collective-permute-start.12 = (bf16[72,576]{1,0:T(8,128)(2,1)S(1)}, bf16[72,576]{1,0:T(8,128)(2,1)S(1)}, u32[]{:S(2)}, u32[]{:S(2)}) collective-permute-start(bf16[72,576]{1,0:T(8,128)(2,1)S(1)} %get-tuple-element.92), channel_id=1, source_target_pairs={{0,128},{1,129},{2,130},{3,131},{4,132},{5,133},{6,134},{7,135},{8... | collective-permute-start | bytes 248840 | tf_op jit(solution)/shard_map/ppermute | solution.py:40
  60.1 6.0 %collective-permute-start.13 = (bf16[72,576]{1,0:T(8,128)(2,1)S(1)}, bf16[72,576]{1,0:T(8,128)(2,1)S(1)}, u32[]{:S(2)}, u32[]{:S(2)}) collective-permute-start(bf16[72,576]{1,0:T(8,128)(2,1)S(1)} %get-tuple-element.93), channel_id=1, source_target_pairs={{0,1},{1,128},{2,3},{3,130},{4,5},{5,132},{6,7},{7,134},{8,9},{9,1... | collective-permute-start | bytes 248840 | tf_op jit(solution)/shard_map/ppermute | solution.py:40
  60.2 5.9 %collective-permute-start.14 = (bf16[72,576]{1,0:T(8,128)(2,1)S(1)}, bf16[72,576]{1,0:T(8,128)(2,1)S(1)}, u32[]{:S(2)}, u32[]{:S(2)}) collective-permute-start(bf16[72,576]{1,0:T(8,128)(2,1)S(1)} %get-tuple-element.94), channel_id=1, source_target_pairs={{0,129},{1,0},{2,131},{3,2},{4,133},{5,4},{6,135},{7,6},{8,137},{9... | collective-permute-start | bytes 248840 | tf_op jit(solution)/shard_map/ppermute | solution.py:40

commit v10 on v7

--- a/solution.py
+++ b/solution.py
@@ -250,9 +250,13 @@
         out[...] = pieces[lax.rem(place + turn, 4)]
 
 
-def head_body(keep, other, images, images2, *rest):
+def head_own_body(keep, images, out):
+    out[...] = mm(keep[...], images[...], (0, 0))
+
+
+def head_body(base, other, images2, *rest):
     outs, pieces = rest[:4], rest[4]
-    total = mm(keep[...], images[...], (0, 0)) + mm(other[...], images2[...], (0, 0))
+    total = base[...] + mm(other[...], images2[...], (0, 0))
     rows, half = pieces.shape[1], total.shape[1] // 2
 
     @pl.when(lax.axis_index("core") == 0)
@@ -389,9 +393,10 @@
         par, dimg, given, unit_img, pnorm,
     )
     other = moved(send, swap)
+    (base,) = call(head_own_body, [((half, width), F32)], keep, ordered)
     quarter = ((half // 4, width), BF)
     parts = call(
-        head_body, [quarter] * 4, keep, other, ordered, ordered2,
+        head_body, [quarter] * 4, base, other, ordered2,
         scratch=[pltpu.VMEM((4, half // 4, width), BF)],
     )
     parts = list(parts)

time: 97.8 us -> 97.5 us (level)
    pallas_call x16 -> x17, Pallas kernels: 19 us -> 19.2 us  [call(): pl.pallas_call(body, out_shape=shapes, in_specs=in_specs, out_specs=[pl.B...]
  transfers between devices with their start and end apart: 18 -> 18, of which waited for: 8 -> 7; matrix products, arithmetic and copies ran while one was open for 0% -> 0% of each run, Pallas kernels for 13% -> 13%
where the time goes in v10:
time: 97.5 us; the launch traced here: 97.1 us
  starting transfers between devices  31.2 us (32%)
  blocking collectives  30.7 us (31%)
  Pallas kernels  19.2 us (20%)
  waiting for transfers between devices  13.1 us (13%)
  between operations  2.07 us (2%)
    ppermute x18, starting transfers between devices, moved(): return lax.ppermute(value, AXES, pairs)  31.2 us
    pallas_call x17, Pallas kernels, call(): pl.pallas_call(body, out_shape=shapes, in_specs=in_specs, out_specs=[pl.B...  19.2 us
    all_to_all x1, blocking collectives, on_device(): part = lax.all_to_all(part, ('yh', 'x', 'core'), 0, 0)  15.5 us
    all_to_all x1, blocking collectives, on_device(): part = lax.all_to_all(part, 'z', 0, 0)  15.2 us
    ppermute x18, waiting for transfers between devices, moved(): return lax.ppermute(value, AXES, pairs)  13.1 us
  transfers between devices with their start and end apart: 18, of which 7 were waited for; matrix products, arithmetic and copies ran while one was open for 0% of the time, Pallas kernels for 13%

profile of v10, /device:TPU:1, one launch (start us, length us, event | category | flops | bytes accessed | tf_op | source)
XLA Modules:
  0.0 97.1 jit_solution(4170330251386394011)
XLA Ops:
  1.9 3.3 %shard_map.76 = (f32[2,128]{1,0:T(2,128)S(1)}, bf16[128,1152]{1,0:T(8,128)(2,1)S(1)}, bf16[128,1152]{1,0:T(8,128)(2,1)S(1)}, bf16[128,1152]{1,0:T(8,128)(2,1)S(1...) custom-call(f32[1]{0:T(128)S(6)} %copy.8.scale, ...), custom_call_target="tpu_custom_call" | custom-call | bytes 7964672 | tf_op jit(solution)/shard_map/pallas_call | solution.py:53
  5.2 3.3 %collective-permute-start.8 = (bf16[768,1152]{1,0:T(8,128)(2,1)S(1)}, bf16[768,1152]{1,0:T(8,128)(2,1)S(1)}, u32[]{:S(2)}, u32[]{:S(2)}) collective-permute-start(bf16[768,1152]{1,0:T(8,128)(2,1)S(1)} %get-tuple-element.57.both), channel_id=1, source_target_pairs={{0,16},{1,17},{2,18},{3,19},{4,20},{5,21},{6,22},{7,23},{8,24},{9,... | collective-permute-start | bytes 5308424 | tf_op jit(solution)/shard_map/ppermute | solution.py:40
  8.6 3.4 %collective-permute-start = (bf16[128,1152]{1,0:T(8,128)(2,1)S(1)}, bf16[128,1152]{1,0:T(8,128)(2,1)S(1)}, u32[]{:S(2)}, u32[]{:S(2)}) collective-permute-start(bf16[128,1152]{1,0:T(8,128)(2,1)S(1)} %get-tuple-element.56), channel_id=1, source_target_pairs={{0,32},{1,33},{2,34},{3,35},{4,36},{5,37},{6,38},{7,39},{8,40},{9,... | collective-permute-start | bytes 884744 | tf_op jit(solution)/shard_map/ppermute | solution.py:40
  11.9 5.1 %collective-permute-start.4 = (bf16[128,1152]{1,0:T(8,128)(2,1)S(1)}, bf16[128,1152]{1,0:T(8,128)(2,1)S(1)}, u32[]{:S(2)}, u32[]{:S(2)}) collective-permute-start(bf16[128,1152]{1,0:T(8,128)(2,1)S(1)} %get-tuple-element.62), channel_id=1, source_target_pairs={{0,32},{1,33},{2,34},{3,35},{4,36},{5,37},{6,38},{7,39},{8,40},{9,... | collective-permute-start | bytes 884744 | tf_op jit(solution)/shard_map/ppermute | solution.py:40
  17.0 1.1 %shard_map.77 = (f32[256,1152]{1,0:T(8,128)S(1)}, f32[256,1152]{1,0:T(8,128)S(1)}) custom-call(f32[2,128]{1,0:T(2,128)S(1)} %get-tuple-element.55.par, bf16[768,1152]{1,0:T(8,128)(2,1)S(1)} %get-tuple-element.57.both), custom_call_target="tpu_custom_call" | custom-call | bytes 4129792 | tf_op jit(solution)/shard_map/pallas_call | solution.py:53
  18.2 5.2 %collective-permute-start.1 = (bf16[128,1152]{1,0:T(8,128)(2,1)S(1)}, bf16[128,1152]{1,0:T(8,128)(2,1)S(1)}, u32[]{:S(2)}, u32[]{:S(2)}) collective-permute-start(bf16[128,1152]{1,0:T(8,128)(2,1)S(1)} %collective-permute-done.p1a), channel_id=1, source_target_pairs={{0,32},{1,33},{2,34},{3,35},{4,36},{5,37},{6,38},{7,39},{8,40},{9,... | collective-permute-start | bytes 884744 | tf_op jit(solution)/shard_map/ppermute | solution.py:40
  23.3 5.6 %collective-permute-start.5 = (bf16[128,1152]{1,0:T(8,128)(2,1)S(1)}, bf16[128,1152]{1,0:T(8,128)(2,1)S(1)}, u32[]{:S(2)}, u32[]{:S(2)}) collective-permute-start(bf16[128,1152]{1,0:T(8,128)(2,1)S(1)} %collective-permute-done.4.p1b), channel_id=1, source_target_pairs={{0,32},{1,33},{2,34},{3,35},{4,36},{5,37},{6,38},{7,39},{8,40},{9,... | collective-permute-start | bytes 884744 | tf_op jit(solution)/shard_map/ppermute | solution.py:40
  29.0 1.0 %shard_map.79 = (bf16[256,1152]{1,0:T(8,128)(2,1)S(1)}, bf16[256,1152]{1,0:T(8,128)(2,1)S(1)}) custom-call(bf16[768,1152]{1,0:T(8,128)(2,1)S(1)} %get-tuple-element.57.both, bf16[768,1152]{1,0:T(8,128)(2,1)S(1)} %collective-permute-done.8.both_s), custom_call_target="tpu_custom_call" | custom-call | bytes 4718592 | tf_op jit(solution)/shard_map/pallas_call | solution.py:53
  30.0 3.5 %shard_map.78 = (f32[256,1152]{1,0:T(8,128)S(1)}, f32[256,1152]{1,0:T(8,128)S(1)}, f32[256,1152]{1,0:T(8,128)S(1)}, f32[256,1152]{1,0:T(8,128)S(1)}) custom-call(f32[2,128]{1,0:T(2,128)S(1)} %get-tuple-element.55.par, bf16[128,1152]{1,0:T(8,128)(2,1)S(1)} %collective-permute-done.p1a, bf16[128,1152]{1,0:T(8,128)(2,1)S(1)} %collective-permute-done.4.p1b, ...), custom_call_target="tpu_custom_call" | custom-call | bytes 11797504 | tf_op jit(solution)/shard_map/pallas_call | solution.py:53
  33.5 1.6 %collective-permute-done.3.p2a = bf16[128,1152]{1,0:T(8,128)(2,1)S(1)} collective-permute-done((bf16[128,1152]{1,0:T(8,128)(2,1)S(1)}, bf16[128,1152]{1,0:T(8,128)(2,1)S(1)}, u32[]{:S(2)}, u32[]{:S(2)}) %collective-permute-start.3) | collective-permute-done | bytes 294944 | tf_op jit(solution)/shard_map/ppermute | solution.py:40
  36.0 4.5 %collective-permute-done.7.p2b = bf16[128,1152]{1,0:T(8,128)(2,1)S(1)} collective-permute-done((bf16[128,1152]{1,0:T(8,128)(2,1)S(1)}, bf16[128,1152]{1,0:T(8,128)(2,1)S(1)}, u32[]{:S(2)}, u32[]{:S(2)}) %collective-permute-start.7) | collective-permute-done | bytes 294944 | tf_op jit(solution)/shard_map/ppermute | solution.py:40
  41.5 0.9 shard_map.80.old
  42.4 1.0 %collective-permute-done.9.given = bf16[256,1152]{1,0:T(8,128)(2,1)S(1)} collective-permute-done((bf16[256,1152]{1,0:T(8,128)(2,1)S(1)}, bf16[256,1152]{1,0:T(8,128)(2,1)S(1)}, u32[]{:S(2)}, u32[]{:S(2)}) %collective-permute-start.9) | collective-permute-done | bytes 589856 | tf_op jit(solution)/shard_map/ppermute | solution.py:40
  44.4 1.4 %collective-permute-start.14 = (bf16[256,1152]{1,0:T(8,128)(2,1)S(1)}, bf16[256,1152]{1,0:T(8,128)(2,1)S(1)}, u32[]{:S(2)}, u32[]{:S(2)}) collective-permute-start(bf16[256,1152]{1,0:T(8,128)(2,1)S(1)} %shard_map.86), channel_id=1, source_target_pairs={{0,16},{1,17},{2,18},{3,19},{4,20},{5,21},{6,22},{7,23},{8,24},{9,... | collective-permute-start | bytes 1769480 | tf_op jit(solution)/shard_map/ppermute | solution.py:40
  46.3 1.0 shard_map.84
  47.3 1.4 %collective-permute-start.11 = (bf16[144,1152]{1,0:T(8,128)(2,1)S(1)}, bf16[144,1152]{1,0:T(8,128)(2,1)S(1)}, u32[]{:S(2)}, u32[]{:S(2)}) collective-permute-start(bf16[144,1152]{1,0:T(8,128)(2,1)S(1)} %get-tuple-element.85), channel_id=1, source_target_pairs={{0,64},{1,65},{2,66},{3,67},{4,68},{5,69},{6,70},{7,71},{8,72},{9,... | collective-permute-start | bytes 995336 | tf_op jit(solution)/shard_map/ppermute | solution.py:40
  48.9 2.4 %collective-permute-start.13 = (bf16[144,1152]{1,0:T(8,128)(2,1)S(1)}, bf16[144,1152]{1,0:T(8,128)(2,1)S(1)}, u32[]{:S(2)}, u32[]{:S(2)}) collective-permute-start(bf16[144,1152]{1,0:T(8,128)(2,1)S(1)} %get-tuple-element.87), channel_id=1, source_target_pairs={{0,96},{1,97},{2,98},{3,99},{4,100},{5,101},{6,102},{7,103},{8,104... | collective-permute-start | bytes 995336 | tf_op jit(solution)/shard_map/ppermute | solution.py:40
  53.1 2.1 %shard_map.85 = f32[256,1152]{1,0:T(8,128)} custom-call(bf16[256,1152]{1,0:T(8,128)(2,1)S(1)} %get-tuple-element.88.dproj, bf16[1152,1152]{1,0:T(8,128)(2,1)S(1)} %copy-done), custom_call_target="tpu_custom_call" | custom-call | bytes 4423680 | tf_op jit(solution)/shard_map/pallas_call | solution.py:53
  55.2 3.5 %collective-permute-done.12.c = bf16[144,1152]{1,0:T(8,128)(2,1)S(1)} collective-permute-done((bf16[144,1152]{1,0:T(8,128)(2,1)S(1)}, bf16[144,1152]{1,0:T(8,128)(2,1)S(1)}, u32[]{:S(2)}, u32[]{:S(2)}) %collective-permute-start.12) | collective-permute-done | bytes 331808 | tf_op jit(solution)/shard_map/ppermute | solution.py:40
  60.2 1.8 %collective-permute-start.17 = (bf16[72,576]{1,0:T(8,128)(2,1)S(1)}, bf16[72,576]{1,0:T(8,128)(2,1)S(1)}, u32[]{:S(2)}, u32[]{:S(2)}) collective-permute-start(bf16[72,576]{1,0:T(8,128)(2,1)S(1)} %get-tuple-element.99), channel_id=1, source_target_pairs={{0,129},{1,0},{2,131},{3,2},{4,133},{5,4},{6,135},{7,6},{8,137},{9... | collective-permute-start | bytes 248840 | tf_op jit(solution)/shard_map/ppermute | solution.py:40
  62.0 1.6 %shard_map.89 = f32[256,1152]{1,0:T(8,128)} custom-call(f32[2,128]{1,0:T(2,128)S(1)} %get-tuple-element.55.par, f32[256,1152]{1,0:T(8,128)S(1)} %shard_map.87.old, bf16[256,1152]{1,0:T(8,128)(2,1)S(1)} %collective-permute-done.14.given, bf16[256,1152]{1,0:T(8,128)(2,1)S(1)} %copy-done.1), custom_call_target="tpu_custom_call" | custom-call | bytes 3539968 | tf_op jit(solution)/shard_map/pallas_call | solution.py:53
  65.3 15.2 %all_to_all.10.parts = bf16[8,24,216]{2,1,0:T(8,128)(2,1)S(1)} all-to-all(bf16[8,24,216]{2,1,0:T(8,128)(2,1)S(1)} %shard_map.90), channel_id=1, replica_groups=mesh['yh'=2,'x'=4,'core'=2,'z'=8,'yl'=2] {'z'}, dimensions={0} | all-to-all | bytes 165888 | tf_op jit(solution)/shard_map/all_to_all | solution.py:424
  80.6 15.5 %all_to_all.11.parts = bf16[16,24,216]{2,1,0:T(8,128)(2,1)S(1)} all-to-all(bf16[16,24,216]{2,1,0:T(8,128)(2,1)S(1)} %shard_map.91), channel_id=1, replica_groups=mesh['yh'=2,'x'=4,'core'=2,'z'=8,'yl'=2] {'yh','x','core'}, dimensions={0} | all-to-all | bytes 331776 | tf_op jit(solution)/shard_map/all_to_all | solution.py:426
  96.1 1.0 shard_map.92
  (35 shorter events, 8.7 us)
Async XLA Ops:
  5.2 23.7 %collective-permute-start.8 = (bf16[768,1152]{1,0:T(8,128)(2,1)S(1)}, bf16[768,1152]{1,0:T(8,128)(2,1)S(1)}, u32[]{:S(2)}, u32[]{:S(2)}) collective-permute-start(bf16[768,1152]{1,0:T(8,128)(2,1)S(1)} %get-tuple-element.57.both), channel_id=1, source_target_pairs={{0,16},{1,17},{2,18},{3,19},{4,20},{5,21},{6,22},{7,23},{8,24},{9,... | collective-permute-start | bytes 5308424 | tf_op jit(solution)/shard_map/ppermute | solution.py:40
  8.6 9.6 %collective-permute-start = (bf16[128,1152]{1,0:T(8,128)(2,1)S(1)}, bf16[128,1152]{1,0:T(8,128)(2,1)S(1)}, u32[]{:S(2)}, u32[]{:S(2)}) collective-permute-start(bf16[128,1152]{1,0:T(8,128)(2,1)S(1)} %get-tuple-element.56), channel_id=1, source_target_pairs={{0,32},{1,33},{2,34},{3,35},{4,36},{5,37},{6,38},{7,39},{8,40},{9,... | collective-permute-start | bytes 884744 | tf_op jit(solution)/shard_map/ppermute | solution.py:40
  11.9 11.4 %collective-permute-start.2 = (bf16[128,1152]{1,0:T(8,128)(2,1)S(1)}, bf16[128,1152]{1,0:T(8,128)(2,1)S(1)}, u32[]{:S(2)}, u32[]{:S(2)}) collective-permute-start(bf16[128,1152]{1,0:T(8,128)(2,1)S(1)} %get-tuple-element.61), channel_id=1, source_target_pairs={{0,224},{1,225},{2,226},{3,227},{4,228},{5,229},{6,230},{7,231},{8... | collective-permute-start | bytes 884744 | tf_op jit(solution)/shard_map/ppermute | solution.py:40
  11.9 11.4 %collective-permute-start.4 = (bf16[128,1152]{1,0:T(8,128)(2,1)S(1)}, bf16[128,1152]{1,0:T(8,128)(2,1)S(1)}, u32[]{:S(2)}, u32[]{:S(2)}) collective-permute-start(bf16[128,1152]{1,0:T(8,128)(2,1)S(1)} %get-tuple-element.62), channel_id=1, source_target_pairs={{0,32},{1,33},{2,34},{3,35},{4,36},{5,37},{6,38},{7,39},{8,40},{9,... | collective-permute-start | bytes 884744 | tf_op jit(solution)/shard_map/ppermute | solution.py:40
  17.0 12.0 %collective-permute-start.6 = (bf16[128,1152]{1,0:T(8,128)(2,1)S(1)}, bf16[128,1152]{1,0:T(8,128)(2,1)S(1)}, u32[]{:S(2)}, u32[]{:S(2)}) collective-permute-start(bf16[128,1152]{1,0:T(8,128)(2,1)S(1)} %get-tuple-element.63), channel_id=1, source_target_pairs={{0,224},{1,225},{2,226},{3,227},{4,228},{5,229},{6,230},{7,231},{8... | collective-permute-start | bytes 884744 | tf_op jit(solution)/shard_map/ppermute | solution.py:40
  18.2 15.4 %collective-permute-start.1 = (bf16[128,1152]{1,0:T(8,128)(2,1)S(1)}, bf16[128,1152]{1,0:T(8,128)(2,1)S(1)}, u32[]{:S(2)}, u32[]{:S(2)}) collective-permute-start(bf16[128,1152]{1,0:T(8,128)(2,1)S(1)} %collective-permute-done.p1a), channel_id=1, source_target_pairs={{0,32},{1,33},{2,34},{3,35},{4,36},{5,37},{6,38},{7,39},{8,40},{9,... | collective-permute-start | bytes 884744 | tf_op jit(solution)/shard_map/ppermute | solution.py:40
  23.3 11.8 %collective-permute-start.3 = (bf16[128,1152]{1,0:T(8,128)(2,1)S(1)}, bf16[128,1152]{1,0:T(8,128)(2,1)S(1)}, u32[]{:S(2)}, u32[]{:S(2)}) collective-permute-start(bf16[128,1152]{1,0:T(8,128)(2,1)S(1)} %collective-permute-done.2.p2a), channel_id=1, source_target_pairs={{0,224},{1,225},{2,226},{3,227},{4,228},{5,229},{6,230},{7,231},{8... | collective-permute-start | bytes 884744 | tf_op jit(solution)/shard_map/ppermute | solution.py:40
  23.3 12.6 %collective-permute-start.5 = (bf16[128,1152]{1,0:T(8,128)(2,1)S(1)}, bf16[128,1152]{1,0:T(8,128)(2,1)S(1)}, u32[]{:S(2)}, u32[]{:S(2)}) collective-permute-start(bf16[128,1152]{1,0:T(8,128)(2,1)S(1)} %collective-permute-done.4.p1b), channel_id=1, source_target_pairs={{0,32},{1,33},{2,34},{3,35},{4,36},{5,37},{6,38},{7,39},{8,40},{9,... | collective-permute-start | bytes 884744 | tf_op jit(solution)/shard_map/ppermute | solution.py:40
  29.0 11.4 %collective-permute-start.7 = (bf16[128,1152]{1,0:T(8,128)(2,1)S(1)}, bf16[128,1152]{1,0:T(8,128)(2,1)S(1)}, u32[]{:S(2)}, u32[]{:S(2)}) collective-permute-start(bf16[128,1152]{1,0:T(8,128)(2,1)S(1)} %collective-permute-done.6.p2b), channel_id=1, source_target_pairs={{0,224},{1,225},{2,226},{3,227},{4,228},{5,229},{6,230},{7,231},{8... | collective-permute-start | bytes 884744 | tf_op jit(solution)/shard_map/ppermute | solution.py:40
  41.4 2.1 %collective-permute-start.9 = (bf16[256,1152]{1,0:T(8,128)(2,1)S(1)}, bf16[256,1152]{1,0:T(8,128)(2,1)S(1)}, u32[]{:S(2)}, u32[]{:S(2)}) collective-permute-start(bf16[256,1152]{1,0:T(8,128)(2,1)S(1)} %shard_map.81), channel_id=1, source_target_pairs={{0,16},{1,17},{2,18},{3,19},{4,20},{5,21},{6,22},{7,23},{8,24},{9,... | collective-permute-start | bytes 1769480 | tf_op jit(solution)/shard_map/ppermute | solution.py:40
  44.1 2.2 %collective-permute-start.10 = (bf16[256,576]{1,0:T(8,128)(2,1)S(1)}, bf16[256,576]{1,0:T(8,128)(2,1)S(1)}, u32[]{:S(2)}, u32[]{:S(2)}) collective-permute-start(bf16[256,576]{1,0:T(8,128)(2,1)S(1)} %get-tuple-element.82), channel_id=1, source_target_pairs={{0,16},{1,17},{2,18},{3,19},{4,20},{5,21},{6,22},{7,23},{8,24},{9,... | collective-permute-start | bytes 884744 | tf_op jit(solution)/shard_map/ppermute | solution.py:40
  44.4 10.8 %collective-permute-start.14 = (bf16[256,1152]{1,0:T(8,128)(2,1)S(1)}, bf16[256,1152]{1,0:T(8,128)(2,1)S(1)}, u32[]{:S(2)}, u32[]{:S(2)}) collective-permute-start(bf16[256,1152]{1,0:T(8,128)(2,1)S(1)} %shard_map.86), channel_id=1, source_target_pairs={{0,16},{1,17},{2,18},{3,19},{4,20},{5,21},{6,22},{7,23},{8,24},{9,... | collective-permute-start | bytes 1769480 | tf_op jit(solution)/shard_map/ppermute | solution.py:40
  47.3 7.9 %collective-permute-start.11 = (bf16[144,1152]{1,0:T(8,128)(2,1)S(1)}, bf16[144,1152]{1,0:T(8,128)(2,1)S(1)}, u32[]{:S(2)}, u32[]{:S(2)}) collective-permute-start(bf16[144,1152]{1,0:T(8,128)(2,1)S(1)} %get-tuple-element.85), channel_id=1, source_target_pairs={{0,64},{1,65},{2,66},{3,67},{4,68},{5,69},{6,70},{7,71},{8,72},{9,... | collective-permute-start | bytes 995336 | tf_op jit(solution)/shard_map/ppermute | solution.py:40
  48.7 10.0 %collective-permute-start.12 = (bf16[144,1152]{1,0:T(8,128)(2,1)S(1)}, bf16[144,1152]{1,0:T(8,128)(2,1)S(1)}, u32[]{:S(2)}, u32[]{:S(2)}) collective-permute-start(bf16[144,1152]{1,0:T(8,128)(2,1)S(1)} %get-tuple-element.86), channel_id=1, source_target_pairs={{0,32},{1,33},{2,34},{3,35},{4,36},{5,37},{6,38},{7,39},{8,40},{9,... | collective-permute-start | bytes 995336 | tf_op jit(solution)/shard_map/ppermute | solution.py:40
  48.9 9.7 %collective-permute-start.13 = (bf16[144,1152]{1,0:T(8,128)(2,1)S(1)}, bf16[144,1152]{1,0:T(8,128)(2,1)S(1)}, u32[]{:S(2)}, u32[]{:S(2)}) collective-permute-start(bf16[144,1152]{1,0:T(8,128)(2,1)S(1)} %get-tuple-element.87), channel_id=1, source_target_pairs={{0,96},{1,97},{2,98},{3,99},{4,100},{5,101},{6,102},{7,103},{8,104... | collective-permute-start | bytes 995336 | tf_op jit(solution)/shard_map/ppermute | solution.py:40
  51.4 1.7 %copy-start = (bf16[1152,1152]{1,0:T(8,128)(2,1)S(1)}, bf16[1152,1152]{1,0:T(8,128)(2,1)}, u32[]{:S(2)}) copy-start(bf16[1152,1152]{1,0:T(8,128)(2,1)} %head.3) | copy-start | bytes 7962628
  55.2 6.8 %copy-start.1 = (bf16[256,1152]{1,0:T(8,128)(2,1)S(1)}, bf16[256,1152]{1,0:T(8,128)(2,1)}, u32[]{:S(2)}) copy-start(bf16[256,1152]{1,0:T(8,128)(2,1)} %texts.3) | copy-start | bytes 1769476
  59.1 5.3 %collective-permute-start.15 = (bf16[72,576]{1,0:T(8,128)(2,1)S(1)}, bf16[72,576]{1,0:T(8,128)(2,1)S(1)}, u32[]{:S(2)}, u32[]{:S(2)}) collective-permute-start(bf16[72,576]{1,0:T(8,128)(2,1)S(1)} %get-tuple-element.97), channel_id=1, source_target_pairs={{0,128},{1,129},{2,130},{3,131},{4,132},{5,133},{6,134},{7,135},{8... | collective-permute-start | bytes 248840 | tf_op jit(solution)/shard_map/ppermute | solution.py:40
  59.2 6.0 %collective-permute-start.16 = (bf16[72,576]{1,0:T(8,128)(2,1)S(1)}, bf16[72,576]{1,0:T(8,128)(2,1)S(1)}, u32[]{:S(2)}, u32[]{:S(2)}) collective-permute-start(bf16[72,576]{1,0:T(8,128)(2,1)S(1)} %get-tuple-element.98), channel_id=1, source_target_pairs={{0,1},{1,128},{2,3},{3,130},{4,5},{5,132},{6,7},{7,134},{8,9},{9,1... | collective-permute-start | bytes 248840 | tf_op jit(solution)/shard_map/ppermute | solution.py:40
  60.2 5.0 %collective-permute-start.17 = (bf16[72,576]{1,0:T(8,128)(2,1)S(1)}, bf16[72,576]{1,0:T(8,128)(2,1)S(1)}, u32[]{:S(2)}, u32[]{:S(2)}) collective-permute-start(bf16[72,576]{1,0:T(8,128)(2,1)S(1)} %get-tuple-element.99), channel_id=1, source_target_pairs={{0,129},{1,0},{2,131},{3,2},{4,133},{5,4},{6,135},{7,6},{8,137},{9... | collective-permute-start | bytes 248840 | tf_op jit(solution)/shard_map/ppermute | solution.py:40
